TPU v7x, 32 devices: a whole 2x2x4 slice. The times are simulated.
32 devices in a mesh: band: 8 (over y, x, core), grp: 4 (over z).
Axes of the slice: x: 2, y: 2, z: 4, core: 2. Of those that a mesh axis runs over, the one named last changes fastest.
Arguments:
- spectral: bfloat16 [640, 2, 4, 16, 640], P(('band', 'grp')), may hold values from -6 to 6
- legendre: bfloat16 [640, 640, 640], P(('band', 'grp')), may hold values from -4 to 4
- owner_table: int32 [640], replicated, may hold values from 0 to 639, as said below
Outputs:
- spectral_out: float32 [640, 2, 4, 16, 640], P(('band', 'grp'))
Inputs may be any that keep to these rules, and one draw needn't show every extreme that they name: `owner_table`: A permutation of the zonal wavenumbers. Slot s of the whole array belongs to device s // 20 along band+grp. For each q below 10, slots 2q and 2q + 1 of every device hold wavenumbers whose sum is (4q + 2) * 32 - 1.
All inputs are finite; a program needn't handle non-finite values.
Results may differ from a plain program's by a relative error of at most 0.0067.
Values may be sent and summed in bfloat16 or wider, within the bound.
No kernel may reach another device: no remote copies, remote signals or barrier semaphores. Data moves between devices by JAX's collectives and lax.ppermute only.
A program may use at most 192 MiB of HBM per device.

v0:
```python
import functools
import math

import jax
import jax.numpy as jnp
from jax import lax
from jax.experimental import pallas as pl
from jax.experimental.pallas import tpu as pltpu
from jax.sharding import PartitionSpec as P

LANES = 128
AXES = ("band", "grp")
VMEM_BYTES = 62 * 1024 * 1024


def synthesis_kernel(slots, levels, fields, least, scale, first_ref, owner_ref, spec_ref, *refs):
    table_refs, out_ref, rows_ref = refs[:-2], refs[-2], refs[-1]
    tiles = rows_ref.shape[1]
    step = pl.program_id(0)
    block = spec_ref.shape[0]
    row_total = spec_ref.shape[1]
    stride = 2 * slots

    def run(group):
        start = least[group]
        for j in range(block):
            spec = spec_ref[j, :, start:]
            wave = owner_ref[first_ref[0] + group * block + j]
            distance = lax.broadcasted_iota(jnp.int32, (1, spec.shape[1]), 1) + (start - wave)
            keep = jnp.where(distance >= 0, 1.0, 0.0)
            flip = jnp.where(distance % 2 == 0, keep, -keep)
            both = jnp.concatenate([spec * keep.astype(spec.dtype), spec * flip.astype(spec.dtype)], axis=0)
            table = jnp.concatenate([ref[j, start:, :] for ref in table_refs], axis=1)
            halves = jnp.dot(both, table, preferred_element_type=jnp.float32) * scale
            first = 2 * (group * block + j)
            for hemi in range(2):
                for part in range(2):
                    for field in range(fields):
                        at = hemi * row_total + (part * fields + field) * levels
                        target = pl.ds(hemi * levels * stride + first + part, levels, stride=stride)
                        for tile in range(tiles):
                            lanes = slice(tile * LANES, (tile + 1) * LANES)
                            rows_ref[field, tile, target, :] = halves[at : at + levels, lanes]

    for group in range(slots // block):
        pl.when(step == group)(functools.partial(run, group))

    @pl.when(step == pl.num_programs(0) - 1)
    def _():
        for field in range(fields):
            for tile in range(tiles):
                lanes = pl.ds((field * tiles + tile) * LANES, LANES)
                out_ref[:, lanes] = rows_ref[field, tile].astype(out_ref.dtype)


def synthesize(first, owner_table, spec_rows, legendre, chunk, fields, levels, least):
    slots, row_total, degrees = spec_rows.shape
    block = slots // len(least)
    rows = 2 * levels * 2 * slots
    at, tiles = chunk
    shape = (rows, fields * tiles * LANES)
    return pl.pallas_call(
        functools.partial(synthesis_kernel, slots, levels, fields, least, 1.0 / math.sqrt(degrees)),
        grid_spec=pltpu.PrefetchScalarGridSpec(
            num_scalar_prefetch=2,
            grid=(slots // block,),
            in_specs=[
                pl.BlockSpec((block, row_total, degrees), lambda i, *_: (i, 0, 0)),
            ]
            + [pl.BlockSpec((block, degrees, LANES), lambda i, *_, t=at + t: (i, 0, t)) for t in range(tiles)],
            out_specs=pl.BlockSpec(shape, lambda i, *_: (0, 0)),
            scratch_shapes=[pltpu.VMEM((fields, tiles, rows, LANES), jnp.float32)],
        ),
        out_shape=jax.ShapeDtypeStruct(shape, jnp.bfloat16),
        compiler_params=pltpu.CompilerParams(vmem_limit_bytes=VMEM_BYTES),
        cost_estimate=pl.CostEstimate(
            flops=4 * slots * row_total * degrees * tiles * LANES,
            bytes_accessed=2 * slots * degrees * (row_total + tiles * LANES) + 2 * rows * shape[1],
            transcendentals=0,
        ),
        name="synthesis",
    )(first, owner_table, spec_rows, *[legendre] * tiles)


def longitude_kernel(fields, grid_scale, zonal_scale, rows_ref, by_lon_ref, by_wave_ref, out_ref, sum_ref):
    step = pl.program_id(0)
    values = jnp.dot(by_lon_ref[...], rows_ref[...], preferred_element_type=jnp.float32) * grid_scale
    one = values.shape[1] // fields
    following = jnp.concatenate([values[:, one:], values[:, :one]], axis=1)
    product = (values * following).astype(jnp.bfloat16)
    share = jnp.dot(by_wave_ref[...], product, preferred_element_type=jnp.float32)

    @pl.when(step == 0)
    def _():
        sum_ref[...] = share

    @pl.when(step > 0)
    def _():
        sum_ref[...] += share

    @pl.when(step == pl.num_programs(0) - 1)
    def _():
        out_ref[...] = (sum_ref[...] * zonal_scale).astype(out_ref.dtype)


def longitudes(rows, by_lon, by_wave, fields):
    depth, width = rows.shape
    lon_count = by_lon.shape[0]
    lon_block = lon_count // 5
    return pl.pallas_call(
        functools.partial(longitude_kernel, fields, 1.0 / math.sqrt(depth // 2), 2.0 / math.sqrt(lon_count)),
        grid=(lon_count // lon_block,),
        in_specs=[
            pl.BlockSpec((depth, width), lambda i: (0, 0)),
            pl.BlockSpec((lon_block, depth), lambda i: (i, 0)),
            pl.BlockSpec((depth, lon_block), lambda i: (0, i)),
        ],
        out_specs=pl.BlockSpec((depth, width), lambda i: (0, 0)),
        out_shape=jax.ShapeDtypeStruct((depth, width), jnp.bfloat16),
        scratch_shapes=[pltpu.VMEM((depth, width), jnp.float32)],
        compiler_params=pltpu.CompilerParams(vmem_limit_bytes=VMEM_BYTES),
        cost_estimate=pl.CostEstimate(
            flops=4 * depth * width * lon_count,
            bytes_accessed=4 * depth * (width + lon_count),
            transcendentals=0,
        ),
        name="longitudes",
    )(rows, by_lon, by_wave)


def fold_kernel(slots, levels, fields, arrived_ref, out_ref, rows_ref):
    tiles = rows_ref.shape[1]
    stride = 2 * slots
    half = levels * stride
    for field in range(fields):
        for tile in range(tiles):
            lanes = pl.ds((field * tiles + tile) * LANES, LANES)
            rows_ref[field, tile] = arrived_ref[:, lanes].astype(jnp.float32)
    for slot in range(slots):
        for part in range(2):
            for field in range(fields):
                for tile in range(tiles):
                    first = 2 * slot + part
                    north = rows_ref[field, tile, pl.ds(first, levels, stride=stride), :]
                    south = rows_ref[field, tile, pl.ds(half + first, levels, stride=stride), :]
                    lanes = pl.ds(tile * LANES, LANES)
                    at = (part * fields + field) * levels
                    out_ref[slot, at : at + levels, lanes] = (north + south).astype(out_ref.dtype)
                    at += 2 * fields * levels
                    out_ref[slot, at : at + levels, lanes] = (north - south).astype(out_ref.dtype)


def fold(arrived, slots, levels, fields):
    row_total = 2 * fields * levels
    rows, width = arrived.shape
    tiles = width // (fields * LANES)
    shape = (slots, 2 * row_total, tiles * LANES)
    return pl.pallas_call(
        functools.partial(fold_kernel, slots, levels, fields),
        in_specs=[pl.BlockSpec((rows, width), lambda: (0, 0))],
        out_specs=pl.BlockSpec(shape, lambda: (0, 0, 0)),
        out_shape=jax.ShapeDtypeStruct(shape, jnp.bfloat16),
        scratch_shapes=[pltpu.VMEM((fields, tiles, rows, LANES), jnp.float32)],
        compiler_params=pltpu.CompilerParams(vmem_limit_bytes=VMEM_BYTES),
        cost_estimate=pl.CostEstimate(flops=2 * rows * width, bytes_accessed=4 * rows * width, transcendentals=0),
        name="fold",
    )(arrived)


def analysis_kernel(chunks, least, adds, *refs):
    folded_refs = refs[:chunks]
    even_ref, odd_ref = refs[chunks : chunks + 2]
    out_ref = refs[-1]
    table_refs = refs[chunks + 2 : -2 if adds else -1]
    row_total, degrees = out_ref.shape[1:]
    step = pl.program_id(0)

    def run(group):
        start = least[group]
        for j in range(out_ref.shape[0]):
            folded = jnp.concatenate([ref[j] for ref in folded_refs], axis=1)
            table = jnp.concatenate([ref[j, start:, :] for ref in table_refs], axis=1)
            sums = lax.dot_general(folded, table, (((1,), (1,)), ((), ())), preferred_element_type=jnp.float32)
            kept = sums[:row_total] * even_ref[j, :, start:] + sums[row_total:] * odd_ref[j, :, start:]
            if adds:
                kept = kept + refs[-2][j, :, start:]
            out_ref[j, :, start:] = kept
            if start:
                out_ref[j, :, :start] = jnp.zeros((row_total, start), out_ref.dtype)

    for group in range(len(least)):
        pl.when(step == group)(functools.partial(run, group))


def analyze(folded, even, odd, legendre, row_total, least, first_tile, base=None):
    slots, degrees, _ = legendre.shape
    block = slots // len(least)
    lat_count = sum(x.shape[2] for x in folded)
    tiles = lat_count // LANES
    mask_spec = pl.BlockSpec((block, 1, degrees), lambda i: (i, 0, 0))
    sums_spec = pl.BlockSpec((block, row_total, degrees), lambda i: (i, 0, 0))
    return pl.pallas_call(
        functools.partial(analysis_kernel, len(folded), least, base is not None),
        grid=(len(least),),
        in_specs=[pl.BlockSpec((block,) + x.shape[1:], lambda i: (i, 0, 0)) for x in folded]
        + [mask_spec, mask_spec]
        + [pl.BlockSpec((block, degrees, LANES), lambda i, t=first_tile + t: (i, 0, t)) for t in range(tiles)]
        + ([sums_spec] if base is not None else []),
        out_specs=sums_spec,
        out_shape=jax.ShapeDtypeStruct((slots, row_total, degrees), jnp.float32),
        compiler_params=pltpu.CompilerParams(vmem_limit_bytes=VMEM_BYTES),
        cost_estimate=pl.CostEstimate(
            flops=4 * slots * row_total * degrees * lat_count,
            bytes_accessed=2 * slots * (degrees * lat_count + 2 * row_total * (lat_count + degrees)),
            transcendentals=0,
        ),
        name="analysis",
    )(*folded, even, odd, *[legendre] * tiles, *([base] if base is not None else []))


def after(value, *others):
    return lax.optimization_barrier((value, others))[0]


def trig_kernel(cos_base_ref, sin_base_ref, cos_turn_ref, sin_turn_ref, cos_base_t, sin_base_t, cos_turn_t, sin_turn_t, by_wave_ref, by_lon_ref):
    for j in range(cos_base_ref.shape[1]):
        lanes = pl.ds(j * LANES, LANES)
        cos_base, sin_base = cos_base_ref[:, j : j + 1], sin_base_ref[:, j : j + 1]
        angles = cos_base * cos_turn_ref[...] - sin_base * sin_turn_ref[...]
        by_wave_ref[:, lanes] = angles.astype(by_wave_ref.dtype)
        cos_base, sin_base = cos_base_t[j : j + 1, :], sin_base_t[j : j + 1, :]
        angles = cos_base * cos_turn_t[...] - sin_base * sin_turn_t[...]
        by_lon_ref[lanes, :] = angles.astype(by_lon_ref.dtype)


def trig_tables(owner_table, lon_count, *others):
    waves = jnp.repeat(owner_table, 2).astype(jnp.float32)[:, None]
    quarter = jnp.tile(jnp.array([0, lon_count // 4], jnp.float32), owner_table.shape[0])[:, None]
    unit = 2.0 * math.pi / lon_count

    def angles(lon, turn):
        phase = waves * lon + turn
        return (phase - lon_count * jnp.floor(phase * (1.0 / lon_count))) * unit

    base = angles(jnp.arange(0, lon_count, LANES, dtype=jnp.float32)[None, :], quarter)
    turn = angles(jnp.arange(LANES, dtype=jnp.float32)[None, :], 0.0)
    depth = waves.shape[0]
    blocks = lon_count // LANES
    rows = 256
    small = pl.BlockSpec((rows, blocks), lambda i: (i, 0))
    wide = pl.BlockSpec((rows, LANES), lambda i: (i, 0))
    small_t = pl.BlockSpec((blocks, rows), lambda i: (0, i))
    wide_t = pl.BlockSpec((LANES, rows), lambda i: (0, i))
    parts = (jnp.cos(base), jnp.sin(base), jnp.cos(turn), jnp.sin(turn))
    parts = after(parts, *others)
    return pl.pallas_call(
        trig_kernel,
        grid=(depth // rows,),
        in_specs=[small, small, wide, wide, small_t, small_t, wide_t, wide_t],
        out_specs=[
            pl.BlockSpec((rows, lon_count), lambda i: (i, 0)),
            pl.BlockSpec((lon_count, rows), lambda i: (0, i)),
        ],
        out_shape=[
            jax.ShapeDtypeStruct((depth, lon_count), jnp.bfloat16),
            jax.ShapeDtypeStruct((lon_count, depth), jnp.bfloat16),
        ],
        compiler_params=pltpu.CompilerParams(vmem_limit_bytes=VMEM_BYTES),
        cost_estimate=pl.CostEstimate(
            flops=8 * depth * lon_count, bytes_accessed=4 * depth * lon_count, transcendentals=0
        ),
        name="trig",
    )(*parts, *[x.T for x in parts])


def exchange(rows):
    return lax.all_to_all(rows, AXES, split_axis=0, concat_axis=0, tiled=True)


def by_hemisphere_and_level(spectral, legendre, owner_table):
    slots, _, fields, levels, degrees = spectral.shape
    half_lat = legendre.shape[2]
    lon_count = 4 * half_lat
    row_total = 2 * fields * levels
    tiles = half_lat // LANES
    first = lax.axis_index(AXES).astype(jnp.int32) * slots
    spec_rows = spectral.reshape(slots, row_total, degrees)
    least = tuple(8 * g * levels for g in range(slots // 4))
    cut = tiles // 2
    chunks = [(cut, tiles - cut), (0, cut)]

    def send(spec, chunk):
        return synthesize(first.reshape(1), owner_table, spec, legendre, chunk, fields, levels, least)

    large = send(spec_rows, chunks[0])
    small = send(after(spec_rows, large), chunks[1])
    arrived = [exchange(large)]
    arrived.append(exchange(after(small, *arrived)))
    by_wave, by_lon = trig_tables(after(owner_table, large), lon_count, small)
    zonal = [longitudes(rows, by_lon, by_wave, fields) for rows in arrived]
    returned = [exchange(zonal[0])]
    returned.append(exchange(after(zonal[1], *returned)))
    wavenumber = lax.dynamic_slice_in_dim(after(owner_table, by_wave), first, slots)
    distance = jnp.arange(degrees, dtype=jnp.int32)[None, :] - wavenumber[:, None]
    scale = 1.0 / math.sqrt(2 * half_lat)
    even = jnp.where((distance >= 0) & (distance % 2 == 0), scale, 0.0).astype(jnp.float32)[:, None, :]
    odd = jnp.where((distance >= 0) & (distance % 2 != 0), scale, 0.0).astype(jnp.float32)[:, None, :]
    out = analyze([fold(returned[0], slots, levels, fields)], even, odd, legendre, row_total, least, cut)
    last = fold(after(returned[1], out), slots, levels, fields)
    out = analyze([last], even, odd, legendre, row_total, least, 0, out)
    return out.reshape(slots, 2, fields, levels, degrees)


def make_trig(wavenumber, lon_count):
    lon_index = jnp.arange(lon_count, dtype=jnp.int32)
    phases = wavenumber[:, None] * lon_index[None, :] % lon_count
    angles = phases.astype(jnp.float32) * (2.0 * math.pi / lon_count)
    return jnp.stack([jnp.cos(angles), -jnp.sin(angles)], axis=1).astype(jnp.bfloat16)


def by_level_and_latitude(spectral, legendre, owner_table):
    slot_count, _, fields, levels, degrees = spectral.shape
    half_lat = legendre.shape[2]
    lat_count = 2 * half_lat
    lon_count = 2 * lat_count
    wave_count = owner_table.shape[0]
    band_count = lax.axis_size("band")
    group_count = lax.axis_size("grp")
    device_count = band_count * group_count
    level_block = levels // band_count
    lat_block = lat_count // group_count
    row_total = 2 * fields * levels
    row_width = fields * level_block * lat_block
    slot_start = lax.axis_index(("band", "grp")) * slot_count
    wavenumber = lax.dynamic_slice_in_dim(owner_table, slot_start, slot_count)
    degree_index = jnp.arange(degrees, dtype=jnp.int32)
    keep_mask = (degree_index[None, :] >= wavenumber[:, None]).astype(jnp.bfloat16)
    odd_part = (degree_index[None, :] - wavenumber[:, None]) % 2
    flip_sign = (1 - 2 * odd_part).astype(jnp.bfloat16)
    spec_rows = spectral.reshape(slot_count, row_total, degrees) * keep_mask[:, None, :]
    both_rows = jnp.concatenate([spec_rows, spec_rows * flip_sign[:, None, :]], axis=1)
    halves = jnp.einsum("srn,snt->srt", both_rows, legendre, preferred_element_type=jnp.float32)
    northern = halves[:, :row_total]
    mirrored = halves[:, row_total:]
    fourier = jnp.concatenate([northern, jnp.flip(mirrored, axis=2)], axis=2)
    fourier = fourier.reshape(
        slot_count, 2, fields, band_count, level_block, group_count, lat_block
    )
    fourier = jnp.transpose(fourier, (0, 1, 2, 3, 5, 4, 6))
    fourier_low = (fourier * (1.0 / math.sqrt(degrees))).astype(jnp.bfloat16)
    packed = fourier_low.reshape(1, slot_count, 2, fields, device_count, level_block, lat_block)
    arrived = lax.all_to_all(packed, ("band", "grp"), split_axis=4, concat_axis=0, tiled=True)
    arrived = arrived.reshape(-1, 2, row_width)
    trig_rows = make_trig(owner_table, lon_count)
    grid_values = jnp.einsum("scw,scl->wl", arrived, trig_rows, preferred_element_type=jnp.float32)
    grid_values = (grid_values * (1.0 / math.sqrt(wave_count))).reshape(
        fields, level_block * lat_block, lon_count
    )
    product = (grid_values * jnp.roll(grid_values, -1, axis=0)).astype(jnp.bfloat16)
    zonal_coeffs = jnp.einsum(
        "wl,scl->scw",
        product.reshape(row_width, lon_count),
        trig_rows,
        preferred_element_type=jnp.float32,
    )
    zonal_coeffs = (zonal_coeffs * (2.0 / math.sqrt(lon_count))).astype(jnp.bfloat16)
    sendback = zonal_coeffs.reshape(device_count, slot_count, 2, fields, 1, level_block, lat_block)
    returned = lax.all_to_all(sendback, ("band", "grp"), split_axis=0, concat_axis=4, tiled=True)
    returned = returned.reshape(
        slot_count, 2, fields, band_count, group_count, level_block, lat_block
    )
    returned = jnp.transpose(returned, (0, 1, 2, 3, 5, 4, 6)).reshape(slot_count, row_total, lat_count)
    northern_part = returned[:, :, :half_lat].astype(jnp.float32)
    mirror_part = jnp.flip(returned[:, :, half_lat:], axis=2).astype(jnp.float32)
    plus_part = (northern_part + mirror_part).astype(jnp.bfloat16)
    minus_part = (northern_part - mirror_part).astype(jnp.bfloat16)
    stacked = jnp.concatenate([plus_part, minus_part], axis=1)
    projected = jnp.einsum("srt,snt->srn", stacked, legendre, preferred_element_type=jnp.float32)
    even_rows = flip_sign[:, None, :] > 0
    chosen = jnp.where(even_rows, projected[:, :row_total], projected[:, row_total:])
    chosen = chosen * keep_mask.astype(jnp.float32)[:, None, :] * (1.0 / math.sqrt(lat_count))
    return chosen.reshape(slot_count, 2, fields, levels, degrees)


def on_device(spectral, legendre, owner_table):
    slots, _, _, levels, _ = spectral.shape
    whole_hemispheres = lax.axis_size("band") * lax.axis_size("grp") == 2 * levels
    if whole_hemispheres and legendre.shape[2] % LANES == 0 and legendre.shape[2] > LANES and slots % 4 == 0 and levels % 16 == 0:
        return by_hemisphere_and_level(spectral, legendre, owner_table)
    return by_level_and_latitude(spectral, legendre, owner_table)


def solution(mesh):
    placed = (P(("band", "grp"), None, None, None, None), P(("band", "grp"), None, None), P())
    return jax.shard_map(
        on_device,
        mesh=mesh,
        in_specs=placed,
        out_specs=P(("band", "grp"), None, None, None, None),
        check_vma=False,
    )
```

profile of v0, /device:TPU:0, one launch (start us, length us, event | category | flops | bytes accessed | tf_op | source)
XLA Modules:
  0.0 340.7 jit_solution(2929215414278116299)
XLA Ops:
  0.0 10.8 %synthesis.2 = bf16[1280,1536]{1,0:T(8,128)(2,1)} custom-call(s32[1]{0:T(128)} %bitcast.first_ref, s32[640]{0:T(1024)} %owner_ref.3, bf16[20,128,640]{2,1,0:T(8,128)(2,1)} %bitcast.16, bf16[20,640,640]{2,1,0:T(8,128)(2,1)} %refs_4_.3, bf16[20,640,640]{2,1,0:T(8,128)(2,1)} %refs_4_.3, bf16[20,640,640]{2,1,0:T(8,128)(2,1)} %refs_4_.3), custom_call_target="tpu_custom_call" | custom-call | flops 2516582400 | bytes 17039360 | tf_op jit(solution)/shard_map/synthesis/pallas_call | solution.py:62
  10.8 7.4 %all-to-all-start = ((bf16[32,40,1536]{2,1,0:T(8,128)(2,1)}), bf16[32,40,1536]{2,1,0:T(8,128)(2,1)}, u32[]{:S(2)}, u32[]{:S(2)}) async-start(bf16[32,40,1536]{2,1,0:T(8,128)(2,1)} %bitcast.15), calls=%async_computation | async-start | bytes 7864320 | tf_op jit(solution)/shard_map/all_to_all | solution.py:277
  18.2 9.0 %synthesis.3 = bf16[1280,1024]{1,0:T(8,128)(2,1)} custom-call(s32[1]{0:T(128)} %bitcast.first_ref, s32[640]{0:T(1024)} %owner_ref.3, bf16[20,128,640]{2,1,0:T(8,128)(2,1)} %bitcast.17, bf16[20,640,640]{2,1,0:T(8,128)(2,1)} %refs_4_.3, bf16[20,640,640]{2,1,0:T(8,128)(2,1)} %refs_4_.3), custom_call_target="tpu_custom_call" | custom-call | flops 1677721600 | bytes 12451840 | tf_op jit(solution)/shard_map/synthesis/pallas_call | solution.py:62
  27.2 77.8 %all-to-all-done = bf16[32,40,1536]{2,1,0:T(8,128)(2,1)} async-done(((bf16[32,40,1536]{2,1,0:T(8,128)(2,1)}), bf16[32,40,1536]{2,1,0:T(8,128)(2,1)}, u32[]{:S(2)}, u32[]{:S(2)}) %all-to-all-start) | async-done | bytes 3932192 | tf_op jit(solution)/shard_map/all_to_all | solution.py:277
  105.0 5.7 %all-to-all-start.1 = ((bf16[32,40,1024]{2,1,0:T(8,128)(2,1)}), bf16[32,40,1024]{2,1,0:T(8,128)(2,1)}, u32[]{:S(2)}, u32[]{:S(2)}) async-start(bf16[32,40,1024]{2,1,0:T(8,128)(2,1)} %bitcast.18), calls=%async_computation.1 | async-start | bytes 5242880 | tf_op jit(solution)/shard_map/all_to_all | solution.py:277
  111.3 0.5 fusion.2
  111.9 2.4 fusion
  114.3 1.2 copy.9.cos_base_ref
  115.5 1.1 copy.10.sin_base_ref
  116.6 1.1 copy.11.cos_turn_ref
  117.7 1.1 copy.12.sin_turn_ref
  118.8 11.8 %trig.1 = (bf16[1280,2560]{1,0:T(8,128)(2,1)}, bf16[2560,1280]{1,0:T(8,128)(2,1)}) custom-call(f32[1280,20]{1,0:T(8,128)} %copy.9.cos_base_ref, f32[1280,20]{1,0:T(8,128)} %copy.10.sin_base_ref, f32[1280,128]{1,0:T(8,128)} %copy.11.cos_turn_ref, f32[1280,128]{1,0:T(8,128)} %copy.12.sin_turn_ref, f32[20,1280]{1,0:T(8,128)} %bitcast.24, f32[20,1280]{1,0:T(8,128)} %bitcast.23, ...), custom_call_target="tpu_custom_call" | custom-call | flops 26214400 | bytes 13107200 | tf_op jit(solution)/shard_map/trig/pallas_call | solution.py:256
  130.6 30.8 %longitudes.3 = bf16[1280,1536]{1,0:T(8,128)(2,1)} custom-call(bf16[1280,1536]{1,0:T(8,128)(2,1)} %bitcast.3.rows_ref, bf16[2560,1280]{1,0:T(8,128)(2,1)} %get-tuple-element.24.by_lon_ref, bf16[1280,2560]{1,0:T(8,128)(2,1)} %get-tuple-element.25.by_wave_ref), custom_call_target="tpu_custom_call" | custom-call | flops 20132659200 | bytes 20971520 | tf_op jit(solution)/shard_map/longitudes/pallas_call | solution.py:110
  161.4 8.1 %all-to-all-done.1 = bf16[32,40,1024]{2,1,0:T(8,128)(2,1)} async-done(((bf16[32,40,1024]{2,1,0:T(8,128)(2,1)}), bf16[32,40,1024]{2,1,0:T(8,128)(2,1)}, u32[]{:S(2)}, u32[]{:S(2)}) %all-to-all-start.1) | async-done | bytes 2621472 | tf_op jit(solution)/shard_map/all_to_all | solution.py:277
  169.4 4.9 %all-to-all-start.2 = ((bf16[32,40,1536]{2,1,0:T(8,128)(2,1)}), bf16[32,40,1536]{2,1,0:T(8,128)(2,1)}, u32[]{:S(2)}, u32[]{:S(2)}) async-start(bf16[32,40,1536]{2,1,0:T(8,128)(2,1)} %bitcast.21), calls=%async_computation.2 | async-start | bytes 7864320 | tf_op jit(solution)/shard_map/all_to_all | solution.py:277
  174.3 21.8 %longitudes.2 = bf16[1280,1024]{1,0:T(8,128)(2,1)} custom-call(bf16[1280,1024]{1,0:T(8,128)(2,1)} %bitcast.5.rows_ref, bf16[2560,1280]{1,0:T(8,128)(2,1)} %get-tuple-element.24.by_lon_ref, bf16[1280,2560]{1,0:T(8,128)(2,1)} %get-tuple-element.25.by_wave_ref), custom_call_target="tpu_custom_call" | custom-call | flops 13421772800 | bytes 18350080 | tf_op jit(solution)/shard_map/longitudes/pallas_call | solution.py:110
  196.1 64.7 %all-to-all-done.2 = bf16[32,40,1536]{2,1,0:T(8,128)(2,1)} async-done(((bf16[32,40,1536]{2,1,0:T(8,128)(2,1)}), bf16[32,40,1536]{2,1,0:T(8,128)(2,1)}, u32[]{:S(2)}, u32[]{:S(2)}) %all-to-all-start.2) | async-done | bytes 3932192 | tf_op jit(solution)/shard_map/all_to_all | solution.py:277
  260.9 5.5 %all-to-all-start.3 = ((bf16[32,40,1024]{2,1,0:T(8,128)(2,1)}), bf16[32,40,1024]{2,1,0:T(8,128)(2,1)}, u32[]{:S(2)}, u32[]{:S(2)}) async-start(bf16[32,40,1024]{2,1,0:T(8,128)(2,1)} %bitcast.22), calls=%async_computation.3 | async-start | bytes 5242880 | tf_op jit(solution)/shard_map/all_to_all | solution.py:277
  266.5 1.0 and_select_fusion
  267.5 6.3 %fold.2.refs_0_ = bf16[20,256,384]{2,1,0:T(8,128)(2,1)} custom-call(bf16[1280,1536]{1,0:T(8,128)(2,1)} %bitcast.11.arrived_ref), custom_call_target="tpu_custom_call" | custom-call | flops 3932160 | bytes 7864320 | tf_op jit(solution)/shard_map/fold/pallas_call | solution.py:158
  273.8 10.6 %analysis.2.refs_5_ = f32[20,128,640]{2,1,0:T(8,128)} custom-call(bf16[20,256,384]{2,1,0:T(8,128)(2,1)} %fold.2.refs_0_, f32[20,1,640]{2,1,0:T(1,128)} %get-tuple-element.34.refs_1_, f32[20,1,640]{2,1,0:T(1,128)} %get-tuple-element.33.refs_2_, bf16[20,640,640]{2,1,0:T(8,128)(2,1)} %refs_4_.3, bf16[20,640,640]{2,1,0:T(8,128)(2,1)} %refs_4_.3, ...), custom_call_target="tpu_custom_call" | custom-call | flops 2516582400 | bytes 20316160 | tf_op jit(solution)/shard_map/analysis/pallas_call | solution.py:202
  284.4 40.9 %all-to-all-done.3 = bf16[32,40,1024]{2,1,0:T(8,128)(2,1)} async-done(((bf16[32,40,1024]{2,1,0:T(8,128)(2,1)}), bf16[32,40,1024]{2,1,0:T(8,128)(2,1)}, u32[]{:S(2)}, u32[]{:S(2)}) %all-to-all-start.3) | async-done | bytes 2621472 | tf_op jit(solution)/shard_map/all_to_all | solution.py:277
  325.4 5.0 %fold.3.refs_0_ = bf16[20,256,256]{2,1,0:T(8,128)(2,1)} custom-call(bf16[1280,1024]{1,0:T(8,128)(2,1)} %bitcast.13.arrived_ref), custom_call_target="tpu_custom_call" | custom-call | flops 2621440 | bytes 5242880 | tf_op jit(solution)/shard_map/fold/pallas_call | solution.py:158
  330.3 10.4 %analysis.3 = f32[20,128,640]{2,1,0:T(8,128)} custom-call(bf16[20,256,256]{2,1,0:T(8,128)(2,1)} %fold.3.refs_0_, f32[20,1,640]{2,1,0:T(1,128)} %get-tuple-element.34.refs_1_, f32[20,1,640]{2,1,0:T(1,128)} %get-tuple-element.33.refs_2_, bf16[20,640,640]{2,1,0:T(8,128)(2,1)} %refs_4_.3, bf16[20,640,640]{2,1,0:T(8,128)(2,1)} %refs_4_.3, ...), custom_call_target="tpu_custom_call" | custom-call | flops 1677721600 | bytes 15728640 | tf_op jit(solution)/shard_map/analysis/pallas_call | solution.py:202
  (19 shorter events, 0.7 us)
Async XLA Ops:
  10.8 94.2 %all-to-all-start = ((bf16[32,40,1536]{2,1,0:T(8,128)(2,1)}), bf16[32,40,1536]{2,1,0:T(8,128)(2,1)}, u32[]{:S(2)}, u32[]{:S(2)}) async-start(bf16[32,40,1536]{2,1,0:T(8,128)(2,1)} %bitcast.15), calls=%async_computation | async-start | bytes 7864320 | tf_op jit(solution)/shard_map/all_to_all | solution.py:277
  27.1 83.5 %copy-start.5 = (f32[2]{0:T(128)S(1)}, f32[2]{0:T(128)}, u32[]{:S(2)}) copy-start(f32[2]{0:T(128)} %constant.52.clone) | copy-start | bytes 28
  27.1 83.8 %copy-start.4 = (s32[640]{0:T(1024)S(1)}, s32[640]{0:T(1024)}, u32[]{:S(2)}) copy-start(s32[640]{0:T(1024)} %owner_ref.3) | copy-start | bytes 7684
  105.0 64.5 %all-to-all-start.1 = ((bf16[32,40,1024]{2,1,0:T(8,128)(2,1)}), bf16[32,40,1024]{2,1,0:T(8,128)(2,1)}, u32[]{:S(2)}, u32[]{:S(2)}) async-start(bf16[32,40,1024]{2,1,0:T(8,128)(2,1)} %bitcast.18), calls=%async_computation.1 | async-start | bytes 5242880 | tf_op jit(solution)/shard_map/all_to_all | solution.py:277
  111.8 6.9 %copy-start.2 = (f32[1280,20]{0,1:T(8,128)}, f32[1280,20]{0,1:T(8,128)S(1)}, u32[]{:S(2)}) copy-start(f32[1280,20]{0,1:T(8,128)S(1)} %get-tuple-element.21) | copy-start | bytes 307204
  111.8 6.9 %copy-start.3 = (f32[1280,20]{0,1:T(8,128)}, f32[1280,20]{0,1:T(8,128)S(1)}, u32[]{:S(2)}) copy-start(f32[1280,20]{0,1:T(8,128)S(1)} %get-tuple-element.20) | copy-start | bytes 307204
  114.3 4.5 %copy-start = (f32[1280,128]{0,1:T(8,128)}, f32[1280,128]{0,1:T(8,128)S(1)}, u32[]{:S(2)}) copy-start(f32[1280,128]{0,1:T(8,128)S(1)} %get-tuple-element.23) | copy-start | bytes 1966084
  114.3 4.5 %copy-start.1 = (f32[1280,128]{0,1:T(8,128)}, f32[1280,128]{0,1:T(8,128)S(1)}, u32[]{:S(2)}) copy-start(f32[1280,128]{0,1:T(8,128)S(1)} %get-tuple-element.22) | copy-start | bytes 1966084
  169.4 91.4 %all-to-all-start.2 = ((bf16[32,40,1536]{2,1,0:T(8,128)(2,1)}), bf16[32,40,1536]{2,1,0:T(8,128)(2,1)}, u32[]{:S(2)}, u32[]{:S(2)}) async-start(bf16[32,40,1536]{2,1,0:T(8,128)(2,1)} %bitcast.21), calls=%async_computation.2 | async-start | bytes 7864320 | tf_op jit(solution)/shard_map/all_to_all | solution.py:277
  260.9 64.5 %all-to-all-start.3 = ((bf16[32,40,1024]{2,1,0:T(8,128)(2,1)}), bf16[32,40,1024]{2,1,0:T(8,128)(2,1)}, u32[]{:S(2)}, u32[]{:S(2)}) async-start(bf16[32,40,1024]{2,1,0:T(8,128)(2,1)} %bitcast.22), calls=%async_computation.3 | async-start | bytes 5242880 | tf_op jit(solution)/shard_map/all_to_all | solution.py:277
where the time goes:
time: 342 us; the launch traced here: 341 us
  waiting for transfers between devices  192 us (56%)
  Pallas kernels  116 us (34%)
  starting transfers between devices  23.5 us (7%)
  local copies, waits for them, and re-layouts  5.18 us (2%)
  other arithmetic  3.98 us (1%)
    all_to_all x4, waiting for transfers between devices, exchange(): return lax.all_to_all(rows, AXES, split_axis=0, concat_axis=0, tiled=True)  192 us
    pallas_call x2, Pallas kernels, longitudes(): pl.pallas_call(functools.partial(longitude_kernel, fields, 1.0 / math.sqr...  52.6 us
    all_to_all x4, starting transfers between devices, exchange(): return lax.all_to_all(rows, AXES, split_axis=0, concat_axis=0, tiled=True)  23.5 us
    pallas_call x2, Pallas kernels, analyze(): pl.pallas_call(functools.partial(analysis_kernel, len(folded), least, bas...  21 us
    pallas_call x2, Pallas kernels, synthesize(): pl.pallas_call(functools.partial(synthesis_kernel, slots, levels, fields,...  19.7 us
    pallas_call x1, Pallas kernels, trig_tables(): pl.pallas_call(trig_kernel, grid=(depth // rows,), in_specs=[small, small...  11.8 us
    pallas_call x2, Pallas kernels, fold(): pl.pallas_call(functools.partial(fold_kernel, slots, levels, fields), in_...  11.3 us
  transfers between devices with their start and end apart: 4, of which 4 were waited for; matrix products, arithmetic and copies ran while one was open for 3% of the time, Pallas kernels for 27%

commit v1 on v0

--- a/solution.py
+++ b/solution.py
@@ -13,65 +13,75 @@
 VMEM_BYTES = 62 * 1024 * 1024
 
 
-def synthesis_kernel(slots, levels, fields, least, scale, first_ref, owner_ref, spec_ref, *refs):
-    table_refs, out_ref, rows_ref = refs[:-2], refs[-2], refs[-1]
-    tiles = rows_ref.shape[1]
-    step = pl.program_id(0)
-    block = spec_ref.shape[0]
-    row_total = spec_ref.shape[1]
+def synthesis_kernel(
+    slots, levels, fields, least, chunk, scale, first_ref, owner_ref, spec_ref, table_ref, out_ref, rows_ref, sems, *held
+):
+    at, tiles = chunk
+    groups = len(least)
+    block = slots // groups
+    row_total, degrees = spec_ref.shape[1:]
     stride = 2 * slots
-
-    def run(group):
-        start = least[group]
+    copies = []
+    for group, start in enumerate(least):
+        mine = pl.ds(group * block, block)
+        left = pl.ds(start, degrees - start)
+        lanes = pl.ds(at * LANES, tiles * LANES)
+        copies.append(
+            (
+                pltpu.make_async_copy(spec_ref.at[mine, :, left], held[2 * group], sems.at[2 * group]),
+                pltpu.make_async_copy(table_ref.at[mine, left, lanes], held[2 * group + 1], sems.at[2 * group + 1]),
+            )
+        )
+    order = range(groups - 1, -1, -1)
+    for group in order:
+        for copy in copies[group]:
+            copy.start()
+    for group in order:
+        for copy in copies[group]:
+            copy.wait()
         for j in range(block):
-            spec = spec_ref[j, :, start:]
+            spec = held[2 * group][j]
             wave = owner_ref[first_ref[0] + group * block + j]
-            distance = lax.broadcasted_iota(jnp.int32, (1, spec.shape[1]), 1) + (start - wave)
+            distance = lax.broadcasted_iota(jnp.int32, (1, spec.shape[1]), 1) + (least[group] - wave)
             keep = jnp.where(distance >= 0, 1.0, 0.0)
             flip = jnp.where(distance % 2 == 0, keep, -keep)
             both = jnp.concatenate([spec * keep.astype(spec.dtype), spec * flip.astype(spec.dtype)], axis=0)
-            table = jnp.concatenate([ref[j, start:, :] for ref in table_refs], axis=1)
-            halves = jnp.dot(both, table, preferred_element_type=jnp.float32) * scale
+            halves = jnp.dot(both, held[2 * group + 1][j], preferred_element_type=jnp.float32) * scale
             first = 2 * (group * block + j)
             for hemi in range(2):
                 for part in range(2):
                     for field in range(fields):
-                        at = hemi * row_total + (part * fields + field) * levels
+                        row = hemi * row_total + (part * fields + field) * levels
                         target = pl.ds(hemi * levels * stride + first + part, levels, stride=stride)
                         for tile in range(tiles):
                             lanes = slice(tile * LANES, (tile + 1) * LANES)
-                            rows_ref[field, tile, target, :] = halves[at : at + levels, lanes]
-
-    for group in range(slots // block):
-        pl.when(step == group)(functools.partial(run, group))
-
-    @pl.when(step == pl.num_programs(0) - 1)
-    def _():
-        for field in range(fields):
-            for tile in range(tiles):
-                lanes = pl.ds((field * tiles + tile) * LANES, LANES)
-                out_ref[:, lanes] = rows_ref[field, tile].astype(out_ref.dtype)
+                            rows_ref[field, tile, target, :] = halves[row : row + levels, lanes]
+    for field in range(fields):
+        for tile in range(tiles):
+            lanes = pl.ds((field * tiles + tile) * LANES, LANES)
+            out_ref[:, lanes] = rows_ref[field, tile].astype(out_ref.dtype)
 
 
 def synthesize(first, owner_table, spec_rows, legendre, chunk, fields, levels, least):
     slots, row_total, degrees = spec_rows.shape
     block = slots // len(least)
     rows = 2 * levels * 2 * slots
-    at, tiles = chunk
+    tiles = chunk[1]
     shape = (rows, fields * tiles * LANES)
+    held = []
+    for start in least:
+        held.append(pltpu.VMEM((block, row_total, degrees - start), jnp.bfloat16))
+        held.append(pltpu.VMEM((block, degrees - start, tiles * LANES), jnp.bfloat16))
     return pl.pallas_call(
-        functools.partial(synthesis_kernel, slots, levels, fields, least, 1.0 / math.sqrt(degrees)),
-        grid_spec=pltpu.PrefetchScalarGridSpec(
-            num_scalar_prefetch=2,
-            grid=(slots // block,),
-            in_specs=[
-                pl.BlockSpec((block, row_total, degrees), lambda i, *_: (i, 0, 0)),
-            ]
-            + [pl.BlockSpec((block, degrees, LANES), lambda i, *_, t=at + t: (i, 0, t)) for t in range(tiles)],
-            out_specs=pl.BlockSpec(shape, lambda i, *_: (0, 0)),
-            scratch_shapes=[pltpu.VMEM((fields, tiles, rows, LANES), jnp.float32)],
-        ),
+        functools.partial(synthesis_kernel, slots, levels, fields, least, chunk, 1.0 / math.sqrt(degrees)),
+        in_specs=[pl.BlockSpec(memory_space=pltpu.SMEM)] * 2 + [pl.BlockSpec(memory_space=pl.ANY)] * 2,
+        out_specs=pl.BlockSpec(shape, lambda: (0, 0)),
         out_shape=jax.ShapeDtypeStruct(shape, jnp.bfloat16),
+        scratch_shapes=[
+            pltpu.VMEM((fields, tiles, rows, LANES), jnp.float32),
+            pltpu.SemaphoreType.DMA((2 * len(least),)),
+            *held,
+        ],
         compiler_params=pltpu.CompilerParams(vmem_limit_bytes=VMEM_BYTES),
         cost_estimate=pl.CostEstimate(
             flops=4 * slots * row_total * degrees * tiles * LANES,
@@ -79,7 +89,7 @@
             transcendentals=0,
         ),
         name="synthesis",
-    )(first, owner_table, spec_rows, *[legendre] * tiles)
+    )(first, owner_table, spec_rows, legendre)
 
 
 def longitude_kernel(fields, grid_scale, zonal_scale, rows_ref, by_lon_ref, by_wave_ref, out_ref, sum_ref):
@@ -167,23 +177,19 @@
     )(arrived)
 
 
-def analysis_kernel(chunks, least, adds, *refs):
-    folded_refs = refs[:chunks]
-    even_ref, odd_ref = refs[chunks : chunks + 2]
-    out_ref = refs[-1]
-    table_refs = refs[chunks + 2 : -2 if adds else -1]
+def analysis_kernel(least, folded_ref, even_ref, odd_ref, *refs):
+    table_refs, out_ref = refs[:-1], refs[-1]
     row_total, degrees = out_ref.shape[1:]
     step = pl.program_id(0)
 
     def run(group):
         start = least[group]
         for j in range(out_ref.shape[0]):
-            folded = jnp.concatenate([ref[j] for ref in folded_refs], axis=1)
             table = jnp.concatenate([ref[j, start:, :] for ref in table_refs], axis=1)
-            sums = lax.dot_general(folded, table, (((1,), (1,)), ((), ())), preferred_element_type=jnp.float32)
+            sums = lax.dot_general(
+                folded_ref[j], table, (((1,), (1,)), ((), ())), preferred_element_type=jnp.float32
+            )
             kept = sums[:row_total] * even_ref[j, :, start:] + sums[row_total:] * odd_ref[j, :, start:]
-            if adds:
-                kept = kept + refs[-2][j, :, start:]
             out_ref[j, :, start:] = kept
             if start:
                 out_ref[j, :, :start] = jnp.zeros((row_total, start), out_ref.dtype)
@@ -192,30 +198,130 @@
         pl.when(step == group)(functools.partial(run, group))
 
 
-def analyze(folded, even, odd, legendre, row_total, least, first_tile, base=None):
+def analyze(folded, even, odd, legendre, row_total, least, chunk):
     slots, degrees, _ = legendre.shape
     block = slots // len(least)
-    lat_count = sum(x.shape[2] for x in folded)
-    tiles = lat_count // LANES
+    at, tiles = chunk
     mask_spec = pl.BlockSpec((block, 1, degrees), lambda i: (i, 0, 0))
-    sums_spec = pl.BlockSpec((block, row_total, degrees), lambda i: (i, 0, 0))
     return pl.pallas_call(
-        functools.partial(analysis_kernel, len(folded), least, base is not None),
+        functools.partial(analysis_kernel, least),
         grid=(len(least),),
-        in_specs=[pl.BlockSpec((block,) + x.shape[1:], lambda i: (i, 0, 0)) for x in folded]
-        + [mask_spec, mask_spec]
-        + [pl.BlockSpec((block, degrees, LANES), lambda i, t=first_tile + t: (i, 0, t)) for t in range(tiles)]
-        + ([sums_spec] if base is not None else []),
-        out_specs=sums_spec,
+        in_specs=[pl.BlockSpec((block,) + folded.shape[1:], lambda i: (i, 0, 0)), mask_spec, mask_spec]
+        + [pl.BlockSpec((block, degrees, LANES), lambda i, t=at + t: (i, 0, t)) for t in range(tiles)],
+        out_specs=pl.BlockSpec((block, row_total, degrees), lambda i: (i, 0, 0)),
         out_shape=jax.ShapeDtypeStruct((slots, row_total, degrees), jnp.float32),
         compiler_params=pltpu.CompilerParams(vmem_limit_bytes=VMEM_BYTES),
         cost_estimate=pl.CostEstimate(
-            flops=4 * slots * row_total * degrees * lat_count,
-            bytes_accessed=2 * slots * (degrees * lat_count + 2 * row_total * (lat_count + degrees)),
+            flops=4 * slots * row_total * degrees * tiles * LANES,
+            bytes_accessed=2 * slots * (degrees * tiles * LANES + 2 * row_total * (tiles * LANES + degrees)),
             transcendentals=0,
         ),
         name="analysis",
-    )(*folded, even, odd, *[legendre] * tiles, *([base] if base is not None else []))
+    )(folded, even, odd, *[legendre] * tiles)
+
+
+def closing_kernel(
+    levels, fields, least, chunk, arrived_ref, table_ref, base_ref, even_ref, odd_ref, out_ref, *refs
+):
+    got_ref, north_ref, south_ref, sems = refs[:4]
+    held = refs[4:]
+    at, tiles = chunk
+    groups = len(least)
+    slots, row_total, degrees = base_ref.shape
+    block = slots // groups
+    stride = 2 * slots
+    half = levels * stride
+    arriving = [
+        pltpu.make_async_copy(
+            arrived_ref.at[:, pl.ds(field * tiles * LANES, tiles * LANES)], got_ref.at[field], sems.at[3 * groups + field]
+        )
+        for field in range(fields)
+    ]
+    tables, sums, results = [], [], []
+    for group, start in enumerate(least):
+        mine = pl.ds(group * block, block)
+        left = pl.ds(start, degrees - start)
+        lanes = pl.ds(at * LANES, tiles * LANES)
+        held_table, held_sums = held[2 * group], held[2 * group + 1]
+        tables.append(pltpu.make_async_copy(table_ref.at[mine, left, lanes], held_table, sems.at[3 * group]))
+        sums.append(pltpu.make_async_copy(base_ref.at[mine, :, left], held_sums, sems.at[3 * group + 1]))
+        results.append(pltpu.make_async_copy(held_sums, out_ref.at[mine, :, left], sems.at[3 * group + 2]))
+    for copy in arriving:
+        copy.start()
+    for group in range(groups):
+        tables[group].start()
+        sums[group].start()
+    for field in range(fields):
+        arriving[field].wait()
+        for tile in range(tiles):
+            lanes = pl.ds(tile * LANES, LANES)
+            north = got_ref[field, :half, lanes].astype(jnp.float32)
+            south = got_ref[field, half:, lanes].astype(jnp.float32)
+            north_ref[field, tile] = north + south
+            south_ref[field, tile] = north - south
+    for group, start in enumerate(least):
+        tables[group].wait()
+        sums[group].wait()
+        held_table, held_sums = held[2 * group], held[2 * group + 1]
+        for j in range(block):
+            slot = group * block + j
+            folded = jnp.concatenate(
+                [
+                    jnp.concatenate(
+                        [
+                            ref[field, tile, pl.ds(2 * slot + part, levels, stride=stride), :].astype(jnp.bfloat16)
+                            for ref in (north_ref, south_ref)
+                            for part in range(2)
+                            for field in range(fields)
+                        ],
+                        axis=0,
+                    )
+                    for tile in range(tiles)
+                ],
+                axis=1,
+            )
+            more = lax.dot_general(
+                folded, held_table[j], (((1,), (1,)), ((), ())), preferred_element_type=jnp.float32
+            )
+            even, odd = even_ref[slot, :, start:], odd_ref[slot, :, start:]
+            held_sums[j] = held_sums[j] + more[:row_total] * even + more[row_total:] * odd
+        results[group].start()
+    for copy in results:
+        copy.wait()
+
+
+def close(arrived, base, even, odd, legendre, fields, levels, least, chunk):
+    slots, row_total, degrees = base.shape
+    block = slots // len(least)
+    rows, width = arrived.shape
+    tiles = chunk[1]
+    half = pltpu.VMEM((fields, tiles, rows // 2, LANES), jnp.float32)
+    held = []
+    for start in least:
+        held.append(pltpu.VMEM((block, degrees - start, tiles * LANES), jnp.bfloat16))
+        held.append(pltpu.VMEM((block, row_total, degrees - start), jnp.float32))
+    anywhere = pl.BlockSpec(memory_space=pl.ANY)
+    return pl.pallas_call(
+        functools.partial(closing_kernel, levels, fields, least, chunk),
+        in_specs=[anywhere, anywhere, anywhere] + [pl.BlockSpec(even.shape, lambda: (0, 0, 0))] * 2,
+        out_specs=anywhere,
+        out_shape=jax.ShapeDtypeStruct(base.shape, jnp.float32),
+        input_output_aliases={2: 0},
+        scratch_shapes=[
+            pltpu.VMEM((fields, rows, tiles * LANES), jnp.bfloat16),
+            half,
+            half,
+            pltpu.SemaphoreType.DMA((3 * len(least) + fields,)),
+            *held,
+        ],
+        compiler_params=pltpu.CompilerParams(vmem_limit_bytes=VMEM_BYTES),
+        cost_estimate=pl.CostEstimate(
+            flops=4 * slots * row_total * degrees * tiles * LANES,
+            bytes_accessed=8 * slots * row_total * degrees + 2 * rows * width,
+            transcendentals=0,
+        ),
+        name="closing",
+    )(arrived, legendre, base, even, odd)
 
 
 def after(value, *others):
@@ -286,8 +392,8 @@
     first = lax.axis_index(AXES).astype(jnp.int32) * slots
     spec_rows = spectral.reshape(slots, row_total, degrees)
     least = tuple(8 * g * levels for g in range(slots // 4))
-    cut = tiles // 2
-    chunks = [(cut, tiles - cut), (0, cut)]
+    cut = tiles - tiles // 2
+    chunks = [(0, cut), (cut, tiles - cut)]
 
     def send(spec, chunk):
         return synthesize(first.reshape(1), owner_table, spec, legendre, chunk, fields, levels, least)
@@ -305,9 +411,9 @@
     scale = 1.0 / math.sqrt(2 * half_lat)
     even = jnp.where((distance >= 0) & (distance % 2 == 0), scale, 0.0).astype(jnp.float32)[:, None, :]
     odd = jnp.where((distance >= 0) & (distance % 2 != 0), scale, 0.0).astype(jnp.float32)[:, None, :]
-    out = analyze([fold(returned[0], slots, levels, fields)], even, odd, legendre, row_total, least, cut)
-    last = fold(after(returned[1], out), slots, levels, fields)
-    out = analyze([last], even, odd, legendre, row_total, least, 0, out)
+    base = analyze(fold(returned[0], slots, levels, fields), even, odd, legendre, row_total, least, chunks[0])
+    last = after(returned[1], base)
+    out = close(last, base, even, odd, legendre, fields, levels, least, chunks[1])
     return out.reshape(slots, 2, fields, levels, degrees)
 
 

time: 342 us -> 330 us (0.965)
  Pallas kernels: 116 us -> 102 us
    pallas_call x2, Pallas kernels: 19.7 us -> 14.3 us  [synthesize(): pl.pallas_call(functools.partial(synthesis_kernel, slots, levels, fields,...]
    pallas_call x2 -> x1, Pallas kernels: 11.3 us -> 6.26 us  [fold(): pl.pallas_call(functools.partial(fold_kernel, slots, levels, fields), in_...]
    pallas_call x2, Pallas kernels: 21 us -> 17.1 us  [the longest x1 10.5 us: analyze(): pl.pallas_call(functools.partial(analysis_kernel, least), grid=(len(least...]
where the time goes in v1:
time: 330 us; the launch traced here: 329 us
  waiting for transfers between devices  194 us (59%)
  Pallas kernels  102 us (31%)
  starting transfers between devices  23.5 us (7%)
  local copies, waits for them, and re-layouts  5.18 us (2%)
  other arithmetic  3.96 us (1%)
    all_to_all x4, waiting for transfers between devices, exchange(): return lax.all_to_all(rows, AXES, split_axis=0, concat_axis=0, tiled=True)  194 us
    pallas_call x2, Pallas kernels, longitudes(): pl.pallas_call(functools.partial(longitude_kernel, fields, 1.0 / math.sqr...  52.6 us
    all_to_all x4, starting transfers between devices, exchange(): return lax.all_to_all(rows, AXES, split_axis=0, concat_axis=0, tiled=True)  23.5 us
    pallas_call x2, Pallas kernels, synthesize(): pl.pallas_call(functools.partial(synthesis_kernel, slots, levels, fields,...  14.3 us
    pallas_call x1, Pallas kernels, trig_tables(): pl.pallas_call(trig_kernel, grid=(depth // rows,), in_specs=[small, small...  11.8 us
    pallas_call x1, Pallas kernels, analyze(): pl.pallas_call(functools.partial(analysis_kernel, least), grid=(len(least...  10.5 us
    pallas_call x1, Pallas kernels, close(): pl.pallas_call(functools.partial(closing_kernel, levels, fields, least, c...  6.61 us
  transfers between devices with their start and end apart: 4, of which 4 were waited for; matrix products, arithmetic and copies ran while one was open for 3% of the time, Pallas kernels for 27%

profile of v1, /device:TPU:0, one launch (start us, length us, event | category | flops | bytes accessed | tf_op | source)
XLA Modules:
  0.0 329.3 jit_solution(6152043084655159917)
XLA Ops:
  0.0 7.9 %synthesis.2 = bf16[1280,1536]{1,0:T(8,128)(2,1)} custom-call(s32[1]{0:T(128)} %bitcast.first_ref, s32[640]{0:T(1024)} %owner_ref.3, bf16[20,128,640]{2,1,0:T(8,128)(2,1)} %bitcast.16, bf16[20,640,640]{2,1,0:T(8,128)(2,1)} %table_ref.5), custom_call_target="tpu_custom_call" | custom-call | flops 2516582400 | bytes 17039360 | tf_op jit(solution)/shard_map/synthesis/pallas_call | solution.py:75
  7.9 7.4 %all-to-all-start = ((bf16[32,40,1536]{2,1,0:T(8,128)(2,1)}), bf16[32,40,1536]{2,1,0:T(8,128)(2,1)}, u32[]{:S(2)}, u32[]{:S(2)}) async-start(bf16[32,40,1536]{2,1,0:T(8,128)(2,1)} %bitcast.15), calls=%async_computation | async-start | bytes 7864320 | tf_op jit(solution)/shard_map/all_to_all | solution.py:383
  15.3 6.4 %synthesis.3 = bf16[1280,1024]{1,0:T(8,128)(2,1)} custom-call(s32[1]{0:T(128)} %bitcast.first_ref, s32[640]{0:T(1024)} %owner_ref.3, bf16[20,128,640]{2,1,0:T(8,128)(2,1)} %bitcast.17, bf16[20,640,640]{2,1,0:T(8,128)(2,1)} %table_ref.5), custom_call_target="tpu_custom_call" | custom-call | flops 1677721600 | bytes 12451840 | tf_op jit(solution)/shard_map/synthesis/pallas_call | solution.py:75
  21.8 80.4 %all-to-all-done = bf16[32,40,1536]{2,1,0:T(8,128)(2,1)} async-done(((bf16[32,40,1536]{2,1,0:T(8,128)(2,1)}), bf16[32,40,1536]{2,1,0:T(8,128)(2,1)}, u32[]{:S(2)}, u32[]{:S(2)}) %all-to-all-start) | async-done | bytes 3932192 | tf_op jit(solution)/shard_map/all_to_all | solution.py:383
  102.1 5.7 %all-to-all-start.1 = ((bf16[32,40,1024]{2,1,0:T(8,128)(2,1)}), bf16[32,40,1024]{2,1,0:T(8,128)(2,1)}, u32[]{:S(2)}, u32[]{:S(2)}) async-start(bf16[32,40,1024]{2,1,0:T(8,128)(2,1)} %bitcast.18), calls=%async_computation.1 | async-start | bytes 5242880 | tf_op jit(solution)/shard_map/all_to_all | solution.py:383
  108.2 0.2 convert_element_type.12
  108.5 0.5 fusion.2
  109.0 2.4 fusion
  111.4 1.2 copy.10.cos_base_ref
  112.7 1.1 copy.11.sin_base_ref
  113.8 1.1 copy.12.cos_turn_ref
  114.8 1.1 copy.13.sin_turn_ref
  116.0 11.8 %trig.1 = (bf16[1280,2560]{1,0:T(8,128)(2,1)}, bf16[2560,1280]{1,0:T(8,128)(2,1)}) custom-call(f32[1280,20]{1,0:T(8,128)} %copy.10.cos_base_ref, f32[1280,20]{1,0:T(8,128)} %copy.11.sin_base_ref, f32[1280,128]{1,0:T(8,128)} %copy.12.cos_turn_ref, f32[1280,128]{1,0:T(8,128)} %copy.13.sin_turn_ref, f32[20,1280]{1,0:T(8,128)} %bitcast.24, f32[20,1280]{1,0:T(8,128)} %bitcast.23, ...), custom_call_target="tpu_custom_call" | custom-call | flops 26214400 | bytes 13107200 | tf_op jit(solution)/shard_map/trig/pallas_call | solution.py:362
  127.7 30.8 %longitudes.3 = bf16[1280,1536]{1,0:T(8,128)(2,1)} custom-call(bf16[1280,1536]{1,0:T(8,128)(2,1)} %bitcast.3.rows_ref, bf16[2560,1280]{1,0:T(8,128)(2,1)} %get-tuple-element.24.by_lon_ref, bf16[1280,2560]{1,0:T(8,128)(2,1)} %get-tuple-element.25.by_wave_ref), custom_call_target="tpu_custom_call" | custom-call | flops 20132659200 | bytes 20971520 | tf_op jit(solution)/shard_map/longitudes/pallas_call | solution.py:120
  158.5 8.1 %all-to-all-done.1 = bf16[32,40,1024]{2,1,0:T(8,128)(2,1)} async-done(((bf16[32,40,1024]{2,1,0:T(8,128)(2,1)}), bf16[32,40,1024]{2,1,0:T(8,128)(2,1)}, u32[]{:S(2)}, u32[]{:S(2)}) %all-to-all-start.1) | async-done | bytes 2621472 | tf_op jit(solution)/shard_map/all_to_all | solution.py:383
  166.6 4.9 %all-to-all-start.2 = ((bf16[32,40,1536]{2,1,0:T(8,128)(2,1)}), bf16[32,40,1536]{2,1,0:T(8,128)(2,1)}, u32[]{:S(2)}, u32[]{:S(2)}) async-start(bf16[32,40,1536]{2,1,0:T(8,128)(2,1)} %bitcast.21), calls=%async_computation.2 | async-start | bytes 7864320 | tf_op jit(solution)/shard_map/all_to_all | solution.py:383
  171.5 21.8 %longitudes.2 = bf16[1280,1024]{1,0:T(8,128)(2,1)} custom-call(bf16[1280,1024]{1,0:T(8,128)(2,1)} %bitcast.5.rows_ref, bf16[2560,1280]{1,0:T(8,128)(2,1)} %get-tuple-element.24.by_lon_ref, bf16[1280,2560]{1,0:T(8,128)(2,1)} %get-tuple-element.25.by_wave_ref), custom_call_target="tpu_custom_call" | custom-call | flops 13421772800 | bytes 18350080 | tf_op jit(solution)/shard_map/longitudes/pallas_call | solution.py:120
  193.3 64.7 %all-to-all-done.2 = bf16[32,40,1536]{2,1,0:T(8,128)(2,1)} async-done(((bf16[32,40,1536]{2,1,0:T(8,128)(2,1)}), bf16[32,40,1536]{2,1,0:T(8,128)(2,1)}, u32[]{:S(2)}, u32[]{:S(2)}) %all-to-all-start.2) | async-done | bytes 3932192 | tf_op jit(solution)/shard_map/all_to_all | solution.py:383
  258.1 5.5 %all-to-all-start.3 = ((bf16[32,40,1024]{2,1,0:T(8,128)(2,1)}), bf16[32,40,1024]{2,1,0:T(8,128)(2,1)}, u32[]{:S(2)}, u32[]{:S(2)}) async-start(bf16[32,40,1024]{2,1,0:T(8,128)(2,1)} %bitcast.22), calls=%async_computation.3 | async-start | bytes 5242880 | tf_op jit(solution)/shard_map/all_to_all | solution.py:383
  263.7 1.0 and_select_fusion
  264.7 6.3 %fold.1.folded_ref = bf16[20,256,384]{2,1,0:T(8,128)(2,1)} custom-call(bf16[1280,1536]{1,0:T(8,128)(2,1)} %bitcast.11.arrived_ref), custom_call_target="tpu_custom_call" | custom-call | flops 3932160 | bytes 7864320 | tf_op jit(solution)/shard_map/fold/pallas_call | solution.py:168
  270.9 10.5 %analysis.1.base_ref = f32[20,128,640]{2,1,0:T(8,128)} custom-call(bf16[20,256,384]{2,1,0:T(8,128)(2,1)} %fold.1.folded_ref, f32[20,1,640]{2,1,0:T(1,128)} %get-tuple-element.34.even_ref, f32[20,1,640]{2,1,0:T(1,128)} %get-tuple-element.33.odd_ref, bf16[20,640,640]{2,1,0:T(8,128)(2,1)} %table_ref.5, bf16[20,640,640]{2,1,0:T(8,128)(2,1)} %table_ref.5, ...), custom_call_target="tpu_custom_call" | custom-call | flops 2516582400 | bytes 20316160 | tf_op jit(solution)/shard_map/analysis/pallas_call | solution.py:206
  281.5 41.1 %all-to-all-done.3 = bf16[32,40,1024]{2,1,0:T(8,128)(2,1)} async-done(((bf16[32,40,1024]{2,1,0:T(8,128)(2,1)}), bf16[32,40,1024]{2,1,0:T(8,128)(2,1)}, u32[]{:S(2)}, u32[]{:S(2)}) %all-to-all-start.3) | async-done | bytes 2621472 | tf_op jit(solution)/shard_map/all_to_all | solution.py:383
  322.5 6.6 %closing.1 = f32[20,128,640]{2,1,0:T(8,128)} custom-call(bf16[1280,1024]{1,0:T(8,128)(2,1)} %bitcast.13.arrived_ref, bf16[20,640,640]{2,1,0:T(8,128)(2,1)} %table_ref.5, f32[20,128,640]{2,1,0:T(8,128)} %analysis.1.base_ref, f32[20,1,640]{2,1,0:T(1,128)} %get-tuple-element.34.even_ref, ...), custom_call_target="tpu_custom_call", output_to_operand_aliasing={{}: (2, {})} | custom-call | flops 1677721600 | bytes 15728640 | tf_op jit(solution)/shard_map/closing/pallas_call | solution.py:304
  (18 shorter events, 0.5 us)
Async XLA Ops:
  7.9 94.2 %all-to-all-start = ((bf16[32,40,1536]{2,1,0:T(8,128)(2,1)}), bf16[32,40,1536]{2,1,0:T(8,128)(2,1)}, u32[]{:S(2)}, u32[]{:S(2)}) async-start(bf16[32,40,1536]{2,1,0:T(8,128)(2,1)} %bitcast.15), calls=%async_computation | async-start | bytes 7864320 | tf_op jit(solution)/shard_map/all_to_all | solution.py:383
  21.8 86.1 %copy-start.5 = (f32[2]{0:T(128)S(1)}, f32[2]{0:T(128)}, u32[]{:S(2)}) copy-start(f32[2]{0:T(128)} %constant.52.clone) | copy-start | bytes 28
  21.8 86.3 %copy-start.4 = (s32[640]{0:T(1024)S(1)}, s32[640]{0:T(1024)}, u32[]{:S(2)}) copy-start(s32[640]{0:T(1024)} %owner_ref.3) | copy-start | bytes 7684
  102.1 64.5 %all-to-all-start.1 = ((bf16[32,40,1024]{2,1,0:T(8,128)(2,1)}), bf16[32,40,1024]{2,1,0:T(8,128)(2,1)}, u32[]{:S(2)}, u32[]{:S(2)}) async-start(bf16[32,40,1024]{2,1,0:T(8,128)(2,1)} %bitcast.18), calls=%async_computation.1 | async-start | bytes 5242880 | tf_op jit(solution)/shard_map/all_to_all | solution.py:383
  109.0 6.9 %copy-start.2 = (f32[1280,20]{0,1:T(8,128)}, f32[1280,20]{0,1:T(8,128)S(1)}, u32[]{:S(2)}) copy-start(f32[1280,20]{0,1:T(8,128)S(1)} %get-tuple-element.21) | copy-start | bytes 307204
  109.0 6.9 %copy-start.3 = (f32[1280,20]{0,1:T(8,128)}, f32[1280,20]{0,1:T(8,128)S(1)}, u32[]{:S(2)}) copy-start(f32[1280,20]{0,1:T(8,128)S(1)} %get-tuple-element.20) | copy-start | bytes 307204
  111.4 4.5 %copy-start = (f32[1280,128]{0,1:T(8,128)}, f32[1280,128]{0,1:T(8,128)S(1)}, u32[]{:S(2)}) copy-start(f32[1280,128]{0,1:T(8,128)S(1)} %get-tuple-element.23) | copy-start | bytes 1966084
  111.4 4.5 %copy-start.1 = (f32[1280,128]{0,1:T(8,128)}, f32[1280,128]{0,1:T(8,128)S(1)}, u32[]{:S(2)}) copy-start(f32[1280,128]{0,1:T(8,128)S(1)} %get-tuple-element.22) | copy-start | bytes 1966084
  166.6 91.4 %all-to-all-start.2 = ((bf16[32,40,1536]{2,1,0:T(8,128)(2,1)}), bf16[32,40,1536]{2,1,0:T(8,128)(2,1)}, u32[]{:S(2)}, u32[]{:S(2)}) async-start(bf16[32,40,1536]{2,1,0:T(8,128)(2,1)} %bitcast.21), calls=%async_computation.2 | async-start | bytes 7864320 | tf_op jit(solution)/shard_map/all_to_all | solution.py:383
  258.1 64.5 %all-to-all-start.3 = ((bf16[32,40,1024]{2,1,0:T(8,128)(2,1)}), bf16[32,40,1024]{2,1,0:T(8,128)(2,1)}, u32[]{:S(2)}, u32[]{:S(2)}) async-start(bf16[32,40,1024]{2,1,0:T(8,128)(2,1)} %bitcast.22), calls=%async_computation.3 | async-start | bytes 5242880 | tf_op jit(solution)/shard_map/all_to_all | solution.py:383

commit v2 on v1

--- a/solution.py
+++ b/solution.py
@@ -380,7 +380,7 @@
 
 
 def exchange(rows):
-    return lax.all_to_all(rows, AXES, split_axis=0, concat_axis=0, tiled=True)
+    return lax.all_to_all(rows, AXES[::-1], split_axis=0, concat_axis=0, tiled=True)
 
 
 def by_hemisphere_and_level(spectral, legendre, owner_table):
@@ -402,7 +402,9 @@
     small = send(after(spec_rows, large), chunks[1])
     arrived = [exchange(large)]
     arrived.append(exchange(after(small, *arrived)))
-    by_wave, by_lon = trig_tables(after(owner_table, large), lon_count, small)
+    bands, planes = lax.axis_size("band"), lax.axis_size("grp")
+    arriving = jnp.swapaxes(owner_table.reshape(bands, planes, slots), 0, 1).reshape(-1)
+    by_wave, by_lon = trig_tables(after(arriving, large), lon_count, small)
     zonal = [longitudes(rows, by_lon, by_wave, fields) for rows in arrived]
     returned = [exchange(zonal[0])]
     returned.append(exchange(after(zonal[1], *returned)))

time: 330 us -> 332 us (level)
  waiting for transfers between devices: 194 us -> 200 us
  starting transfers between devices: 23.5 us -> 19.9 us
    all_to_all x4, waiting for transfers between devices: 194 us -> 200 us  [exchange(): lax.all_to_all(rows, AXES[::-1], split_axis=0, concat_axis=0, tiled=True)]
    all_to_all x4, starting transfers between devices: 23.5 us -> 19.9 us  [exchange(): lax.all_to_all(rows, AXES[::-1], split_axis=0, concat_axis=0, tiled=True)]
  transfers between devices with their start and end apart: 4 -> 4, of which waited for: 4 -> 4; matrix products, arithmetic and copies ran while one was open for 3% -> 3% of each run, Pallas kernels for 27% -> 26%
where the time goes in v2:
time: 332 us; the launch traced here: 331 us
  waiting for transfers between devices  200 us (60%)
  Pallas kernels  102 us (31%)
  starting transfers between devices  19.9 us (6%)
  local copies, waits for them, and re-layouts  5.4 us (2%)
  other arithmetic  3.96 us (1%)
    all_to_all x4, waiting for transfers between devices, exchange(): lax.all_to_all(rows, AXES[::-1], split_axis=0, concat_axis=0, tiled=True)  200 us
    pallas_call x2, Pallas kernels, longitudes(): pl.pallas_call(functools.partial(longitude_kernel, fields, 1.0 / math.sqr...  52.6 us
    all_to_all x4, starting transfers between devices, exchange(): lax.all_to_all(rows, AXES[::-1], split_axis=0, concat_axis=0, tiled=True)  19.9 us
    pallas_call x2, Pallas kernels, synthesize(): pl.pallas_call(functools.partial(synthesis_kernel, slots, levels, fields,...  14.3 us
    pallas_call x1, Pallas kernels, trig_tables(): pl.pallas_call(trig_kernel, grid=(depth // rows,), in_specs=[small, small...  11.8 us
    pallas_call x1, Pallas kernels, analyze(): pl.pallas_call(functools.partial(analysis_kernel, least), grid=(len(least...  10.5 us
  transfers between devices with their start and end apart: 4, of which 4 were waited for; matrix products, arithmetic and copies ran while one was open for 3% of the time, Pallas kernels for 26%

profile of v2, /device:TPU:0, one launch (start us, length us, event | category | flops | bytes accessed | tf_op | source)
XLA Modules:
  0.0 331.3 jit_solution(4563832066072941665)
XLA Ops:
  0.0 7.9 %synthesis.2 = bf16[1280,1536]{1,0:T(8,128)(2,1)} custom-call(s32[1]{0:T(128)} %bitcast.first_ref, s32[640]{0:T(1024)} %owner_ref.3, bf16[20,128,640]{2,1,0:T(8,128)(2,1)} %bitcast.17, bf16[20,640,640]{2,1,0:T(8,128)(2,1)} %table_ref.5), custom_call_target="tpu_custom_call" | custom-call | flops 2516582400 | bytes 17039360 | tf_op jit(solution)/shard_map/synthesis/pallas_call | solution.py:75
  7.9 7.4 %all-to-all-start = ((bf16[32,40,1536]{2,1,0:T(8,128)(2,1)}), bf16[32,40,1536]{2,1,0:T(8,128)(2,1)}, u32[]{:S(2)}, u32[]{:S(2)}) async-start(bf16[32,40,1536]{2,1,0:T(8,128)(2,1)} %bitcast.16), calls=%async_computation | async-start | bytes 7864320 | tf_op jit(solution)/shard_map/all_to_all | solution.py:383
  15.3 6.4 %synthesis.3 = bf16[1280,1024]{1,0:T(8,128)(2,1)} custom-call(s32[1]{0:T(128)} %bitcast.first_ref, s32[640]{0:T(1024)} %owner_ref.3, bf16[20,128,640]{2,1,0:T(8,128)(2,1)} %bitcast.18, bf16[20,640,640]{2,1,0:T(8,128)(2,1)} %table_ref.5), custom_call_target="tpu_custom_call" | custom-call | flops 1677721600 | bytes 12451840 | tf_op jit(solution)/shard_map/synthesis/pallas_call | solution.py:75
  21.8 81.8 %all-to-all-done = bf16[32,40,1536]{2,1,0:T(8,128)(2,1)} async-done(((bf16[32,40,1536]{2,1,0:T(8,128)(2,1)}), bf16[32,40,1536]{2,1,0:T(8,128)(2,1)}, u32[]{:S(2)}, u32[]{:S(2)}) %all-to-all-start) | async-done | bytes 3932192 | tf_op jit(solution)/shard_map/all_to_all | solution.py:383
  103.6 4.3 %all-to-all-start.1 = ((bf16[32,40,1024]{2,1,0:T(8,128)(2,1)}), bf16[32,40,1024]{2,1,0:T(8,128)(2,1)}, u32[]{:S(2)}, u32[]{:S(2)}) async-start(bf16[32,40,1024]{2,1,0:T(8,128)(2,1)} %bitcast.19), calls=%async_computation.1 | async-start | bytes 5242880 | tf_op jit(solution)/shard_map/all_to_all | solution.py:383
  108.5 0.2 convert_element_type.12
  108.8 0.5 fusion.2
  109.3 2.4 fusion
  111.7 1.2 copy.15.cos_base_ref
  112.9 1.1 copy.16.sin_base_ref
  114.0 1.1 copy.17.cos_turn_ref
  115.1 1.1 copy.18.sin_turn_ref
  116.2 11.8 %trig.1 = (bf16[1280,2560]{1,0:T(8,128)(2,1)}, bf16[2560,1280]{1,0:T(8,128)(2,1)}) custom-call(f32[1280,20]{1,0:T(8,128)} %copy.15.cos_base_ref, f32[1280,20]{1,0:T(8,128)} %copy.16.sin_base_ref, f32[1280,128]{1,0:T(8,128)} %copy.17.cos_turn_ref, f32[1280,128]{1,0:T(8,128)} %copy.18.sin_turn_ref, f32[20,1280]{1,0:T(8,128)} %bitcast.25, f32[20,1280]{1,0:T(8,128)} %bitcast.24, ...), custom_call_target="tpu_custom_call" | custom-call | flops 26214400 | bytes 13107200 | tf_op jit(solution)/shard_map/trig/pallas_call | solution.py:362
  128.0 30.8 %longitudes.3 = bf16[1280,1536]{1,0:T(8,128)(2,1)} custom-call(bf16[1280,1536]{1,0:T(8,128)(2,1)} %bitcast.3.rows_ref, bf16[2560,1280]{1,0:T(8,128)(2,1)} %get-tuple-element.24.by_lon_ref, bf16[1280,2560]{1,0:T(8,128)(2,1)} %get-tuple-element.25.by_wave_ref), custom_call_target="tpu_custom_call" | custom-call | flops 20132659200 | bytes 20971520 | tf_op jit(solution)/shard_map/longitudes/pallas_call | solution.py:120
  158.8 9.1 %all-to-all-done.1 = bf16[32,40,1024]{2,1,0:T(8,128)(2,1)} async-done(((bf16[32,40,1024]{2,1,0:T(8,128)(2,1)}), bf16[32,40,1024]{2,1,0:T(8,128)(2,1)}, u32[]{:S(2)}, u32[]{:S(2)}) %all-to-all-start.1) | async-done | bytes 2621472 | tf_op jit(solution)/shard_map/all_to_all | solution.py:383
  168.0 4.2 %all-to-all-start.2 = ((bf16[32,40,1536]{2,1,0:T(8,128)(2,1)}), bf16[32,40,1536]{2,1,0:T(8,128)(2,1)}, u32[]{:S(2)}, u32[]{:S(2)}) async-start(bf16[32,40,1536]{2,1,0:T(8,128)(2,1)} %bitcast.22), calls=%async_computation.2 | async-start | bytes 7864320 | tf_op jit(solution)/shard_map/all_to_all | solution.py:383
  172.2 21.8 %longitudes.2 = bf16[1280,1024]{1,0:T(8,128)(2,1)} custom-call(bf16[1280,1024]{1,0:T(8,128)(2,1)} %bitcast.5.rows_ref, bf16[2560,1280]{1,0:T(8,128)(2,1)} %get-tuple-element.24.by_lon_ref, bf16[1280,2560]{1,0:T(8,128)(2,1)} %get-tuple-element.25.by_wave_ref), custom_call_target="tpu_custom_call" | custom-call | flops 13421772800 | bytes 18350080 | tf_op jit(solution)/shard_map/longitudes/pallas_call | solution.py:120
  194.0 66.4 %all-to-all-done.2 = bf16[32,40,1536]{2,1,0:T(8,128)(2,1)} async-done(((bf16[32,40,1536]{2,1,0:T(8,128)(2,1)}), bf16[32,40,1536]{2,1,0:T(8,128)(2,1)}, u32[]{:S(2)}, u32[]{:S(2)}) %all-to-all-start.2) | async-done | bytes 3932192 | tf_op jit(solution)/shard_map/all_to_all | solution.py:383
  260.4 3.9 %all-to-all-start.3 = ((bf16[32,40,1024]{2,1,0:T(8,128)(2,1)}), bf16[32,40,1024]{2,1,0:T(8,128)(2,1)}, u32[]{:S(2)}, u32[]{:S(2)}) async-start(bf16[32,40,1024]{2,1,0:T(8,128)(2,1)} %bitcast.23), calls=%async_computation.3 | async-start | bytes 5242880 | tf_op jit(solution)/shard_map/all_to_all | solution.py:383
  264.4 1.0 and_select_fusion
  265.4 6.3 %fold.1.folded_ref = bf16[20,256,384]{2,1,0:T(8,128)(2,1)} custom-call(bf16[1280,1536]{1,0:T(8,128)(2,1)} %bitcast.12.arrived_ref), custom_call_target="tpu_custom_call" | custom-call | flops 3932160 | bytes 7864320 | tf_op jit(solution)/shard_map/fold/pallas_call | solution.py:168
  271.7 10.5 %analysis.1.base_ref = f32[20,128,640]{2,1,0:T(8,128)} custom-call(bf16[20,256,384]{2,1,0:T(8,128)(2,1)} %fold.1.folded_ref, f32[20,1,640]{2,1,0:T(1,128)} %get-tuple-element.34.even_ref, f32[20,1,640]{2,1,0:T(1,128)} %get-tuple-element.33.odd_ref, bf16[20,640,640]{2,1,0:T(8,128)(2,1)} %table_ref.5, bf16[20,640,640]{2,1,0:T(8,128)(2,1)} %table_ref.5, ...), custom_call_target="tpu_custom_call" | custom-call | flops 2516582400 | bytes 20316160 | tf_op jit(solution)/shard_map/analysis/pallas_call | solution.py:206
  282.2 42.2 %all-to-all-done.3 = bf16[32,40,1024]{2,1,0:T(8,128)(2,1)} async-done(((bf16[32,40,1024]{2,1,0:T(8,128)(2,1)}), bf16[32,40,1024]{2,1,0:T(8,128)(2,1)}, u32[]{:S(2)}, u32[]{:S(2)}) %all-to-all-start.3) | async-done | bytes 2621472 | tf_op jit(solution)/shard_map/all_to_all | solution.py:383
  324.5 6.6 %closing.1 = f32[20,128,640]{2,1,0:T(8,128)} custom-call(bf16[1280,1024]{1,0:T(8,128)(2,1)} %bitcast.14.arrived_ref, bf16[20,640,640]{2,1,0:T(8,128)(2,1)} %table_ref.5, f32[20,128,640]{2,1,0:T(8,128)} %analysis.1.base_ref, f32[20,1,640]{2,1,0:T(1,128)} %get-tuple-element.34.even_ref, ...), custom_call_target="tpu_custom_call", output_to_operand_aliasing={{}: (2, {})} | custom-call | flops 1677721600 | bytes 15728640 | tf_op jit(solution)/shard_map/closing/pallas_call | solution.py:304
  (21 shorter events, 0.7 us)
Async XLA Ops:
  7.9 95.7 %all-to-all-start = ((bf16[32,40,1536]{2,1,0:T(8,128)(2,1)}), bf16[32,40,1536]{2,1,0:T(8,128)(2,1)}, u32[]{:S(2)}, u32[]{:S(2)}) async-start(bf16[32,40,1536]{2,1,0:T(8,128)(2,1)} %bitcast.16), calls=%async_computation | async-start | bytes 7864320 | tf_op jit(solution)/shard_map/all_to_all | solution.py:383
  21.8 86.1 %copy-start.4 = (s32[640]{0:T(1024)S(1)}, s32[640]{0:T(1024)}, u32[]{:S(2)}) copy-start(s32[640]{0:T(1024)} %owner_ref.3) | copy-start | bytes 7684
  21.8 86.4 %copy-start.5 = (f32[2]{0:T(128)S(1)}, f32[2]{0:T(128)}, u32[]{:S(2)}) copy-start(f32[2]{0:T(128)} %constant.52.clone) | copy-start | bytes 28
  103.6 64.4 %all-to-all-start.1 = ((bf16[32,40,1024]{2,1,0:T(8,128)(2,1)}), bf16[32,40,1024]{2,1,0:T(8,128)(2,1)}, u32[]{:S(2)}, u32[]{:S(2)}) async-start(bf16[32,40,1024]{2,1,0:T(8,128)(2,1)} %bitcast.19), calls=%async_computation.1 | async-start | bytes 5242880 | tf_op jit(solution)/shard_map/all_to_all | solution.py:383
  109.3 6.9 %copy-start.2 = (f32[1280,20]{0,1:T(8,128)}, f32[1280,20]{0,1:T(8,128)S(1)}, u32[]{:S(2)}) copy-start(f32[1280,20]{0,1:T(8,128)S(1)} %get-tuple-element.21) | copy-start | bytes 307204
  109.3 6.9 %copy-start.3 = (f32[1280,20]{0,1:T(8,128)}, f32[1280,20]{0,1:T(8,128)S(1)}, u32[]{:S(2)}) copy-start(f32[1280,20]{0,1:T(8,128)S(1)} %get-tuple-element.20) | copy-start | bytes 307204
  111.7 4.5 %copy-start = (f32[1280,128]{0,1:T(8,128)}, f32[1280,128]{0,1:T(8,128)S(1)}, u32[]{:S(2)}) copy-start(f32[1280,128]{0,1:T(8,128)S(1)} %get-tuple-element.23) | copy-start | bytes 1966084
  111.7 4.5 %copy-start.1 = (f32[1280,128]{0,1:T(8,128)}, f32[1280,128]{0,1:T(8,128)S(1)}, u32[]{:S(2)}) copy-start(f32[1280,128]{0,1:T(8,128)S(1)} %get-tuple-element.22) | copy-start | bytes 1966084
  168.0 92.4 %all-to-all-start.2 = ((bf16[32,40,1536]{2,1,0:T(8,128)(2,1)}), bf16[32,40,1536]{2,1,0:T(8,128)(2,1)}, u32[]{:S(2)}, u32[]{:S(2)}) async-start(bf16[32,40,1536]{2,1,0:T(8,128)(2,1)} %bitcast.22), calls=%async_computation.2 | async-start | bytes 7864320 | tf_op jit(solution)/shard_map/all_to_all | solution.py:383
  260.4 64.1 %all-to-all-start.3 = ((bf16[32,40,1024]{2,1,0:T(8,128)(2,1)}), bf16[32,40,1024]{2,1,0:T(8,128)(2,1)}, u32[]{:S(2)}, u32[]{:S(2)}) async-start(bf16[32,40,1024]{2,1,0:T(8,128)(2,1)} %bitcast.23), calls=%async_computation.3 | async-start | bytes 5242880 | tf_op jit(solution)/shard_map/all_to_all | solution.py:383

commit v3 on v2

--- a/solution.py
+++ b/solution.py
@@ -18,7 +18,7 @@
 ):
     at, tiles = chunk
     groups = len(least)
-    block = slots // groups
+    block = 4
     row_total, degrees = spec_ref.shape[1:]
     stride = 2 * slots
     copies = []
@@ -63,8 +63,9 @@
 
 
 def synthesize(first, owner_table, spec_rows, legendre, chunk, fields, levels, least):
-    slots, row_total, degrees = spec_rows.shape
-    block = slots // len(least)
+    _, row_total, degrees = spec_rows.shape
+    block = 4
+    slots = block * len(least)
     rows = 2 * levels * 2 * slots
     tiles = chunk[1]
     shape = (rows, fields * tiles * LANES)
@@ -92,10 +93,18 @@
     )(first, owner_table, spec_rows, legendre)
 
 
-def longitude_kernel(fields, grid_scale, zonal_scale, rows_ref, by_lon_ref, by_wave_ref, out_ref, sum_ref):
+def longitude_kernel(
+    fields, chunk, grid_scale, zonal_scale, rows_ref, far_ref, by_lon_ref, by_wave_ref, out_ref, far_out_ref, sum_ref
+):
     step = pl.program_id(0)
-    values = jnp.dot(by_lon_ref[...], rows_ref[...], preferred_element_type=jnp.float32) * grid_scale
+    near = rows_ref.shape[0]
+    values = jnp.dot(by_lon_ref[:, :near], rows_ref[...], preferred_element_type=jnp.float32)
     one = values.shape[1] // fields
+    each = far_ref.shape[1] // fields
+    starts = [field * each + chunk[0] * LANES for field in range(fields)]
+    far = jnp.concatenate([far_ref[:, start : start + one] for start in starts], axis=1)
+    values = values + jnp.dot(by_lon_ref[:, near:], far, preferred_element_type=jnp.float32)
+    values = values * grid_scale
     following = jnp.concatenate([values[:, one:], values[:, :one]], axis=1)
     product = (values * following).astype(jnp.bfloat16)
     share = jnp.dot(by_wave_ref[...], product, preferred_element_type=jnp.float32)
@@ -110,23 +119,27 @@
 
     @pl.when(step == pl.num_programs(0) - 1)
     def _():
-        out_ref[...] = (sum_ref[...] * zonal_scale).astype(out_ref.dtype)
-
-
-def longitudes(rows, by_lon, by_wave, fields):
-    depth, width = rows.shape
+        out_ref[...] = (sum_ref[:near, :] * zonal_scale).astype(out_ref.dtype)
+        far_out_ref[...] = (sum_ref[near:, :] * zonal_scale).astype(far_out_ref.dtype)
+
+
+def longitudes(rows, far, by_lon, by_wave, fields, chunk):
+    depth, width = rows.shape[0] + far.shape[0], rows.shape[1]
     lon_count = by_lon.shape[0]
     lon_block = lon_count // 5
+    near_spec = pl.BlockSpec(rows.shape, lambda i: (0, 0))
+    far_out = jax.ShapeDtypeStruct((far.shape[0], width), jnp.bfloat16)
     return pl.pallas_call(
-        functools.partial(longitude_kernel, fields, 1.0 / math.sqrt(depth // 2), 2.0 / math.sqrt(lon_count)),
+        functools.partial(longitude_kernel, fields, chunk, 1.0 / math.sqrt(depth // 2), 2.0 / math.sqrt(lon_count)),
         grid=(lon_count // lon_block,),
         in_specs=[
-            pl.BlockSpec((depth, width), lambda i: (0, 0)),
+            near_spec,
+            pl.BlockSpec(far.shape, lambda i: (0, 0)),
             pl.BlockSpec((lon_block, depth), lambda i: (i, 0)),
             pl.BlockSpec((depth, lon_block), lambda i: (0, i)),
         ],
-        out_specs=pl.BlockSpec((depth, width), lambda i: (0, 0)),
-        out_shape=jax.ShapeDtypeStruct((depth, width), jnp.bfloat16),
+        out_specs=[near_spec, pl.BlockSpec(far_out.shape, lambda i: (0, 0))],
+        out_shape=[jax.ShapeDtypeStruct(rows.shape, jnp.bfloat16), far_out],
         scratch_shapes=[pltpu.VMEM((depth, width), jnp.float32)],
         compiler_params=pltpu.CompilerParams(vmem_limit_bytes=VMEM_BYTES),
         cost_estimate=pl.CostEstimate(
@@ -135,7 +148,118 @@
             transcendentals=0,
         ),
         name="longitudes",
-    )(rows, by_lon, by_wave)
+    )(rows, far, by_lon, by_wave)
+
+
+def far_synthesis_kernel(levels, fields, scale, place_ref, waves_ref, own_ref, partner_ref, *refs):
+    out_refs, rows_ref = refs[:-1], refs[-1]
+    tiles = rows_ref.shape[1]
+    half_lat = tiles * LANES
+    stride = rows_ref.shape[2] // levels
+    degree = lax.broadcasted_iota(jnp.int32, (1, LANES), 1)
+    for slot in range(8):
+        pack_ref, local = (own_ref, slot) if slot < 4 else (partner_ref, slot - 4)
+        rows = pl.ds(min(local, 2) * LANES, LANES)
+        distance = degree - waves_ref[slot] + (LANES // 2 if local == 2 else 0)
+        keep = jnp.where(distance >= 0, 1.0, 0.0)
+        if local >= 2:
+            keep = jnp.where((degree < LANES // 2) if local == 2 else (degree >= LANES // 2), keep, 0.0)
+        turned = jnp.where(distance % 2 == 0, keep, -keep)
+        sign = jnp.where(place_ref[0] == 0, keep, turned)
+        spec = pack_ref[rows, half_lat:]
+        table = pack_ref[rows, :half_lat]
+        sums = jnp.dot(spec * sign.astype(spec.dtype), table, preferred_element_type=jnp.float32) * scale
+        for part in range(2):
+            for field in range(fields):
+                row = (part * fields + field) * levels
+                for tile in range(tiles):
+                    target = pl.ds(2 * slot + part, levels, stride=stride)
+                    rows_ref[field, tile, target, :] = sums[row : row + levels, tile * LANES : (tile + 1) * LANES]
+    for apart, out_ref in enumerate(out_refs):
+        rows = pl.ds(pl.multiple_of((place_ref[1] ^ apart) * stride, stride), stride)
+        for field in range(fields):
+            for tile in range(tiles):
+                lanes = pl.ds((field * tiles + tile) * LANES, LANES)
+                out_ref[:, lanes] = rows_ref[field, tile, rows, :].astype(out_ref.dtype)
+
+
+def far_synthesize(place, waves, own, partner, levels, fields, scale):
+    tiles = own.shape[1] // LANES - 1
+    shape = (16, fields * tiles * LANES)
+    whole = pl.BlockSpec(own.shape, lambda: (0, 0))
+    return pl.pallas_call(
+        functools.partial(far_synthesis_kernel, levels, fields, scale),
+        in_specs=[pl.BlockSpec(memory_space=pltpu.SMEM)] * 2 + [whole, whole],
+        out_specs=[pl.BlockSpec(shape, lambda: (0, 0))] * levels,
+        out_shape=[jax.ShapeDtypeStruct(shape, jnp.bfloat16)] * levels,
+        scratch_shapes=[pltpu.VMEM((fields, tiles, 16 * levels, LANES), jnp.float32)],
+        compiler_params=pltpu.CompilerParams(vmem_limit_bytes=VMEM_BYTES),
+        cost_estimate=pl.CostEstimate(
+            flops=16 * 2 * fields * levels * LANES * tiles * LANES, bytes_accessed=4 * own.size, transcendentals=0
+        ),
+        name="far_synthesis",
+    )(place, waves, own, partner)
+
+
+def far_analysis_kernel(levels, fields, chunks, place_ref, own_ref, partner_ref, *refs):
+    zonal_refs, own_out_ref, partner_out_ref, rows_ref = refs[:levels], refs[-3], refs[-2], refs[-1]
+    tiles = rows_ref.shape[1]
+    stride = rows_ref.shape[2] // levels
+    for apart, zonal_ref in enumerate(zonal_refs):
+        rows = pl.ds(pl.multiple_of((place_ref[1] ^ apart) * stride, stride), stride)
+        offset = 0
+        for at, count in chunks:
+            for field in range(fields):
+                for tile in range(at, at + count):
+                    rows_ref[field, tile, rows, :] = zonal_ref[:, pl.ds(offset, LANES)].astype(jnp.float32)
+                    offset += LANES
+    lower = lax.broadcasted_iota(jnp.int32, (1, LANES), 1) < LANES // 2
+    for pack_ref, out_ref, base in ((own_ref, own_out_ref, 0), (partner_ref, partner_out_ref, 4)):
+        sums = []
+        for local in range(4):
+            rows = pl.ds(min(local, 2) * LANES, LANES)
+            zonal = jnp.concatenate(
+                [
+                    jnp.concatenate(
+                        [
+                            rows_ref[field, tile, pl.ds(2 * (base + local) + part, levels, stride=stride), :]
+                            for part in range(2)
+                            for field in range(fields)
+                        ],
+                        axis=0,
+                    ).astype(jnp.bfloat16)
+                    for tile in range(tiles)
+                ],
+                axis=1,
+            )
+            table = pack_ref[rows, : tiles * LANES]
+            sums.append(
+                lax.dot_general(zonal, table, (((1,), (1,)), ((), ())), preferred_element_type=jnp.float32)
+            )
+        sums[2] = jnp.where(lower, sums[2], sums[3])
+        size = sums[0].shape[0]
+        for block in range(3):
+            out_ref[pl.ds(block * size, size), :] = sums[block].astype(out_ref.dtype)
+
+
+def far_analyze(place, own, partner, zonal, levels, fields, chunks):
+    tiles = own.shape[1] // LANES - 1
+    shape = (3 * 2 * fields * levels, LANES)
+    whole = pl.BlockSpec(own.shape, lambda: (0, 0))
+    out_spec = pl.BlockSpec(shape, lambda: (0, 0))
+    return pl.pallas_call(
+        functools.partial(far_analysis_kernel, levels, fields, chunks),
+        in_specs=[pl.BlockSpec(memory_space=pltpu.SMEM), whole, whole]
+        + [pl.BlockSpec(x.shape, lambda: (0, 0)) for x in zonal],
+        out_specs=[out_spec, out_spec],
+        out_shape=[jax.ShapeDtypeStruct(shape, jnp.float32), jax.ShapeDtypeStruct(shape, jnp.bfloat16)],
+        scratch_shapes=[pltpu.VMEM((fields, tiles, 16 * levels, LANES), jnp.float32)],
+        compiler_params=pltpu.CompilerParams(vmem_limit_bytes=VMEM_BYTES),
+        cost_estimate=pl.CostEstimate(
+            flops=16 * 2 * fields * levels * LANES * tiles * LANES, bytes_accessed=4 * own.size, transcendentals=0
+        ),
+        name="far_analysis",
+    )(place, own, partner, *zonal)
 
 
 def fold_kernel(slots, levels, fields, arrived_ref, out_ref, rows_ref):
@@ -177,7 +301,7 @@
     )(arrived)
 
 
-def analysis_kernel(least, folded_ref, even_ref, odd_ref, *refs):
+def analysis_kernel(least, folded_ref, far_ref, even_ref, odd_ref, *refs):
     table_refs, out_ref = refs[:-1], refs[-1]
     row_total, degrees = out_ref.shape[1:]
     step = pl.program_id(0)
@@ -197,17 +321,32 @@
     for group in range(len(least)):
         pl.when(step == group)(functools.partial(run, group))
 
-
-def analyze(folded, even, odd, legendre, row_total, least, chunk):
+    @pl.when(step == len(least))
+    def _():
+        width = far_ref.shape[2]
+        out_ref[:, :, : degrees - width] = jnp.zeros((out_ref.shape[0], row_total, degrees - width), out_ref.dtype)
+        out_ref[:, :, degrees - width :] = far_ref[...]
+
+
+def analyze(folded, far, even, odd, legendre, row_total, least, chunk):
     slots, degrees, _ = legendre.shape
-    block = slots // len(least)
+    block = 4
+    near = len(least) - 1
     at, tiles = chunk
     mask_spec = pl.BlockSpec((block, 1, degrees), lambda i: (i, 0, 0))
     return pl.pallas_call(
         functools.partial(analysis_kernel, least),
-        grid=(len(least),),
-        in_specs=[pl.BlockSpec((block,) + folded.shape[1:], lambda i: (i, 0, 0)), mask_spec, mask_spec]
-        + [pl.BlockSpec((block, degrees, LANES), lambda i, t=at + t: (i, 0, t)) for t in range(tiles)],
+        grid=(len(least) + 1,),
+        in_specs=[
+            pl.BlockSpec((block,) + folded.shape[1:], lambda i: (jnp.minimum(i, near), 0, 0)),
+            pl.BlockSpec(far.shape, lambda i: (0, 0, 0)),
+            mask_spec,
+            mask_spec,
+        ]
+        + [
+            pl.BlockSpec((block, degrees, LANES), lambda i, t=at + t: (jnp.minimum(i, near), 0, t))
+            for t in range(tiles)
+        ],
         out_specs=pl.BlockSpec((block, row_total, degrees), lambda i: (i, 0, 0)),
         out_shape=jax.ShapeDtypeStruct((slots, row_total, degrees), jnp.float32),
         compiler_params=pltpu.CompilerParams(vmem_limit_bytes=VMEM_BYTES),
@@ -217,7 +356,7 @@
             transcendentals=0,
         ),
         name="analysis",
-    )(folded, even, odd, *[legendre] * tiles)
+    )(folded, far, even, odd, *[legendre] * tiles)
 
 
 def closing_kernel(
@@ -227,8 +366,9 @@
     held = refs[4:]
     at, tiles = chunk
     groups = len(least)
-    slots, row_total, degrees = base_ref.shape
-    block = slots // groups
+    _, row_total, degrees = base_ref.shape
+    block = 4
+    slots = block * groups
     stride = 2 * slots
     half = levels * stride
     arriving = [
@@ -292,7 +432,7 @@
 
 def close(arrived, base, even, odd, legendre, fields, levels, least, chunk):
     slots, row_total, degrees = base.shape
-    block = slots // len(least)
+    block = 4
     rows, width = arrived.shape
     tiles = chunk[1]
     half = pltpu.VMEM((fields, tiles, rows // 2, LANES), jnp.float32)
@@ -324,6 +464,26 @@
     )(arrived, legendre, base, even, odd)
 
 
+def across_halves(value):
+    planes = lax.axis_size("grp")
+    return lax.ppermute(value, "grp", [(p, (p + planes // 2) % planes) for p in range(planes)])
+
+
+def within_half(parts):
+    bands, planes = lax.axis_size("band"), lax.axis_size("grp")
+    half = planes // 2
+    moved = [parts[0]]
+    for x in range(1, len(parts)):
+        pairs = []
+        for band in range(bands):
+            for plane in range(planes):
+                level = (plane % half * bands + band) ^ x
+                target = level % bands * planes + plane // half * half + level // bands
+                pairs.append((band * planes + plane, target))
+        moved.append(lax.ppermute(parts[x], AXES, pairs))
+    return moved
+
+
 def after(value, *others):
     return lax.optimization_barrier((value, others))[0]
 
@@ -391,7 +551,10 @@
     tiles = half_lat // LANES
     first = lax.axis_index(AXES).astype(jnp.int32) * slots
     spec_rows = spectral.reshape(slots, row_total, degrees)
-    least = tuple(8 * g * levels for g in range(slots // 4))
+    devices = 2 * levels
+    least = tuple(4 * g * devices for g in range(slots // 4 - 1))
+    near = slots - 4
+    far_least, last_least = near * devices, (near + 2) * devices
     cut = tiles - tiles // 2
     chunks = [(0, cut), (cut, tiles - cut)]
 
@@ -399,21 +562,70 @@
         return synthesize(first.reshape(1), owner_table, spec, legendre, chunk, fields, levels, least)
 
     large = send(spec_rows, chunks[0])
+    arrived = [exchange(large)]
+
+    late_spec, late_table = after((spec_rows, legendre), large)
+    table = jnp.concatenate(
+        [
+            late_table[near : near + 2, far_least:].reshape(-1, half_lat),
+            late_table[near + 2 :, last_least:].reshape(-1, half_lat),
+        ]
+    )
+    spec = late_spec[near:, :, far_least:]
+    width = last_least - far_least
+    packed = jnp.concatenate([spec[2, :, width:], spec[3, :, width:]], axis=1)
+    spec = jnp.concatenate([spec[:2].reshape(2 * row_total, -1), packed])
+    own_pack = jnp.concatenate([table, spec], axis=1)
+    partner_pack = across_halves(own_pack)
+
+    bands, planes = lax.axis_size("band"), lax.axis_size("grp")
+    by_device = jnp.swapaxes(owner_table.reshape(bands, planes, slots), 0, 1).reshape(2, levels, slots)
+    plane = lax.axis_index("grp").astype(jnp.int32)
+    hemi = plane // (planes // 2)
+    level = plane % (planes // 2) * bands + lax.axis_index("band").astype(jnp.int32)
+    place = jnp.stack([hemi, level])
+    far = by_device[:, :, near:]
+    both_halves = jnp.concatenate([far[0], far[1]], axis=1)
+    swapped = jnp.concatenate([far[1], far[0]], axis=1)
+    far_waves = jnp.where(hemi == 0, both_halves, swapped)
+    far_waves = jnp.take(far_waves, jnp.arange(levels, dtype=jnp.int32) ^ level, axis=0)
+    waves = jnp.concatenate([by_device[:, :, :near].reshape(-1), far_waves.reshape(-1)])
+
     small = send(after(spec_rows, large), chunks[1])
-    arrived = [exchange(large)]
-    arrived.append(exchange(after(small, *arrived)))
-    bands, planes = lax.axis_size("band"), lax.axis_size("grp")
-    arriving = jnp.swapaxes(owner_table.reshape(bands, planes, slots), 0, 1).reshape(-1)
-    by_wave, by_lon = trig_tables(after(arriving, large), lon_count, small)
-    zonal = [longitudes(rows, by_lon, by_wave, fields) for rows in arrived]
-    returned = [exchange(zonal[0])]
-    returned.append(exchange(after(zonal[1], *returned)))
+    by_wave, by_lon = trig_tables(after(waves, large), lon_count, small)
+    far_rows = far_synthesize(
+        place, far_waves[0] - far_least, own_pack, partner_pack, levels, fields, 1.0 / math.sqrt(degrees)
+    )
+    arrived.append(exchange(after(small, by_wave, *far_rows, *arrived)))
+    far_rows = jnp.concatenate(within_half(far_rows))
+    zonal = [
+        longitudes(rows, far_rows, by_lon, by_wave, fields, chunk) for rows, chunk in zip(arrived, chunks)
+    ]
+    returned = [exchange(zonal[0][0])]
+    far_zonal = jnp.concatenate([zonal[0][1], zonal[1][1]], axis=1)
+    far_zonal = within_half([far_zonal[16 * x : 16 * x + 16] for x in range(levels)])
+    own_sums, partner_sums = far_analyze(place, own_pack, partner_pack, far_zonal, levels, fields, chunks)
+    returned.append(exchange(after(zonal[1][0], partner_sums, *returned)))
+    other_sums = across_halves(partner_sums).astype(jnp.float32)
+    north = jnp.where(hemi == 0, own_sums, other_sums)
+    south = jnp.where(hemi == 0, other_sums, own_sums)
     wavenumber = lax.dynamic_slice_in_dim(after(owner_table, by_wave), first, slots)
     distance = jnp.arange(degrees, dtype=jnp.int32)[None, :] - wavenumber[:, None]
     scale = 1.0 / math.sqrt(2 * half_lat)
     even = jnp.where((distance >= 0) & (distance % 2 == 0), scale, 0.0).astype(jnp.float32)[:, None, :]
     odd = jnp.where((distance >= 0) & (distance % 2 != 0), scale, 0.0).astype(jnp.float32)[:, None, :]
-    base = analyze(fold(returned[0], slots, levels, fields), even, odd, legendre, row_total, least, chunks[0])
+
+    def unpack(sums):
+        sums = sums.reshape(3, row_total, -1)
+        empty = jnp.zeros((row_total, width), jnp.float32)
+        third = jnp.concatenate([empty, sums[2, :, :width]], axis=1)
+        fourth = jnp.concatenate([empty, sums[2, :, width:]], axis=1)
+        return jnp.concatenate([sums[:2], third[None], fourth[None]])
+
+    far_even, far_odd = even[near:, :, far_least:], odd[near:, :, far_least:]
+    far_out = unpack(north + south) * far_even + unpack(north - south) * far_odd
+    folded = fold(returned[0], near, levels, fields)
+    base = analyze(folded, far_out, even, odd, legendre, row_total, least, chunks[0])
     last = after(returned[1], base)
     out = close(last, base, even, odd, legendre, fields, levels, least, chunks[1])
     return out.reshape(slots, 2, fields, levels, degrees)
@@ -493,7 +705,9 @@
 def on_device(spectral, legendre, owner_table):
     slots, _, _, levels, _ = spectral.shape
     whole_hemispheres = lax.axis_size("band") * lax.axis_size("grp") == 2 * levels
-    if whole_hemispheres and legendre.shape[2] % LANES == 0 and legendre.shape[2] > LANES and slots % 4 == 0 and levels % 16 == 0:
+    halves = lax.axis_size("grp") % 2 == 0 and levels & (levels - 1) == 0
+    few_left = legendre.shape[1] - (slots - 4) * 2 * levels == LANES
+    if whole_hemispheres and halves and few_left and legendre.shape[2] % LANES == 0 and legendre.shape[2] > LANES and slots % 4 == 0 and levels % 16 == 0:
         return by_hemisphere_and_level(spectral, legendre, owner_table)
     return by_level_and_latitude(spectral, legendre, owner_table)
 

time: 332 us -> 390 us (1.17); the launches traced: 331 us -> 384 us
  starting transfers between devices: 19.9 us -> 79 us
  waiting for transfers between devices: 200 us -> 162 us
  Pallas kernels: 102 us -> 120 us
  local copies, waits for them, and re-layouts: 5.4 us -> 16.1 us
    all_to_all x4, waiting for transfers between devices: 200 us -> 0.01 us  [exchange(): lax.all_to_all(rows, AXES[::-1], split_axis=0, concat_axis=0, tiled=True)]
    ppermute x0 -> x32, waiting for transfers between devices: none -> 162 us  [the longest x2 107 us: across_halves(): lax.ppermute(value, 'grp', [(p, (p + planes // 2) % planes) for p in rang...]
    ppermute x0 -> x32, starting transfers between devices: none -> 52.8 us  [the longest x30 47.1 us: within_half(): moved.append(lax.ppermute(parts[x], AXES, pairs))]
    pallas_call x2 -> x4, Pallas kernels: 52.6 us -> 60.2 us  [the longest x2 53 us: longitudes(): pl.pallas_call(functools.partial(longitude_kernel, fields, chunk, 1.0 / m...]
    all_to_all x4, starting transfers between devices: 19.9 us -> 26.3 us  [exchange(): lax.all_to_all(rows, AXES[::-1], split_axis=0, concat_axis=0, tiled=True)]
    pallas_call x2, Pallas kernels: 14.3 us -> 20 us  [synthesize(): pl.pallas_call(functools.partial(synthesis_kernel, slots, levels, fields,...]
  transfers between devices with their start and end apart: 4 -> 36, of which waited for: 4 -> 14; matrix products, arithmetic and copies ran while one was open for 3% -> 5% of each run, Pallas kernels for 26% -> 26%
where the time goes in v3:
time: 390 us; the launch traced here: 384 us
  waiting for transfers between devices  162 us (42%)
  Pallas kernels  120 us (31%)
  starting transfers between devices  79 us (20%)
  local copies, waits for them, and re-layouts  16.1 us (4%)
  other arithmetic  6.16 us (2%)
    ppermute x2, waiting for transfers between devices, across_halves(): lax.ppermute(value, 'grp', [(p, (p + planes // 2) % planes) for p in rang...  107 us
    ppermute x30, waiting for transfers between devices, within_half(): moved.append(lax.ppermute(parts[x], AXES, pairs))  54.9 us
    pallas_call x2, Pallas kernels, longitudes(): pl.pallas_call(functools.partial(longitude_kernel, fields, chunk, 1.0 / m...  53 us
    ppermute x30, starting transfers between devices, within_half(): moved.append(lax.ppermute(parts[x], AXES, pairs))  47.1 us
    all_to_all x4, starting transfers between devices, exchange(): lax.all_to_all(rows, AXES[::-1], split_axis=0, concat_axis=0, tiled=True)  26.3 us
    pallas_call x2, Pallas kernels, synthesize(): pl.pallas_call(functools.partial(synthesis_kernel, slots, levels, fields,...  20 us
    pallas_call x1, Pallas kernels, trig_tables(): pl.pallas_call(trig_kernel, grid=(depth // rows,), in_specs=[small, small...  11.9 us
    pallas_call x1, Pallas kernels, fold(): pl.pallas_call(functools.partial(fold_kernel, slots, levels, fields), in_...  9.96 us
  transfers between devices with their start and end apart: 36, of which 14 were waited for; matrix products, arithmetic and copies ran while one was open for 5% of the time, Pallas kernels for 26%

profile of v3, /device:TPU:0, one launch (start us, length us, event | category | flops | bytes accessed | tf_op | source)
XLA Modules:
  0.0 384.2 jit_solution(17390281809301062041)
XLA Ops:
  0.0 12.1 %synthesis.2 = bf16[1024,1536]{1,0:T(8,128)(2,1)} custom-call(s32[1]{0:T(128)} %bitcast.first_ref, s32[640]{0:T(1024)} %owner_ref.3, bf16[20,128,640]{2,1,0:T(8,128)(2,1)} %bitcast.57, bf16[20,640,640]{2,1,0:T(8,128)(2,1)} %table_ref.5), custom_call_target="tpu_custom_call" | custom-call | flops 2013265920 | bytes 13631488 | tf_op jit(solution)/shard_map/synthesis/pallas_call | solution.py:76
  12.1 7.6 %all-to-all-start = ((bf16[32,32,1536]{2,1,0:T(8,128)(2,1)}), bf16[32,32,1536]{2,1,0:T(8,128)(2,1)}, u32[]{:S(2)}, u32[]{:S(2)}) async-start(bf16[32,32,1536]{2,1,0:T(8,128)(2,1)} %bitcast.61), calls=%async_computation | async-start | bytes 6291456 | tf_op jit(solution)/shard_map/all_to_all | solution.py:543
  31.8 7.8 %synthesis.3 = bf16[1024,1024]{1,0:T(8,128)(2,1)} custom-call(s32[1]{0:T(128)} %bitcast.first_ref, s32[640]{0:T(1024)} %owner_ref.3, bf16[20,128,640]{2,1,0:T(8,128)(2,1)} %bitcast.60, bf16[20,640,640]{2,1,0:T(8,128)(2,1)} %table_ref.5), custom_call_target="tpu_custom_call" | custom-call | flops 1342177280 | bytes 9961472 | tf_op jit(solution)/shard_map/synthesis/pallas_call | solution.py:76
  44.9 11.9 %trig.1 = (bf16[1280,2560]{1,0:T(8,128)(2,1)}, bf16[2560,1280]{1,0:T(8,128)(2,1)}) custom-call(f32[1280,20]{1,0:T(8,128)} %copy.31.cos_base_ref, f32[1280,20]{1,0:T(8,128)} %copy.32.sin_base_ref, f32[1280,128]{1,0:T(8,128)} %copy.33.cos_turn_ref, f32[1280,128]{1,0:T(8,128)} %copy.34.sin_turn_ref, f32[20,1280]{1,0:T(8,128)} %bitcast.69, f32[20,1280]{1,0:T(8,128)} %bitcast.68, ...), custom_call_target="tpu_custom_call" | custom-call | flops 26214400 | bytes 13107200 | tf_op jit(solution)/shard_map/trig/pallas_call | solution.py:522
  58.0 58.5 %collective-permute-done.partner_ref = bf16[384,768]{1,0:T(8,128)(2,1)} collective-permute-done((bf16[384,768]{1,0:T(8,128)(2,1)S(1)}, bf16[384,768]{1,0:T(8,128)(2,1)}, u32[]{:S(2)}, u32[]{:S(2)}) %collective-permute-start) | collective-permute-done | bytes 589856 | tf_op jit(solution)/shard_map/ppermute | solution.py:469
  116.4 3.7 far_synthesis.1
  137.5 5.0 %all-to-all-start.1 = ((bf16[32,32,1024]{2,1,0:T(8,128)(2,1)}), bf16[32,32,1024]{2,1,0:T(8,128)(2,1)}, u32[]{:S(2)}, u32[]{:S(2)}) async-start(bf16[32,32,1024]{2,1,0:T(8,128)(2,1)} %bitcast.62), calls=%async_computation.1 | async-start | bytes 4194304 | tf_op jit(solution)/shard_map/all_to_all | solution.py:543
  142.5 3.6 collective-permute-start.14
  146.3 33.2 %collective-permute-done.14 = bf16[16,2560]{1,0:T(8,128)(2,1)S(1)} collective-permute-done((bf16[16,2560]{1,0:T(8,128)(2,1)S(1)}, bf16[16,2560]{1,0:T(8,128)(2,1)S(1)}, u32[]{:S(2)}, u32[]{:S(2)}) %collective-permute-start.14) | collective-permute-done | bytes 81952 | tf_op jit(solution)/shard_map/ppermute | solution.py:483
  182.3 31.1 %longitudes.3 = (bf16[1024,1536]{1,0:T(8,128)(2,1)}, bf16[256,1536]{1,0:T(8,128)(2,1)}) custom-call(bf16[1024,1536]{1,0:T(8,128)(2,1)} %bitcast.20.rows_ref, bf16[256,2560]{1,0:T(8,128)(2,1)} %copy-done.24, bf16[2560,1280]{1,0:T(8,128)(2,1)} %get-tuple-element.67.by_lon_ref, bf16[1280,2560]{1,0:T(8,128)(2,1)} %get-tuple-element.47.by_wave_ref), custom_call_target="tpu_custom_call" | custom-call | flops 20132659200 | bytes 20971520 | tf_op jit(solution)/shard_map/longitudes/pallas_call | solution.py:132
  213.3 8.3 %all-to-all-start.2 = ((bf16[32,32,1536]{2,1,0:T(8,128)(2,1)}), bf16[32,32,1536]{2,1,0:T(8,128)(2,1)}, u32[]{:S(2)}, u32[]{:S(2)}) async-start(bf16[32,32,1536]{2,1,0:T(8,128)(2,1)} %bitcast.65), calls=%async_computation.2 | async-start | bytes 6291456 | tf_op jit(solution)/shard_map/all_to_all | solution.py:543
  221.7 22.0 %longitudes.2 = (bf16[1024,1024]{1,0:T(8,128)(2,1)}, bf16[256,1024]{1,0:T(8,128)(2,1)}) custom-call(bf16[1024,1024]{1,0:T(8,128)(2,1)} %bitcast.22.rows_ref, bf16[256,2560]{1,0:T(8,128)(2,1)} %copy-done.24, bf16[2560,1280]{1,0:T(8,128)(2,1)} %get-tuple-element.67.by_lon_ref, bf16[1280,2560]{1,0:T(8,128)(2,1)} %get-tuple-element.47.by_wave_ref), custom_call_target="tpu_custom_call" | custom-call | flops 13421772800 | bytes 18350080 | tf_op jit(solution)/shard_map/longitudes/pallas_call | solution.py:132
  252.0 5.3 %collective-permute-start.22 = (bf16[16,2560]{1,0:T(8,128)(2,1)S(1)}, bf16[16,2560]{1,0:T(8,128)(2,1)S(1)}, u32[]{:S(2)}, u32[]{:S(2)}) collective-permute-start(bf16[16,2560]{1,0:T(8,128)(2,1)S(1)} %get-tuple-element.87), channel_id=1, source_target_pairs={{0,28},{1,29},{2,30},{3,31},{4,24},{5,25},{6,26},{7,27},{8,20},{9,... | collective-permute-start | bytes 245768 | tf_op jit(solution)/shard_map/ppermute | solution.py:483
  259.6 4.6 %collective-permute-start.25 = (bf16[16,2560]{1,0:T(8,128)(2,1)S(1)}, bf16[16,2560]{1,0:T(8,128)(2,1)S(1)}, u32[]{:S(2)}, u32[]{:S(2)}) collective-permute-start(bf16[16,2560]{1,0:T(8,128)(2,1)S(1)} %get-tuple-element.84), channel_id=1, source_target_pairs={{0,9},{1,8},{2,11},{3,10},{4,13},{5,12},{6,15},{7,14},{8,1},{9,0},... | collective-permute-start | bytes 245768 | tf_op jit(solution)/shard_map/ppermute | solution.py:483
  265.7 4.7 %collective-permute-start.27 = (bf16[16,2560]{1,0:T(8,128)(2,1)S(1)}, bf16[16,2560]{1,0:T(8,128)(2,1)S(1)}, u32[]{:S(2)}, u32[]{:S(2)}) collective-permute-start(bf16[16,2560]{1,0:T(8,128)(2,1)S(1)} %get-tuple-element.82), channel_id=1, source_target_pairs={{0,17},{1,16},{2,19},{3,18},{4,21},{5,20},{6,23},{7,22},{8,25},{9,... | collective-permute-start | bytes 245768 | tf_op jit(solution)/shard_map/ppermute | solution.py:483
  270.4 5.1 %collective-permute-done.23.refs_8_ = bf16[16,2560]{1,0:T(8,128)(2,1)S(1)} collective-permute-done((bf16[16,2560]{1,0:T(8,128)(2,1)S(1)}, bf16[16,2560]{1,0:T(8,128)(2,1)S(1)}, u32[]{:S(2)}, u32[]{:S(2)}) %collective-permute-start.23) | collective-permute-done | bytes 81952 | tf_op jit(solution)/shard_map/ppermute | solution.py:483
  284.3 4.7 %collective-permute-done.29.refs_14_ = bf16[16,2560]{1,0:T(8,128)(2,1)S(1)} collective-permute-done((bf16[16,2560]{1,0:T(8,128)(2,1)S(1)}, bf16[16,2560]{1,0:T(8,128)(2,1)S(1)}, u32[]{:S(2)}, u32[]{:S(2)}) %collective-permute-start.29) | collective-permute-done | bytes 81952 | tf_op jit(solution)/shard_map/ppermute | solution.py:483
  289.0 3.8 collective-permute-done.30.refs_15_
  293.4 3.5 far_analysis.1
  297.0 5.3 %all-to-all-start.3 = ((bf16[32,32,1024]{2,1,0:T(8,128)(2,1)}), bf16[32,32,1024]{2,1,0:T(8,128)(2,1)}, u32[]{:S(2)}, u32[]{:S(2)}) async-start(bf16[32,32,1024]{2,1,0:T(8,128)(2,1)} %bitcast.66), calls=%async_computation.3 | async-start | bytes 4194304 | tf_op jit(solution)/shard_map/all_to_all | solution.py:543
  306.3 49.0 %collective-permute-done.31 = bf16[384,128]{1,0:T(8,128)(2,1)S(1)} collective-permute-done((bf16[384,128]{1,0:T(8,128)(2,1)S(1)}, bf16[384,128]{1,0:T(8,128)(2,1)S(1)}, u32[]{:S(2)}, u32[]{:S(2)}) %collective-permute-start.31) | collective-permute-done | bytes 98336 | tf_op jit(solution)/shard_map/ppermute | solution.py:469
  356.5 10.0 %fold.1.folded_ref = bf16[16,256,384]{2,1,0:T(8,128)(2,1)} custom-call(bf16[1024,1536]{1,0:T(8,128)(2,1)} %bitcast.24.arrived_ref), custom_call_target="tpu_custom_call" | custom-call | flops 3145728 | bytes 6291456 | tf_op jit(solution)/shard_map/fold/pallas_call | solution.py:292
  366.4 9.0 %analysis.1.base_ref = f32[20,128,640]{2,1,0:T(8,128)} custom-call(bf16[16,256,384]{2,1,0:T(8,128)(2,1)} %fold.1.folded_ref, f32[4,128,128]{2,1,0:T(8,128)} %fusion.2.far_ref, f32[20,1,640]{2,1,0:T(1,128)} %copy-done.5, f32[20,1,640]{2,1,0:T(1,128)} %copy-done.6, bf16[20,640,640]{2,1,0:T(8,128)(2,1)} %table_ref.5, bf16[20,640,640]{2,1,0:T(8,128)(2,1)} %table_ref.5, ...), custom_call_target="tpu_custom_call" | custom-call | flops 2516582400 | bytes 20316160 | tf_op jit(solution)/shard_map/analysis/pallas_call | solution.py:337
  375.4 8.5 %closing.1 = f32[20,128,640]{2,1,0:T(8,128)} custom-call(bf16[1024,1024]{1,0:T(8,128)(2,1)} %bitcast.26.arrived_ref, bf16[20,640,640]{2,1,0:T(8,128)(2,1)} %table_ref.5, f32[20,128,640]{2,1,0:T(8,128)} %analysis.1.base_ref, f32[20,1,640]{2,1,0:T(1,128)} %copy-done.5, f32[20,1,640]{2,1,0:T(1,128)} %copy-done.6), custom_call_target="tpu_custom_call", output_to_operand_aliasing={{}: (2, {})} | custom-call | flops 1677721600 | bytes 15204352 | tf_op jit(solution)/shard_map/closing/pallas_call | solution.py:444
  (180 shorter events, 65.1 us)
Async XLA Ops:
  12.1 125.3 %all-to-all-start = ((bf16[32,32,1536]{2,1,0:T(8,128)(2,1)}), bf16[32,32,1536]{2,1,0:T(8,128)(2,1)}, u32[]{:S(2)}, u32[]{:S(2)}) async-start(bf16[32,32,1536]{2,1,0:T(8,128)(2,1)} %bitcast.61), calls=%async_computation | async-start | bytes 6291456 | tf_op jit(solution)/shard_map/all_to_all | solution.py:543
  23.5 92.9 %collective-permute-start = (bf16[384,768]{1,0:T(8,128)(2,1)S(1)}, bf16[384,768]{1,0:T(8,128)(2,1)}, u32[]{:S(2)}, u32[]{:S(2)}) collective-permute-start(bf16[384,768]{1,0:T(8,128)(2,1)S(1)} %maximum_maximum_fusion.own_ref), channel_id=1, source_target_pairs={{0,2},{1,3},{2,0},{3,1},{4,6},{5,7},{6,4},{7,5},{8,10},{9,11},{10,... | collective-permute-start | bytes 1769480 | tf_op jit(solution)/shard_map/ppermute | solution.py:469
  128.3 14.2 %collective-permute-start.9 = (bf16[16,2560]{1,0:T(8,128)(2,1)}, bf16[16,2560]{1,0:T(8,128)(2,1)S(1)}, u32[]{:S(2)}, u32[]{:S(2)}) collective-permute-start(bf16[16,2560]{1,0:T(8,128)(2,1)} %get-tuple-element.59), channel_id=1, source_target_pairs={{0,5},{1,4},{2,7},{3,6},{4,1},{5,0},{6,3},{7,2},{8,13},{9,12},{10,... | collective-permute-start | bytes 245768 | tf_op jit(solution)/shard_map/ppermute | solution.py:483
  131.9 14.2 %collective-permute-start.10 = (bf16[16,2560]{1,0:T(8,128)(2,1)}, bf16[16,2560]{1,0:T(8,128)(2,1)S(1)}, u32[]{:S(2)}, u32[]{:S(2)}) collective-permute-start(bf16[16,2560]{1,0:T(8,128)(2,1)} %get-tuple-element.60), channel_id=1, source_target_pairs={{0,9},{1,8},{2,11},{3,10},{4,13},{5,12},{6,15},{7,14},{8,1},{9,0},... | collective-permute-start | bytes 245768 | tf_op jit(solution)/shard_map/ppermute | solution.py:483
  132.4 13.8 %collective-permute-start.11 = (bf16[16,2560]{1,0:T(8,128)(2,1)}, bf16[16,2560]{1,0:T(8,128)(2,1)S(1)}, u32[]{:S(2)}, u32[]{:S(2)}) collective-permute-start(bf16[16,2560]{1,0:T(8,128)(2,1)} %get-tuple-element.61), channel_id=1, source_target_pairs={{0,13},{1,12},{2,15},{3,14},{4,9},{5,8},{6,11},{7,10},{8,5},{9,4},... | collective-permute-start | bytes 245768 | tf_op jit(solution)/shard_map/ppermute | solution.py:483
  135.5 10.8 %collective-permute-start.12 = (bf16[16,2560]{1,0:T(8,128)(2,1)}, bf16[16,2560]{1,0:T(8,128)(2,1)S(1)}, u32[]{:S(2)}, u32[]{:S(2)}) collective-permute-start(bf16[16,2560]{1,0:T(8,128)(2,1)} %get-tuple-element.62), channel_id=1, source_target_pairs={{0,17},{1,16},{2,19},{3,18},{4,21},{5,20},{6,23},{7,22},{8,25},{9,... | collective-permute-start | bytes 245768 | tf_op jit(solution)/shard_map/ppermute | solution.py:483
  137.5 75.9 %all-to-all-start.1 = ((bf16[32,32,1024]{2,1,0:T(8,128)(2,1)}), bf16[32,32,1024]{2,1,0:T(8,128)(2,1)}, u32[]{:S(2)}, u32[]{:S(2)}) async-start(bf16[32,32,1024]{2,1,0:T(8,128)(2,1)} %bitcast.62), calls=%async_computation.1 | async-start | bytes 4194304 | tf_op jit(solution)/shard_map/all_to_all | solution.py:543
  142.5 37.0 %collective-permute-start.14 = (bf16[16,2560]{1,0:T(8,128)(2,1)S(1)}, bf16[16,2560]{1,0:T(8,128)(2,1)S(1)}, u32[]{:S(2)}, u32[]{:S(2)}) collective-permute-start(bf16[16,2560]{1,0:T(8,128)(2,1)S(1)} %copy-done.28), channel_id=1, source_target_pairs={{0,25},{1,24},{2,27},{3,26},{4,29},{5,28},{6,31},{7,30},{8,17},{9,... | collective-permute-start | bytes 245768 | tf_op jit(solution)/shard_map/ppermute | solution.py:483
  146.1 35.1 %collective-permute-start.15 = (bf16[16,2560]{1,0:T(8,128)(2,1)S(1)}, bf16[16,2560]{1,0:T(8,128)(2,1)S(1)}, u32[]{:S(2)}, u32[]{:S(2)}) collective-permute-start(bf16[16,2560]{1,0:T(8,128)(2,1)S(1)} %copy-done.27), channel_id=1, source_target_pairs={{0,29},{1,28},{2,31},{3,30},{4,25},{5,24},{6,27},{7,26},{8,21},{9,... | collective-permute-start | bytes 245768 | tf_op jit(solution)/shard_map/ppermute | solution.py:483
  213.3 83.6 %all-to-all-start.2 = ((bf16[32,32,1536]{2,1,0:T(8,128)(2,1)}), bf16[32,32,1536]{2,1,0:T(8,128)(2,1)}, u32[]{:S(2)}, u32[]{:S(2)}) async-start(bf16[32,32,1536]{2,1,0:T(8,128)(2,1)} %bitcast.65), calls=%async_computation.2 | async-start | bytes 6291456 | tf_op jit(solution)/shard_map/all_to_all | solution.py:543
  247.6 10.2 %collective-permute-start.18 = (bf16[16,2560]{1,0:T(8,128)(2,1)S(1)}, bf16[16,2560]{1,0:T(8,128)(2,1)S(1)}, u32[]{:S(2)}, u32[]{:S(2)}) collective-permute-start(bf16[16,2560]{1,0:T(8,128)(2,1)S(1)} %get-tuple-element.91), channel_id=1, source_target_pairs={{0,12},{1,13},{2,14},{3,15},{4,8},{5,9},{6,10},{7,11},{8,4},{9,5},... | collective-permute-start | bytes 245768 | tf_op jit(solution)/shard_map/ppermute | solution.py:483
  247.6 10.2 %collective-permute-start.19 = (bf16[16,2560]{1,0:T(8,128)(2,1)S(1)}, bf16[16,2560]{1,0:T(8,128)(2,1)S(1)}, u32[]{:S(2)}, u32[]{:S(2)}) collective-permute-start(bf16[16,2560]{1,0:T(8,128)(2,1)S(1)} %get-tuple-element.90), channel_id=1, source_target_pairs={{0,16},{1,17},{2,18},{3,19},{4,20},{5,21},{6,22},{7,23},{8,24},{9,... | collective-permute-start | bytes 245768 | tf_op jit(solution)/shard_map/ppermute | solution.py:483
  249.3 10.3 %collective-permute-start.20 = (bf16[16,2560]{1,0:T(8,128)(2,1)S(1)}, bf16[16,2560]{1,0:T(8,128)(2,1)S(1)}, u32[]{:S(2)}, u32[]{:S(2)}) collective-permute-start(bf16[16,2560]{1,0:T(8,128)(2,1)S(1)} %get-tuple-element.89), channel_id=1, source_target_pairs={{0,20},{1,21},{2,22},{3,23},{4,16},{5,17},{6,18},{7,19},{8,28},{9,... | collective-permute-start | bytes 245768 | tf_op jit(solution)/shard_map/ppermute | solution.py:483
  249.4 14.7 %collective-permute-start.21 = (bf16[16,2560]{1,0:T(8,128)(2,1)S(1)}, bf16[16,2560]{1,0:T(8,128)(2,1)S(1)}, u32[]{:S(2)}, u32[]{:S(2)}) collective-permute-start(bf16[16,2560]{1,0:T(8,128)(2,1)S(1)} %get-tuple-element.88), channel_id=1, source_target_pairs={{0,24},{1,25},{2,26},{3,27},{4,28},{5,29},{6,30},{7,31},{8,16},{9,... | collective-permute-start | bytes 245768 | tf_op jit(solution)/shard_map/ppermute | solution.py:483
  252.0 13.7 %collective-permute-start.22 = (bf16[16,2560]{1,0:T(8,128)(2,1)S(1)}, bf16[16,2560]{1,0:T(8,128)(2,1)S(1)}, u32[]{:S(2)}, u32[]{:S(2)}) collective-permute-start(bf16[16,2560]{1,0:T(8,128)(2,1)S(1)} %get-tuple-element.87), channel_id=1, source_target_pairs={{0,28},{1,29},{2,30},{3,31},{4,24},{5,25},{6,26},{7,27},{8,20},{9,... | collective-permute-start | bytes 245768 | tf_op jit(solution)/shard_map/ppermute | solution.py:483
  257.8 17.7 %collective-permute-start.23 = (bf16[16,2560]{1,0:T(8,128)(2,1)S(1)}, bf16[16,2560]{1,0:T(8,128)(2,1)S(1)}, u32[]{:S(2)}, u32[]{:S(2)}) collective-permute-start(bf16[16,2560]{1,0:T(8,128)(2,1)S(1)} %get-tuple-element.86), channel_id=1, source_target_pairs={{0,1},{1,0},{2,3},{3,2},{4,5},{5,4},{6,7},{7,6},{8,9},{9,8},{10,11... | collective-permute-start | bytes 245768 | tf_op jit(solution)/shard_map/ppermute | solution.py:483
  257.8 20.0 %collective-permute-start.24 = (bf16[16,2560]{1,0:T(8,128)(2,1)S(1)}, bf16[16,2560]{1,0:T(8,128)(2,1)S(1)}, u32[]{:S(2)}, u32[]{:S(2)}) collective-permute-start(bf16[16,2560]{1,0:T(8,128)(2,1)S(1)} %get-tuple-element.85), channel_id=1, source_target_pairs={{0,5},{1,4},{2,7},{3,6},{4,1},{5,0},{6,3},{7,2},{8,13},{9,12},{10,... | collective-permute-start | bytes 245768 | tf_op jit(solution)/shard_map/ppermute | solution.py:483
  259.6 21.5 %collective-permute-start.25 = (bf16[16,2560]{1,0:T(8,128)(2,1)S(1)}, bf16[16,2560]{1,0:T(8,128)(2,1)S(1)}, u32[]{:S(2)}, u32[]{:S(2)}) collective-permute-start(bf16[16,2560]{1,0:T(8,128)(2,1)S(1)} %get-tuple-element.84), channel_id=1, source_target_pairs={{0,9},{1,8},{2,11},{3,10},{4,13},{5,12},{6,15},{7,14},{8,1},{9,0},... | collective-permute-start | bytes 245768 | tf_op jit(solution)/shard_map/ppermute | solution.py:483
  264.2 18.0 %collective-permute-start.26 = (bf16[16,2560]{1,0:T(8,128)(2,1)S(1)}, bf16[16,2560]{1,0:T(8,128)(2,1)S(1)}, u32[]{:S(2)}, u32[]{:S(2)}) collective-permute-start(bf16[16,2560]{1,0:T(8,128)(2,1)S(1)} %get-tuple-element.83), channel_id=1, source_target_pairs={{0,13},{1,12},{2,15},{3,14},{4,9},{5,8},{6,11},{7,10},{8,5},{9,4},... | collective-permute-start | bytes 245768 | tf_op jit(solution)/shard_map/ppermute | solution.py:483
  265.7 16.9 %collective-permute-start.27 = (bf16[16,2560]{1,0:T(8,128)(2,1)S(1)}, bf16[16,2560]{1,0:T(8,128)(2,1)S(1)}, u32[]{:S(2)}, u32[]{:S(2)}) collective-permute-start(bf16[16,2560]{1,0:T(8,128)(2,1)S(1)} %get-tuple-element.82), channel_id=1, source_target_pairs={{0,17},{1,16},{2,19},{3,18},{4,21},{5,20},{6,23},{7,22},{8,25},{9,... | collective-permute-start | bytes 245768 | tf_op jit(solution)/shard_map/ppermute | solution.py:483
  277.8 11.2 %collective-permute-start.29 = (bf16[16,2560]{1,0:T(8,128)(2,1)S(1)}, bf16[16,2560]{1,0:T(8,128)(2,1)S(1)}, u32[]{:S(2)}, u32[]{:S(2)}) collective-permute-start(bf16[16,2560]{1,0:T(8,128)(2,1)S(1)} %get-tuple-element.80), channel_id=1, source_target_pairs={{0,25},{1,24},{2,27},{3,26},{4,29},{5,28},{6,31},{7,30},{8,17},{9,... | collective-permute-start | bytes 245768 | tf_op jit(solution)/shard_map/ppermute | solution.py:483
  281.1 11.7 %collective-permute-start.30 = (bf16[16,2560]{1,0:T(8,128)(2,1)S(1)}, bf16[16,2560]{1,0:T(8,128)(2,1)S(1)}, u32[]{:S(2)}, u32[]{:S(2)}) collective-permute-start(bf16[16,2560]{1,0:T(8,128)(2,1)S(1)} %get-tuple-element.79), channel_id=1, source_target_pairs={{0,29},{1,28},{2,31},{3,30},{4,25},{5,24},{6,27},{7,26},{8,21},{9,... | collective-permute-start | bytes 245768 | tf_op jit(solution)/shard_map/ppermute | solution.py:483
  297.0 78.5 %all-to-all-start.3 = ((bf16[32,32,1024]{2,1,0:T(8,128)(2,1)}), bf16[32,32,1024]{2,1,0:T(8,128)(2,1)}, u32[]{:S(2)}, u32[]{:S(2)}) async-start(bf16[32,32,1024]{2,1,0:T(8,128)(2,1)} %bitcast.66), calls=%async_computation.3 | async-start | bytes 4194304 | tf_op jit(solution)/shard_map/all_to_all | solution.py:543
  303.0 52.2 %collective-permute-start.31 = (bf16[384,128]{1,0:T(8,128)(2,1)S(1)}, bf16[384,128]{1,0:T(8,128)(2,1)S(1)}, u32[]{:S(2)}, u32[]{:S(2)}) collective-permute-start(bf16[384,128]{1,0:T(8,128)(2,1)S(1)} %copy-done.26), channel_id=1, source_target_pairs={{0,2},{1,3},{2,0},{3,1},{4,6},{5,7},{6,4},{7,5},{8,10},{9,11},{10,... | collective-permute-start | bytes 294920 | tf_op jit(solution)/shard_map/ppermute | solution.py:469
  (42 other events, 663.9 us)

commit v4 on v3

--- a/solution.py
+++ b/solution.py
@@ -11,6 +11,10 @@
 LANES = 128
 AXES = ("band", "grp")
 VMEM_BYTES = 62 * 1024 * 1024
+
+
+def padded(slots):
+    return 2 * slots + 8
 
 
 def synthesis_kernel(
@@ -20,7 +24,7 @@
     groups = len(least)
     block = 4
     row_total, degrees = spec_ref.shape[1:]
-    stride = 2 * slots
+    stride = padded(slots)
     copies = []
     for group, start in enumerate(least):
         mine = pl.ds(group * block, block)
@@ -59,7 +63,8 @@
     for field in range(fields):
         for tile in range(tiles):
             lanes = pl.ds((field * tiles + tile) * LANES, LANES)
-            out_ref[:, lanes] = rows_ref[field, tile].astype(out_ref.dtype)
+            rows = rows_ref[field, tile].reshape(2 * levels, stride, LANES)[:, : 2 * slots]
+            out_ref[:, lanes] = rows.reshape(out_ref.shape[0], LANES).astype(out_ref.dtype)
 
 
 def synthesize(first, owner_table, spec_rows, legendre, chunk, fields, levels, least):
@@ -79,7 +84,7 @@
         out_specs=pl.BlockSpec(shape, lambda: (0, 0)),
         out_shape=jax.ShapeDtypeStruct(shape, jnp.bfloat16),
         scratch_shapes=[
-            pltpu.VMEM((fields, tiles, rows, LANES), jnp.float32),
+            pltpu.VMEM((fields, tiles, 2 * levels * padded(slots), LANES), jnp.float32),
             pltpu.SemaphoreType.DMA((2 * len(least),)),
             *held,
         ],
@@ -149,6 +154,49 @@
         ),
         name="longitudes",
     )(rows, far, by_lon, by_wave)
+
+
+def pack_kernel(near, spec_ref, table_ref, out_ref, tail_ref, sems):
+    degrees, half_lat = table_ref.shape[1:]
+    half = LANES // 2
+    copies = []
+
+    def fetch(source, target):
+        copies.append(pltpu.make_async_copy(source, target, sems.at[len(copies)]))
+        copies[-1].start()
+
+    lanes, sides = pl.ds(0, half_lat), pl.ds(half_lat, LANES)
+    for slot in range(2):
+        rows = pl.ds(slot * LANES, LANES)
+        fetch(table_ref.at[near + slot, pl.ds(degrees - LANES, LANES), :], out_ref.at[rows, lanes])
+        fetch(spec_ref.at[near + slot, :, pl.ds(degrees - LANES, LANES)], out_ref.at[rows, sides])
+    for slot in range(2):
+        rows = pl.ds(2 * LANES + slot * half, half)
+        fetch(table_ref.at[near + 2 + slot, pl.ds(degrees - half, half), :], out_ref.at[rows, lanes])
+        fetch(spec_ref.at[near + 2 + slot, :, pl.ds(degrees - LANES, LANES)], tail_ref.at[slot])
+    for copy in copies:
+        copy.wait()
+    third = pltpu.roll(tail_ref[0].astype(jnp.float32), half, 1)
+    lower = lax.broadcasted_iota(jnp.int32, third.shape, 1) < half
+    both = jnp.where(lower, third, tail_ref[1].astype(jnp.float32))
+    out_ref[pl.ds(2 * LANES, LANES), sides] = both.astype(out_ref.dtype)
+
+
+def pack(spec_rows, legendre, near):
+    shape = (3 * LANES, legendre.shape[2] + LANES)
+    return pl.pallas_call(
+        functools.partial(pack_kernel, near),
+        in_specs=[pl.BlockSpec(memory_space=pl.ANY)] * 2,
+        out_specs=pl.BlockSpec(shape, lambda: (0, 0)),
+        out_shape=jax.ShapeDtypeStruct(shape, jnp.bfloat16),
+        scratch_shapes=[
+            pltpu.VMEM((2, spec_rows.shape[1], LANES), jnp.bfloat16),
+            pltpu.SemaphoreType.DMA((8,)),
+        ],
+        compiler_params=pltpu.CompilerParams(vmem_limit_bytes=VMEM_BYTES),
+        cost_estimate=pl.CostEstimate(flops=0, bytes_accessed=4 * shape[0] * shape[1], transcendentals=0),
+        name="pack",
+    )(spec_rows, legendre)
 
 
 def far_synthesis_kernel(levels, fields, scale, place_ref, waves_ref, own_ref, partner_ref, *refs):
@@ -264,12 +312,15 @@
 
 def fold_kernel(slots, levels, fields, arrived_ref, out_ref, rows_ref):
     tiles = rows_ref.shape[1]
-    stride = 2 * slots
+    stride = padded(slots)
     half = levels * stride
     for field in range(fields):
         for tile in range(tiles):
             lanes = pl.ds((field * tiles + tile) * LANES, LANES)
-            rows_ref[field, tile] = arrived_ref[:, lanes].astype(jnp.float32)
+            rows = arrived_ref[:, lanes].astype(jnp.float32)
+            for source in range(2 * levels):
+                mine = rows[2 * slots * source : 2 * slots * (source + 1)]
+                rows_ref[field, tile, pl.ds(stride * source, 2 * slots), :] = mine
     for slot in range(slots):
         for part in range(2):
             for field in range(fields):
@@ -294,14 +345,14 @@
         in_specs=[pl.BlockSpec((rows, width), lambda: (0, 0))],
         out_specs=pl.BlockSpec(shape, lambda: (0, 0, 0)),
         out_shape=jax.ShapeDtypeStruct(shape, jnp.bfloat16),
-        scratch_shapes=[pltpu.VMEM((fields, tiles, rows, LANES), jnp.float32)],
+        scratch_shapes=[pltpu.VMEM((fields, tiles, 2 * levels * padded(slots), LANES), jnp.float32)],
         compiler_params=pltpu.CompilerParams(vmem_limit_bytes=VMEM_BYTES),
         cost_estimate=pl.CostEstimate(flops=2 * rows * width, bytes_accessed=4 * rows * width, transcendentals=0),
         name="fold",
     )(arrived)
 
 
-def analysis_kernel(least, folded_ref, far_ref, even_ref, odd_ref, *refs):
+def analysis_kernel(least, folded_ref, even_ref, odd_ref, *refs):
     table_refs, out_ref = refs[:-1], refs[-1]
     row_total, degrees = out_ref.shape[1:]
     step = pl.program_id(0)
@@ -323,12 +374,10 @@
 
     @pl.when(step == len(least))
     def _():
-        width = far_ref.shape[2]
-        out_ref[:, :, : degrees - width] = jnp.zeros((out_ref.shape[0], row_total, degrees - width), out_ref.dtype)
-        out_ref[:, :, degrees - width :] = far_ref[...]
-
-
-def analyze(folded, far, even, odd, legendre, row_total, least, chunk):
+        out_ref[...] = jnp.zeros(out_ref.shape, out_ref.dtype)
+
+
+def analyze(folded, even, odd, legendre, row_total, least, chunk):
     slots, degrees, _ = legendre.shape
     block = 4
     near = len(least) - 1
@@ -339,7 +388,6 @@
         grid=(len(least) + 1,),
         in_specs=[
             pl.BlockSpec((block,) + folded.shape[1:], lambda i: (jnp.minimum(i, near), 0, 0)),
-            pl.BlockSpec(far.shape, lambda i: (0, 0, 0)),
             mask_spec,
             mask_spec,
         ]
@@ -356,21 +404,22 @@
             transcendentals=0,
         ),
         name="analysis",
-    )(folded, far, even, odd, *[legendre] * tiles)
+    )(folded, even, odd, *[legendre] * tiles)
 
 
 def closing_kernel(
-    levels, fields, least, chunk, arrived_ref, table_ref, base_ref, even_ref, odd_ref, out_ref, *refs
+    levels, fields, least, chunk, hemi_ref, arrived_ref, table_ref, base_ref, even_ref, odd_ref, own_ref, other_ref, out_ref, *refs
 ):
-    got_ref, north_ref, south_ref, sems = refs[:4]
-    held = refs[4:]
+    got_ref, north_ref, south_ref, far_ref, sems = refs[:5]
+    held = refs[5:]
     at, tiles = chunk
     groups = len(least)
     _, row_total, degrees = base_ref.shape
     block = 4
     slots = block * groups
-    stride = 2 * slots
-    half = levels * stride
+    each = 2 * slots
+    stride = padded(slots)
+    half = levels * each
     arriving = [
         pltpu.make_async_copy(
             arrived_ref.at[:, pl.ds(field * tiles * LANES, tiles * LANES)], got_ref.at[field], sems.at[3 * groups + field]
@@ -391,14 +440,30 @@
     for group in range(groups):
         tables[group].start()
         sums[group].start()
+    for local in range(4):
+        rows = pl.ds(min(local, 2) * row_total, row_total)
+        own, other = own_ref[rows, :], other_ref[rows, :].astype(jnp.float32)
+        both, change = own + other, jnp.where(hemi_ref[0] == 0, own - other, other - own)
+        if local == 2:
+            both, change = pltpu.roll(both, LANES // 2, 1), pltpu.roll(change, LANES // 2, 1)
+        even = even_ref[slots + local, :, degrees - LANES :]
+        odd = odd_ref[slots + local, :, degrees - LANES :]
+        far_ref[local] = both * even + change * odd
+    finished = pltpu.make_async_copy(
+        far_ref, out_ref.at[pl.ds(slots, 4), :, pl.ds(degrees - LANES, LANES)], sems.at[3 * groups + fields]
+    )
+    finished.start()
     for field in range(fields):
         arriving[field].wait()
         for tile in range(tiles):
             lanes = pl.ds(tile * LANES, LANES)
             north = got_ref[field, :half, lanes].astype(jnp.float32)
             south = got_ref[field, half:, lanes].astype(jnp.float32)
-            north_ref[field, tile] = north + south
-            south_ref[field, tile] = north - south
+            plus, minus = north + south, north - south
+            for level in range(levels):
+                rows = pl.ds(stride * level, each)
+                north_ref[field, tile, rows, :] = plus[each * level : each * (level + 1)]
+                south_ref[field, tile, rows, :] = minus[each * level : each * (level + 1)]
     for group, start in enumerate(least):
         tables[group].wait()
         sums[group].wait()
@@ -428,14 +493,15 @@
         results[group].start()
     for copy in results:
         copy.wait()
-
-
-def close(arrived, base, even, odd, legendre, fields, levels, least, chunk):
+    finished.wait()
+
+
+def close(hemi, own, other, arrived, base, even, odd, legendre, fields, levels, least, chunk):
     slots, row_total, degrees = base.shape
     block = 4
     rows, width = arrived.shape
     tiles = chunk[1]
-    half = pltpu.VMEM((fields, tiles, rows // 2, LANES), jnp.float32)
+    half = pltpu.VMEM((fields, tiles, levels * padded(block * len(least)), LANES), jnp.float32)
     held = []
     for start in least:
         held.append(pltpu.VMEM((block, degrees - start, tiles * LANES), jnp.bfloat16))
@@ -443,15 +509,18 @@
     anywhere = pl.BlockSpec(memory_space=pl.ANY)
     return pl.pallas_call(
         functools.partial(closing_kernel, levels, fields, least, chunk),
-        in_specs=[anywhere, anywhere, anywhere] + [pl.BlockSpec(even.shape, lambda: (0, 0, 0))] * 2,
+        in_specs=[pl.BlockSpec(memory_space=pltpu.SMEM), anywhere, anywhere, anywhere]
+        + [pl.BlockSpec(even.shape, lambda: (0, 0, 0))] * 2
+        + [pl.BlockSpec(own.shape, lambda: (0, 0))] * 2,
         out_specs=anywhere,
         out_shape=jax.ShapeDtypeStruct(base.shape, jnp.float32),
-        input_output_aliases={2: 0},
+        input_output_aliases={3: 0},
         scratch_shapes=[
             pltpu.VMEM((fields, rows, tiles * LANES), jnp.bfloat16),
             half,
             half,
-            pltpu.SemaphoreType.DMA((3 * len(least) + fields,)),
+            pltpu.VMEM((4, row_total, LANES), jnp.float32),
+            pltpu.SemaphoreType.DMA((3 * len(least) + fields + 1,)),
             *held,
         ],
         compiler_params=pltpu.CompilerParams(vmem_limit_bytes=VMEM_BYTES),
@@ -461,7 +530,7 @@
             transcendentals=0,
         ),
         name="closing",
-    )(arrived, legendre, base, even, odd)
+    )(hemi, arrived, legendre, base, even, odd, own, other)
 
 
 def across_halves(value):
@@ -554,29 +623,16 @@
     devices = 2 * levels
     least = tuple(4 * g * devices for g in range(slots // 4 - 1))
     near = slots - 4
-    far_least, last_least = near * devices, (near + 2) * devices
+    far_least = near * devices
     cut = tiles - tiles // 2
     chunks = [(0, cut), (cut, tiles - cut)]
 
     def send(spec, chunk):
         return synthesize(first.reshape(1), owner_table, spec, legendre, chunk, fields, levels, least)
 
-    large = send(spec_rows, chunks[0])
-    arrived = [exchange(large)]
-
-    late_spec, late_table = after((spec_rows, legendre), large)
-    table = jnp.concatenate(
-        [
-            late_table[near : near + 2, far_least:].reshape(-1, half_lat),
-            late_table[near + 2 :, last_least:].reshape(-1, half_lat),
-        ]
-    )
-    spec = late_spec[near:, :, far_least:]
-    width = last_least - far_least
-    packed = jnp.concatenate([spec[2, :, width:], spec[3, :, width:]], axis=1)
-    spec = jnp.concatenate([spec[:2].reshape(2 * row_total, -1), packed])
-    own_pack = jnp.concatenate([table, spec], axis=1)
+    own_pack = pack(spec_rows, legendre, near)
     partner_pack = across_halves(own_pack)
+    large = send(after(spec_rows, own_pack), chunks[0])
 
     bands, planes = lax.axis_size("band"), lax.axis_size("grp")
     by_device = jnp.swapaxes(owner_table.reshape(bands, planes, slots), 0, 1).reshape(2, levels, slots)
@@ -593,11 +649,12 @@
 
     small = send(after(spec_rows, large), chunks[1])
     by_wave, by_lon = trig_tables(after(waves, large), lon_count, small)
+    arrived = [exchange(after(large, small, partner_pack))]
     far_rows = far_synthesize(
         place, far_waves[0] - far_least, own_pack, partner_pack, levels, fields, 1.0 / math.sqrt(degrees)
     )
-    arrived.append(exchange(after(small, by_wave, *far_rows, *arrived)))
     far_rows = jnp.concatenate(within_half(far_rows))
+    arrived.append(exchange(after(small, far_rows, *arrived)))
     zonal = [
         longitudes(rows, far_rows, by_lon, by_wave, fields, chunk) for rows, chunk in zip(arrived, chunks)
     ]
@@ -606,28 +663,17 @@
     far_zonal = within_half([far_zonal[16 * x : 16 * x + 16] for x in range(levels)])
     own_sums, partner_sums = far_analyze(place, own_pack, partner_pack, far_zonal, levels, fields, chunks)
     returned.append(exchange(after(zonal[1][0], partner_sums, *returned)))
-    other_sums = across_halves(partner_sums).astype(jnp.float32)
-    north = jnp.where(hemi == 0, own_sums, other_sums)
-    south = jnp.where(hemi == 0, other_sums, own_sums)
+    other_sums = across_halves(partner_sums)
     wavenumber = lax.dynamic_slice_in_dim(after(owner_table, by_wave), first, slots)
     distance = jnp.arange(degrees, dtype=jnp.int32)[None, :] - wavenumber[:, None]
     scale = 1.0 / math.sqrt(2 * half_lat)
     even = jnp.where((distance >= 0) & (distance % 2 == 0), scale, 0.0).astype(jnp.float32)[:, None, :]
     odd = jnp.where((distance >= 0) & (distance % 2 != 0), scale, 0.0).astype(jnp.float32)[:, None, :]
 
-    def unpack(sums):
-        sums = sums.reshape(3, row_total, -1)
-        empty = jnp.zeros((row_total, width), jnp.float32)
-        third = jnp.concatenate([empty, sums[2, :, :width]], axis=1)
-        fourth = jnp.concatenate([empty, sums[2, :, width:]], axis=1)
-        return jnp.concatenate([sums[:2], third[None], fourth[None]])
-
-    far_even, far_odd = even[near:, :, far_least:], odd[near:, :, far_least:]
-    far_out = unpack(north + south) * far_even + unpack(north - south) * far_odd
     folded = fold(returned[0], near, levels, fields)
-    base = analyze(folded, far_out, even, odd, legendre, row_total, least, chunks[0])
+    base = analyze(folded, even, odd, legendre, row_total, least, chunks[0])
     last = after(returned[1], base)
-    out = close(last, base, even, odd, legendre, fields, levels, least, chunks[1])
+    out = close(hemi.reshape(1), own_sums, other_sums, last, base, even, odd, legendre, fields, levels, least, chunks[1])
     return out.reshape(slots, 2, fields, levels, degrees)
 
 

time: 390 us -> 315 us (0.81); the launches traced: 384 us -> 314 us
  waiting for transfers between devices: 162 us -> 114 us
  Pallas kernels: 120 us -> 108 us
  starting transfers between devices: 79 us -> 74 us
  local copies, waits for them, and re-layouts: 16.1 us -> 11.8 us
    ppermute x2, waiting for transfers between devices: 107 us -> 13.4 us  [across_halves(): lax.ppermute(value, 'grp', [(p, (p + planes // 2) % planes) for p in rang...]
    all_to_all x4, waiting for transfers between devices: 0.01 us -> 36.1 us  [exchange(): lax.all_to_all(rows, AXES[::-1], split_axis=0, concat_axis=0, tiled=True)]
    ppermute x30, waiting for transfers between devices: 54.9 us -> 64.8 us  [within_half(): moved.append(lax.ppermute(parts[x], AXES, pairs))]
    pallas_call x2, Pallas kernels: 20 us -> 13.4 us  [synthesize(): pl.pallas_call(functools.partial(synthesis_kernel, slots, levels, fields,...]
    all_to_all x4, starting transfers between devices: 26.3 us -> 21.6 us  [exchange(): lax.all_to_all(rows, AXES[::-1], split_axis=0, concat_axis=0, tiled=True)]
    pallas_call x1, Pallas kernels: 9.96 us -> 5.35 us  [fold(): pl.pallas_call(functools.partial(fold_kernel, slots, levels, fields), in_...]
  transfers between devices with their start and end apart: 36 -> 36, of which waited for: 14 -> 20; matrix products, arithmetic and copies ran while one was open for 5% -> 5% of each run, Pallas kernels for 26% -> 32%
where the time goes in v4:
time: 315 us; the launch traced here: 314 us
  waiting for transfers between devices  114 us (36%)
  Pallas kernels  108 us (34%)
  starting transfers between devices  74 us (23%)
  local copies, waits for them, and re-layouts  11.8 us (4%)
  other arithmetic  5.28 us (2%)
    ppermute x30, waiting for transfers between devices, within_half(): moved.append(lax.ppermute(parts[x], AXES, pairs))  64.8 us
    pallas_call x2, Pallas kernels, longitudes(): pl.pallas_call(functools.partial(longitude_kernel, fields, chunk, 1.0 / m...  53.1 us
    ppermute x30, starting transfers between devices, within_half(): moved.append(lax.ppermute(parts[x], AXES, pairs))  46 us
    all_to_all x4, waiting for transfers between devices, exchange(): lax.all_to_all(rows, AXES[::-1], split_axis=0, concat_axis=0, tiled=True)  36.1 us
    all_to_all x4, starting transfers between devices, exchange(): lax.all_to_all(rows, AXES[::-1], split_axis=0, concat_axis=0, tiled=True)  21.6 us
    pallas_call x2, Pallas kernels, synthesize(): pl.pallas_call(functools.partial(synthesis_kernel, slots, levels, fields,...  13.4 us
    ppermute x2, waiting for transfers between devices, across_halves(): lax.ppermute(value, 'grp', [(p, (p + planes // 2) % planes) for p in rang...  13.4 us
    pallas_call x1, Pallas kernels, trig_tables(): pl.pallas_call(trig_kernel, grid=(depth // rows,), in_specs=[small, small...  11.7 us
  transfers between devices with their start and end apart: 36, of which 20 were waited for; matrix products, arithmetic and copies ran while one was open for 5% of the time, Pallas kernels for 32%

profile of v4, /device:TPU:0, one launch (start us, length us, event | category | flops | bytes accessed | tf_op | source)
XLA Modules:
  0.0 314.0 jit_solution(12413613707166994627)
XLA Ops:
  2.1 4.1 %collective-permute-start = (bf16[384,768]{1,0:T(8,128)(2,1)}, bf16[384,768]{1,0:T(8,128)(2,1)S(1)}, u32[]{:S(2)}, u32[]{:S(2)}) collective-permute-start(bf16[384,768]{1,0:T(8,128)(2,1)} %pack.1.own_ref), channel_id=1, source_target_pairs={{0,2},{1,3},{2,0},{3,1},{4,6},{5,7},{6,4},{7,5},{8,10},{9,11},{10,... | collective-permute-start | bytes 1769480 | tf_op jit(solution)/shard_map/ppermute | solution.py:538
  6.2 7.5 %synthesis.2 = bf16[1024,1536]{1,0:T(8,128)(2,1)} custom-call(s32[1]{0:T(128)} %bitcast.1.first_ref, s32[640]{0:T(1024)} %owner_ref.3, bf16[20,128,640]{2,1,0:T(8,128)(2,1)} %bitcast.29, bf16[20,640,640]{2,1,0:T(8,128)(2,1)} %table_ref.7), custom_call_target="tpu_custom_call" | custom-call | flops 2013265920 | bytes 13631488 | tf_op jit(solution)/shard_map/synthesis/pallas_call | solution.py:81
  14.6 5.9 %synthesis.3 = bf16[1024,1024]{1,0:T(8,128)(2,1)} custom-call(s32[1]{0:T(128)} %bitcast.1.first_ref, s32[640]{0:T(1024)} %owner_ref.3, bf16[20,128,640]{2,1,0:T(8,128)(2,1)} %bitcast.30, bf16[20,640,640]{2,1,0:T(8,128)(2,1)} %table_ref.7), custom_call_target="tpu_custom_call" | custom-call | flops 1342177280 | bytes 9961472 | tf_op jit(solution)/shard_map/synthesis/pallas_call | solution.py:81
  20.5 11.8 %collective-permute-done.partner_ref = bf16[384,768]{1,0:T(8,128)(2,1)S(1)} collective-permute-done((bf16[384,768]{1,0:T(8,128)(2,1)}, bf16[384,768]{1,0:T(8,128)(2,1)S(1)}, u32[]{:S(2)}, u32[]{:S(2)}) %collective-permute-start) | collective-permute-done | bytes 589856 | tf_op jit(solution)/shard_map/ppermute | solution.py:538
  33.2 5.9 %all-to-all-start = ((bf16[32,32,1536]{2,1,0:T(8,128)(2,1)}), bf16[32,32,1536]{2,1,0:T(8,128)(2,1)}, u32[]{:S(2)}, u32[]{:S(2)}) async-start(bf16[32,32,1536]{2,1,0:T(8,128)(2,1)} %bitcast.31), calls=%async_computation | async-start | bytes 6291456 | tf_op jit(solution)/shard_map/all_to_all | solution.py:612
  51.3 12.5 %collective-permute-done.2 = bf16[16,2560]{1,0:T(8,128)(2,1)S(1)} collective-permute-done((bf16[16,2560]{1,0:T(8,128)(2,1)}, bf16[16,2560]{1,0:T(8,128)(2,1)S(1)}, u32[]{:S(2)}, u32[]{:S(2)}) %collective-permute-start.2) | collective-permute-done | bytes 81952 | tf_op jit(solution)/shard_map/ppermute | solution.py:552
  68.6 4.6 %collective-permute-done.6 = bf16[16,2560]{1,0:T(8,128)(2,1)S(1)} collective-permute-done((bf16[16,2560]{1,0:T(8,128)(2,1)}, bf16[16,2560]{1,0:T(8,128)(2,1)S(1)}, u32[]{:S(2)}, u32[]{:S(2)}) %collective-permute-start.6) | collective-permute-done | bytes 81952 | tf_op jit(solution)/shard_map/ppermute | solution.py:552
  76.9 16.5 %collective-permute-done.8 = bf16[16,2560]{1,0:T(8,128)(2,1)S(1)} collective-permute-done((bf16[16,2560]{1,0:T(8,128)(2,1)}, bf16[16,2560]{1,0:T(8,128)(2,1)S(1)}, u32[]{:S(2)}, u32[]{:S(2)}) %collective-permute-start.8) | collective-permute-done | bytes 81952 | tf_op jit(solution)/shard_map/ppermute | solution.py:552
  102.1 4.1 %collective-permute-done.14 = bf16[16,2560]{1,0:T(8,128)(2,1)S(1)} collective-permute-done((bf16[16,2560]{1,0:T(8,128)(2,1)S(1)}, bf16[16,2560]{1,0:T(8,128)(2,1)S(1)}, u32[]{:S(2)}, u32[]{:S(2)}) %collective-permute-start.14) | collective-permute-done | bytes 81952 | tf_op jit(solution)/shard_map/ppermute | solution.py:552
  111.9 4.6 %all-to-all-start.1 = ((bf16[32,32,1024]{2,1,0:T(8,128)(2,1)}), bf16[32,32,1024]{2,1,0:T(8,128)(2,1)}, u32[]{:S(2)}, u32[]{:S(2)}) async-start(bf16[32,32,1024]{2,1,0:T(8,128)(2,1)} %bitcast.12), calls=%async_computation.1 | async-start | bytes 4194304 | tf_op jit(solution)/shard_map/all_to_all | solution.py:612
  124.9 11.7 %trig.1 = (bf16[1280,2560]{1,0:T(8,128)(2,1)}, bf16[2560,1280]{1,0:T(8,128)(2,1)}) custom-call(f32[1280,20]{1,0:T(8,128)} %copy.31.cos_base_ref, f32[1280,20]{1,0:T(8,128)} %copy.32.sin_base_ref, f32[1280,128]{1,0:T(8,128)} %copy.33.cos_turn_ref, f32[1280,128]{1,0:T(8,128)} %copy.34.sin_turn_ref, f32[20,1280]{1,0:T(8,128)} %bitcast.37, f32[20,1280]{1,0:T(8,128)} %bitcast.36, ...), custom_call_target="tpu_custom_call" | custom-call | flops 26214400 | bytes 13107200 | tf_op jit(solution)/shard_map/trig/pallas_call | solution.py:591
  136.6 31.1 %longitudes.3 = (bf16[1024,1536]{1,0:T(8,128)(2,1)}, bf16[256,1536]{1,0:T(8,128)(2,1)}) custom-call(bf16[1024,1536]{1,0:T(8,128)(2,1)} %bitcast.11.rows_ref, bf16[256,2560]{1,0:T(8,128)(2,1)} %copy-done.23, bf16[2560,1280]{1,0:T(8,128)(2,1)} %get-tuple-element.66.by_lon_ref, bf16[1280,2560]{1,0:T(8,128)(2,1)} %get-tuple-element.67.by_wave_ref), custom_call_target="tpu_custom_call" | custom-call | flops 20132659200 | bytes 20971520 | tf_op jit(solution)/shard_map/longitudes/pallas_call | solution.py:137
  167.7 5.9 %all-to-all-start.2 = ((bf16[32,32,1536]{2,1,0:T(8,128)(2,1)}), bf16[32,32,1536]{2,1,0:T(8,128)(2,1)}, u32[]{:S(2)}, u32[]{:S(2)}) async-start(bf16[32,32,1536]{2,1,0:T(8,128)(2,1)} %bitcast.34), calls=%async_computation.2 | async-start | bytes 6291456 | tf_op jit(solution)/shard_map/all_to_all | solution.py:612
  173.7 22.0 %longitudes.2 = (bf16[1024,1024]{1,0:T(8,128)(2,1)}, bf16[256,1024]{1,0:T(8,128)(2,1)}) custom-call(bf16[1024,1024]{1,0:T(8,128)(2,1)} %bitcast.13.rows_ref, bf16[256,2560]{1,0:T(8,128)(2,1)} %copy-done.23, bf16[2560,1280]{1,0:T(8,128)(2,1)} %get-tuple-element.66.by_lon_ref, bf16[1280,2560]{1,0:T(8,128)(2,1)} %get-tuple-element.67.by_wave_ref), custom_call_target="tpu_custom_call" | custom-call | flops 13421772800 | bytes 18350080 | tf_op jit(solution)/shard_map/longitudes/pallas_call | solution.py:137
  203.6 5.5 %collective-permute-start.22 = (bf16[16,2560]{1,0:T(8,128)(2,1)S(1)}, bf16[16,2560]{1,0:T(8,128)(2,1)S(1)}, u32[]{:S(2)}, u32[]{:S(2)}) collective-permute-start(bf16[16,2560]{1,0:T(8,128)(2,1)S(1)} %get-tuple-element.85), channel_id=1, source_target_pairs={{0,28},{1,29},{2,30},{3,31},{4,24},{5,25},{6,26},{7,27},{8,20},{9,... | collective-permute-start | bytes 245768 | tf_op jit(solution)/shard_map/ppermute | solution.py:552
  211.2 4.6 %collective-permute-start.25 = (bf16[16,2560]{1,0:T(8,128)(2,1)S(1)}, bf16[16,2560]{1,0:T(8,128)(2,1)S(1)}, u32[]{:S(2)}, u32[]{:S(2)}) collective-permute-start(bf16[16,2560]{1,0:T(8,128)(2,1)S(1)} %get-tuple-element.82), channel_id=1, source_target_pairs={{0,9},{1,8},{2,11},{3,10},{4,13},{5,12},{6,15},{7,14},{8,1},{9,0},... | collective-permute-start | bytes 245768 | tf_op jit(solution)/shard_map/ppermute | solution.py:552
  217.4 4.3 %collective-permute-start.27 = (bf16[16,2560]{1,0:T(8,128)(2,1)S(1)}, bf16[16,2560]{1,0:T(8,128)(2,1)S(1)}, u32[]{:S(2)}, u32[]{:S(2)}) collective-permute-start(bf16[16,2560]{1,0:T(8,128)(2,1)S(1)} %get-tuple-element.80), channel_id=1, source_target_pairs={{0,17},{1,16},{2,19},{3,18},{4,21},{5,20},{6,23},{7,22},{8,25},{9,... | collective-permute-start | bytes 245768 | tf_op jit(solution)/shard_map/ppermute | solution.py:552
  221.8 5.6 %collective-permute-done.23.refs_8_ = bf16[16,2560]{1,0:T(8,128)(2,1)S(1)} collective-permute-done((bf16[16,2560]{1,0:T(8,128)(2,1)S(1)}, bf16[16,2560]{1,0:T(8,128)(2,1)S(1)}, u32[]{:S(2)}, u32[]{:S(2)}) %collective-permute-start.23) | collective-permute-done | bytes 81952 | tf_op jit(solution)/shard_map/ppermute | solution.py:552
  236.1 4.6 %collective-permute-done.29.refs_14_ = bf16[16,2560]{1,0:T(8,128)(2,1)S(1)} collective-permute-done((bf16[16,2560]{1,0:T(8,128)(2,1)S(1)}, bf16[16,2560]{1,0:T(8,128)(2,1)S(1)}, u32[]{:S(2)}, u32[]{:S(2)}) %collective-permute-start.29) | collective-permute-done | bytes 81952 | tf_op jit(solution)/shard_map/ppermute | solution.py:552
  248.6 5.2 %all-to-all-start.3 = ((bf16[32,32,1024]{2,1,0:T(8,128)(2,1)}), bf16[32,32,1024]{2,1,0:T(8,128)(2,1)}, u32[]{:S(2)}, u32[]{:S(2)}) async-start(bf16[32,32,1024]{2,1,0:T(8,128)(2,1)} %bitcast.35), calls=%async_computation.3 | async-start | bytes 4194304 | tf_op jit(solution)/shard_map/all_to_all | solution.py:612
  257.9 5.4 %fold.1.folded_ref = bf16[16,256,384]{2,1,0:T(8,128)(2,1)} custom-call(bf16[1024,1536]{1,0:T(8,128)(2,1)} %bitcast.19.arrived_ref), custom_call_target="tpu_custom_call" | custom-call | flops 3145728 | bytes 6291456 | tf_op jit(solution)/shard_map/fold/pallas_call | solution.py:343
  263.3 8.5 %analysis.1.base_ref = f32[20,128,640]{2,1,0:T(8,128)} custom-call(bf16[16,256,384]{2,1,0:T(8,128)(2,1)} %fold.1.folded_ref, f32[20,1,640]{2,1,0:T(1,128)} %get-tuple-element.100.even_ref, f32[20,1,640]{2,1,0:T(1,128)} %get-tuple-element.99.odd_ref, bf16[20,640,640]{2,1,0:T(8,128)(2,1)} %table_ref.7, bf16[20,640,640]{2,1,0:T(8,128)(2,1)} %table_ref.7, ...), custom_call_target="tpu_custom_call" | custom-call | flops 2516582400 | bytes 20316160 | tf_op jit(solution)/shard_map/analysis/pallas_call | solution.py:386
  271.8 33.3 %all-to-all-done.3 = bf16[32,32,1024]{2,1,0:T(8,128)(2,1)} async-done(((bf16[32,32,1024]{2,1,0:T(8,128)(2,1)}), bf16[32,32,1024]{2,1,0:T(8,128)(2,1)}, u32[]{:S(2)}, u32[]{:S(2)}) %all-to-all-start.3) | async-done | bytes 2097184 | tf_op jit(solution)/shard_map/all_to_all | solution.py:612
  307.3 6.5 %closing.1 = f32[20,128,640]{2,1,0:T(8,128)} custom-call(s32[1]{0:T(128)} %bitcast.hemi_ref, bf16[1024,1024]{1,0:T(8,128)(2,1)} %bitcast.21.arrived_ref, bf16[20,640,640]{2,1,0:T(8,128)(2,1)} %table_ref.7, f32[20,128,640]{2,1,0:T(8,128)} %analysis.1.base_ref, f32[20,1,640]{2,1,0:T(1,128)} %get-tuple-element.100.even_ref, ...), custom_call_target="tpu_custom_call", output_to_operand_aliasing={{}: (3, {})} | custom-call | flops 1677721600 | bytes 15204352 | tf_op jit(solution)/shard_map/closing/pallas_call | solution.py:510
  (164 shorter events, 81.6 us)
Async XLA Ops:
  2.1 30.3 %collective-permute-start = (bf16[384,768]{1,0:T(8,128)(2,1)}, bf16[384,768]{1,0:T(8,128)(2,1)S(1)}, u32[]{:S(2)}, u32[]{:S(2)}) collective-permute-start(bf16[384,768]{1,0:T(8,128)(2,1)} %pack.1.own_ref), channel_id=1, source_target_pairs={{0,2},{1,3},{2,0},{3,1},{4,6},{5,7},{6,4},{7,5},{8,10},{9,11},{10,... | collective-permute-start | bytes 1769480 | tf_op jit(solution)/shard_map/ppermute | solution.py:538
  33.2 78.7 %all-to-all-start = ((bf16[32,32,1536]{2,1,0:T(8,128)(2,1)}), bf16[32,32,1536]{2,1,0:T(8,128)(2,1)}, u32[]{:S(2)}, u32[]{:S(2)}) async-start(bf16[32,32,1536]{2,1,0:T(8,128)(2,1)} %bitcast.31), calls=%async_computation | async-start | bytes 6291456 | tf_op jit(solution)/shard_map/all_to_all | solution.py:612
  45.2 18.6 %collective-permute-start.2 = (bf16[16,2560]{1,0:T(8,128)(2,1)}, bf16[16,2560]{1,0:T(8,128)(2,1)S(1)}, u32[]{:S(2)}, u32[]{:S(2)}) collective-permute-start(bf16[16,2560]{1,0:T(8,128)(2,1)} %get-tuple-element.45), channel_id=1, source_target_pairs={{0,8},{1,9},{2,10},{3,11},{4,12},{5,13},{6,14},{7,15},{8,0},{9,1},... | collective-permute-start | bytes 245768 | tf_op jit(solution)/shard_map/ppermute | solution.py:552
  46.9 17.8 %collective-permute-start.3 = (bf16[16,2560]{1,0:T(8,128)(2,1)}, bf16[16,2560]{1,0:T(8,128)(2,1)S(1)}, u32[]{:S(2)}, u32[]{:S(2)}) collective-permute-start(bf16[16,2560]{1,0:T(8,128)(2,1)} %get-tuple-element.46), channel_id=1, source_target_pairs={{0,12},{1,13},{2,14},{3,15},{4,8},{5,9},{6,10},{7,11},{8,4},{9,5},... | collective-permute-start | bytes 245768 | tf_op jit(solution)/shard_map/ppermute | solution.py:552
  46.9 18.2 %collective-permute-start.4 = (bf16[16,2560]{1,0:T(8,128)(2,1)}, bf16[16,2560]{1,0:T(8,128)(2,1)S(1)}, u32[]{:S(2)}, u32[]{:S(2)}) collective-permute-start(bf16[16,2560]{1,0:T(8,128)(2,1)} %get-tuple-element.47), channel_id=1, source_target_pairs={{0,16},{1,17},{2,18},{3,19},{4,20},{5,21},{6,22},{7,23},{8,24},{9,... | collective-permute-start | bytes 245768 | tf_op jit(solution)/shard_map/ppermute | solution.py:552
  48.6 18.8 %collective-permute-start.5 = (bf16[16,2560]{1,0:T(8,128)(2,1)}, bf16[16,2560]{1,0:T(8,128)(2,1)S(1)}, u32[]{:S(2)}, u32[]{:S(2)}) collective-permute-start(bf16[16,2560]{1,0:T(8,128)(2,1)} %get-tuple-element.48), channel_id=1, source_target_pairs={{0,20},{1,21},{2,22},{3,23},{4,16},{5,17},{6,18},{7,19},{8,28},{9,... | collective-permute-start | bytes 245768 | tf_op jit(solution)/shard_map/ppermute | solution.py:552
  48.7 24.5 %collective-permute-start.6 = (bf16[16,2560]{1,0:T(8,128)(2,1)}, bf16[16,2560]{1,0:T(8,128)(2,1)S(1)}, u32[]{:S(2)}, u32[]{:S(2)}) collective-permute-start(bf16[16,2560]{1,0:T(8,128)(2,1)} %get-tuple-element.49), channel_id=1, source_target_pairs={{0,24},{1,25},{2,26},{3,27},{4,28},{5,29},{6,30},{7,31},{8,16},{9,... | collective-permute-start | bytes 245768 | tf_op jit(solution)/shard_map/ppermute | solution.py:552
  63.7 13.1 %collective-permute-start.7 = (bf16[16,2560]{1,0:T(8,128)(2,1)}, bf16[16,2560]{1,0:T(8,128)(2,1)S(1)}, u32[]{:S(2)}, u32[]{:S(2)}) collective-permute-start(bf16[16,2560]{1,0:T(8,128)(2,1)} %get-tuple-element.50), channel_id=1, source_target_pairs={{0,28},{1,29},{2,30},{3,31},{4,24},{5,25},{6,26},{7,27},{8,20},{9,... | collective-permute-start | bytes 245768 | tf_op jit(solution)/shard_map/ppermute | solution.py:552
  64.6 28.7 %collective-permute-start.8 = (bf16[16,2560]{1,0:T(8,128)(2,1)}, bf16[16,2560]{1,0:T(8,128)(2,1)S(1)}, u32[]{:S(2)}, u32[]{:S(2)}) collective-permute-start(bf16[16,2560]{1,0:T(8,128)(2,1)} %get-tuple-element.51), channel_id=1, source_target_pairs={{0,1},{1,0},{2,3},{3,2},{4,5},{5,4},{6,7},{7,6},{8,9},{9,8},{10,11... | collective-permute-start | bytes 245768 | tf_op jit(solution)/shard_map/ppermute | solution.py:552
  65.1 30.1 %collective-permute-start.9 = (bf16[16,2560]{1,0:T(8,128)(2,1)}, bf16[16,2560]{1,0:T(8,128)(2,1)S(1)}, u32[]{:S(2)}, u32[]{:S(2)}) collective-permute-start(bf16[16,2560]{1,0:T(8,128)(2,1)} %get-tuple-element.52), channel_id=1, source_target_pairs={{0,5},{1,4},{2,7},{3,6},{4,1},{5,0},{6,3},{7,2},{8,13},{9,12},{10,... | collective-permute-start | bytes 245768 | tf_op jit(solution)/shard_map/ppermute | solution.py:552
  67.4 31.1 %collective-permute-start.10 = (bf16[16,2560]{1,0:T(8,128)(2,1)}, bf16[16,2560]{1,0:T(8,128)(2,1)S(1)}, u32[]{:S(2)}, u32[]{:S(2)}) collective-permute-start(bf16[16,2560]{1,0:T(8,128)(2,1)} %get-tuple-element.53), channel_id=1, source_target_pairs={{0,9},{1,8},{2,11},{3,10},{4,13},{5,12},{6,15},{7,14},{8,1},{9,0},... | collective-permute-start | bytes 245768 | tf_op jit(solution)/shard_map/ppermute | solution.py:552
  73.2 26.6 %collective-permute-start.11 = (bf16[16,2560]{1,0:T(8,128)(2,1)}, bf16[16,2560]{1,0:T(8,128)(2,1)S(1)}, u32[]{:S(2)}, u32[]{:S(2)}) collective-permute-start(bf16[16,2560]{1,0:T(8,128)(2,1)} %get-tuple-element.54), channel_id=1, source_target_pairs={{0,13},{1,12},{2,15},{3,14},{4,9},{5,8},{6,11},{7,10},{8,5},{9,4},... | collective-permute-start | bytes 245768 | tf_op jit(solution)/shard_map/ppermute | solution.py:552
  76.9 23.5 %collective-permute-start.12 = (bf16[16,2560]{1,0:T(8,128)(2,1)}, bf16[16,2560]{1,0:T(8,128)(2,1)S(1)}, u32[]{:S(2)}, u32[]{:S(2)}) collective-permute-start(bf16[16,2560]{1,0:T(8,128)(2,1)} %get-tuple-element.55), channel_id=1, source_target_pairs={{0,17},{1,16},{2,19},{3,18},{4,21},{5,20},{6,23},{7,22},{8,25},{9,... | collective-permute-start | bytes 245768 | tf_op jit(solution)/shard_map/ppermute | solution.py:552
  111.9 55.8 %all-to-all-start.1 = ((bf16[32,32,1024]{2,1,0:T(8,128)(2,1)}), bf16[32,32,1024]{2,1,0:T(8,128)(2,1)}, u32[]{:S(2)}, u32[]{:S(2)}) async-start(bf16[32,32,1024]{2,1,0:T(8,128)(2,1)} %bitcast.12), calls=%async_computation.1 | async-start | bytes 4194304 | tf_op jit(solution)/shard_map/all_to_all | solution.py:612
  167.7 80.9 %all-to-all-start.2 = ((bf16[32,32,1536]{2,1,0:T(8,128)(2,1)}), bf16[32,32,1536]{2,1,0:T(8,128)(2,1)}, u32[]{:S(2)}, u32[]{:S(2)}) async-start(bf16[32,32,1536]{2,1,0:T(8,128)(2,1)} %bitcast.34), calls=%async_computation.2 | async-start | bytes 6291456 | tf_op jit(solution)/shard_map/all_to_all | solution.py:612
  201.0 14.8 %collective-permute-start.21 = (bf16[16,2560]{1,0:T(8,128)(2,1)S(1)}, bf16[16,2560]{1,0:T(8,128)(2,1)S(1)}, u32[]{:S(2)}, u32[]{:S(2)}) collective-permute-start(bf16[16,2560]{1,0:T(8,128)(2,1)S(1)} %get-tuple-element.86), channel_id=1, source_target_pairs={{0,24},{1,25},{2,26},{3,27},{4,28},{5,29},{6,30},{7,31},{8,16},{9,... | collective-permute-start | bytes 245768 | tf_op jit(solution)/shard_map/ppermute | solution.py:552
  203.6 13.8 %collective-permute-start.22 = (bf16[16,2560]{1,0:T(8,128)(2,1)S(1)}, bf16[16,2560]{1,0:T(8,128)(2,1)S(1)}, u32[]{:S(2)}, u32[]{:S(2)}) collective-permute-start(bf16[16,2560]{1,0:T(8,128)(2,1)S(1)} %get-tuple-element.85), channel_id=1, source_target_pairs={{0,28},{1,29},{2,30},{3,31},{4,24},{5,25},{6,26},{7,27},{8,20},{9,... | collective-permute-start | bytes 245768 | tf_op jit(solution)/shard_map/ppermute | solution.py:552
  209.6 17.8 %collective-permute-start.23 = (bf16[16,2560]{1,0:T(8,128)(2,1)S(1)}, bf16[16,2560]{1,0:T(8,128)(2,1)S(1)}, u32[]{:S(2)}, u32[]{:S(2)}) collective-permute-start(bf16[16,2560]{1,0:T(8,128)(2,1)S(1)} %get-tuple-element.84), channel_id=1, source_target_pairs={{0,1},{1,0},{2,3},{3,2},{4,5},{5,4},{6,7},{7,6},{8,9},{9,8},{10,11... | collective-permute-start | bytes 245768 | tf_op jit(solution)/shard_map/ppermute | solution.py:552
  209.6 19.9 %collective-permute-start.24 = (bf16[16,2560]{1,0:T(8,128)(2,1)S(1)}, bf16[16,2560]{1,0:T(8,128)(2,1)S(1)}, u32[]{:S(2)}, u32[]{:S(2)}) collective-permute-start(bf16[16,2560]{1,0:T(8,128)(2,1)S(1)} %get-tuple-element.83), channel_id=1, source_target_pairs={{0,5},{1,4},{2,7},{3,6},{4,1},{5,0},{6,3},{7,2},{8,13},{9,12},{10,... | collective-permute-start | bytes 245768 | tf_op jit(solution)/shard_map/ppermute | solution.py:552
  211.2 21.6 %collective-permute-start.25 = (bf16[16,2560]{1,0:T(8,128)(2,1)S(1)}, bf16[16,2560]{1,0:T(8,128)(2,1)S(1)}, u32[]{:S(2)}, u32[]{:S(2)}) collective-permute-start(bf16[16,2560]{1,0:T(8,128)(2,1)S(1)} %get-tuple-element.82), channel_id=1, source_target_pairs={{0,9},{1,8},{2,11},{3,10},{4,13},{5,12},{6,15},{7,14},{8,1},{9,0},... | collective-permute-start | bytes 245768 | tf_op jit(solution)/shard_map/ppermute | solution.py:552
  215.8 18.1 %collective-permute-start.26 = (bf16[16,2560]{1,0:T(8,128)(2,1)S(1)}, bf16[16,2560]{1,0:T(8,128)(2,1)S(1)}, u32[]{:S(2)}, u32[]{:S(2)}) collective-permute-start(bf16[16,2560]{1,0:T(8,128)(2,1)S(1)} %get-tuple-element.81), channel_id=1, source_target_pairs={{0,13},{1,12},{2,15},{3,14},{4,9},{5,8},{6,11},{7,10},{8,5},{9,4},... | collective-permute-start | bytes 245768 | tf_op jit(solution)/shard_map/ppermute | solution.py:552
  217.4 17.0 %collective-permute-start.27 = (bf16[16,2560]{1,0:T(8,128)(2,1)S(1)}, bf16[16,2560]{1,0:T(8,128)(2,1)S(1)}, u32[]{:S(2)}, u32[]{:S(2)}) collective-permute-start(bf16[16,2560]{1,0:T(8,128)(2,1)S(1)} %get-tuple-element.80), channel_id=1, source_target_pairs={{0,17},{1,16},{2,19},{3,18},{4,21},{5,20},{6,23},{7,22},{8,25},{9,... | collective-permute-start | bytes 245768 | tf_op jit(solution)/shard_map/ppermute | solution.py:552
  248.6 56.5 %all-to-all-start.3 = ((bf16[32,32,1024]{2,1,0:T(8,128)(2,1)}), bf16[32,32,1024]{2,1,0:T(8,128)(2,1)}, u32[]{:S(2)}, u32[]{:S(2)}) async-start(bf16[32,32,1024]{2,1,0:T(8,128)(2,1)} %bitcast.35), calls=%async_computation.3 | async-start | bytes 4194304 | tf_op jit(solution)/shard_map/all_to_all | solution.py:612
  255.6 51.1 %collective-permute-start.31 = (bf16[384,128]{1,0:T(8,128)(2,1)S(1)}, bf16[384,128]{1,0:T(8,128)(2,1)S(1)}, u32[]{:S(2)}, u32[]{:S(2)}) collective-permute-start(bf16[384,128]{1,0:T(8,128)(2,1)S(1)} %copy-done.25), channel_id=1, source_target_pairs={{0,2},{1,3},{2,0},{3,1},{4,6},{5,7},{6,4},{7,5},{8,10},{9,11},{10,... | collective-permute-start | bytes 294920 | tf_op jit(solution)/shard_map/ppermute | solution.py:538
  (41 other events, 628.0 us)

commit v5 on v4

--- a/solution.py
+++ b/solution.py
@@ -557,15 +557,24 @@
     return lax.optimization_barrier((value, others))[0]
 
 
-def trig_kernel(cos_base_ref, sin_base_ref, cos_turn_ref, sin_turn_ref, cos_base_t, sin_base_t, cos_turn_t, sin_turn_t, by_wave_ref, by_lon_ref):
-    for j in range(cos_base_ref.shape[1]):
-        lanes = pl.ds(j * LANES, LANES)
-        cos_base, sin_base = cos_base_ref[:, j : j + 1], sin_base_ref[:, j : j + 1]
-        angles = cos_base * cos_turn_ref[...] - sin_base * sin_turn_ref[...]
-        by_wave_ref[:, lanes] = angles.astype(by_wave_ref.dtype)
-        cos_base, sin_base = cos_base_t[j : j + 1, :], sin_base_t[j : j + 1, :]
-        angles = cos_base * cos_turn_t[...] - sin_base * sin_turn_t[...]
-        by_lon_ref[lanes, :] = angles.astype(by_lon_ref.dtype)
+def trig_kernel(small_ref, cos_turn_ref, sin_turn_ref, by_wave_ref, by_lon_ref):
+    shape = cos_turn_ref.shape
+    cos_start, sin_start, cos_step, sin_step = [
+        jnp.broadcast_to(small_ref[:, column : column + 1], shape) for column in range(4)
+    ]
+    cos_turn, sin_turn = cos_turn_ref[...], sin_turn_ref[...]
+    cosine = cos_start * cos_turn - sin_start * sin_turn
+    sine = sin_start * cos_turn + cos_start * sin_turn
+    flipped = [x.T for x in (cosine, sine, cos_step, sin_step)]
+    blocks = by_wave_ref.shape[1] // LANES
+    for position, (c, s, dc, ds) in enumerate(((cosine, sine, cos_step, sin_step), flipped)):
+        for block in range(blocks):
+            part = pl.ds(block * LANES, LANES)
+            if position == 0:
+                by_wave_ref[:, part] = c.astype(by_wave_ref.dtype)
+            else:
+                by_lon_ref[part, :] = c.astype(by_lon_ref.dtype)
+            c, s = c * dc - s * ds, s * dc + c * ds
 
 
 def trig_tables(owner_table, lon_count, *others):
@@ -573,25 +582,21 @@
     quarter = jnp.tile(jnp.array([0, lon_count // 4], jnp.float32), owner_table.shape[0])[:, None]
     unit = 2.0 * math.pi / lon_count
 
-    def angles(lon, turn):
-        phase = waves * lon + turn
+    def angles(phase):
         return (phase - lon_count * jnp.floor(phase * (1.0 / lon_count))) * unit
 
-    base = angles(jnp.arange(0, lon_count, LANES, dtype=jnp.float32)[None, :], quarter)
-    turn = angles(jnp.arange(LANES, dtype=jnp.float32)[None, :], 0.0)
+    start = angles(quarter)
+    step = angles(waves * LANES)
+    turn = angles(waves * jnp.arange(LANES, dtype=jnp.float32)[None, :])
+    small = jnp.concatenate([jnp.cos(start), jnp.sin(start), jnp.cos(step), jnp.sin(step)], axis=1)
+    parts = after((small, jnp.cos(turn), jnp.sin(turn)), *others)
     depth = waves.shape[0]
-    blocks = lon_count // LANES
     rows = 256
-    small = pl.BlockSpec((rows, blocks), lambda i: (i, 0))
     wide = pl.BlockSpec((rows, LANES), lambda i: (i, 0))
-    small_t = pl.BlockSpec((blocks, rows), lambda i: (0, i))
-    wide_t = pl.BlockSpec((LANES, rows), lambda i: (0, i))
-    parts = (jnp.cos(base), jnp.sin(base), jnp.cos(turn), jnp.sin(turn))
-    parts = after(parts, *others)
     return pl.pallas_call(
         trig_kernel,
         grid=(depth // rows,),
-        in_specs=[small, small, wide, wide, small_t, small_t, wide_t, wide_t],
+        in_specs=[pl.BlockSpec((rows, 4), lambda i: (i, 0)), wide, wide],
         out_specs=[
             pl.BlockSpec((rows, lon_count), lambda i: (i, 0)),
             pl.BlockSpec((lon_count, rows), lambda i: (0, i)),
@@ -602,10 +607,10 @@
         ],
         compiler_params=pltpu.CompilerParams(vmem_limit_bytes=VMEM_BYTES),
         cost_estimate=pl.CostEstimate(
-            flops=8 * depth * lon_count, bytes_accessed=4 * depth * lon_count, transcendentals=0
+            flops=12 * depth * lon_count, bytes_accessed=4 * depth * lon_count, transcendentals=0
         ),
         name="trig",
-    )(*parts, *[x.T for x in parts])
+    )(*parts)
 
 
 def exchange(rows):
@@ -648,8 +653,8 @@
     waves = jnp.concatenate([by_device[:, :, :near].reshape(-1), far_waves.reshape(-1)])
 
     small = send(after(spec_rows, large), chunks[1])
-    by_wave, by_lon = trig_tables(after(waves, large), lon_count, small)
-    arrived = [exchange(after(large, small, partner_pack))]
+    by_wave, by_lon = trig_tables(after(waves, own_pack), lon_count, large)
+    arrived = [exchange(after(large, small, by_wave, partner_pack))]
     far_rows = far_synthesize(
         place, far_waves[0] - far_least, own_pack, partner_pack, levels, fields, 1.0 / math.sqrt(degrees)
     )
@@ -661,8 +666,8 @@
     returned = [exchange(zonal[0][0])]
     far_zonal = jnp.concatenate([zonal[0][1], zonal[1][1]], axis=1)
     far_zonal = within_half([far_zonal[16 * x : 16 * x + 16] for x in range(levels)])
+    returned.append(exchange(after(zonal[1][0], *far_zonal[: levels - 4], *returned)))
     own_sums, partner_sums = far_analyze(place, own_pack, partner_pack, far_zonal, levels, fields, chunks)
-    returned.append(exchange(after(zonal[1][0], partner_sums, *returned)))
     other_sums = across_halves(partner_sums)
     wavenumber = lax.dynamic_slice_in_dim(after(owner_table, by_wave), first, slots)
     distance = jnp.arange(degrees, dtype=jnp.int32)[None, :] - wavenumber[:, None]

time: 315 us -> 323 us (1.025)
  waiting for transfers between devices: 114 us -> 132 us
  starting transfers between devices: 74 us -> 68 us
    ppermute x30, waiting for transfers between devices: 64.8 us -> 98.7 us  [within_half(): moved.append(lax.ppermute(parts[x], AXES, pairs))]
    ppermute x2, waiting for transfers between devices: 13.4 us -> 0.01 us  [across_halves(): lax.ppermute(value, 'grp', [(p, (p + planes // 2) % planes) for p in rang...]
    all_to_all x4, starting transfers between devices: 21.6 us -> 16.7 us  [exchange(): lax.all_to_all(rows, AXES[::-1], split_axis=0, concat_axis=0, tiled=True)]
    ppermute x30, starting transfers between devices: 46 us -> 41.4 us  [within_half(): moved.append(lax.ppermute(parts[x], AXES, pairs))]
    ppermute x2, starting transfers between devices: 6.45 us -> 10 us  [across_halves(): lax.ppermute(value, 'grp', [(p, (p + planes // 2) % planes) for p in rang...]
    optimization_barrier x4 -> x1, local copies, waits for them, and re-layouts: 4.61 us -> 1.13 us  [after(): return lax.optimization_barrier((value, others))[0]]
  transfers between devices with their start and end apart: 36 -> 36, of which waited for: 20 -> 22; matrix products, arithmetic and copies ran while one was open for 5% -> 4% of each run, Pallas kernels for 32% -> 30%
where the time goes in v5:
time: 323 us; the launch traced here: 322 us
  waiting for transfers between devices  132 us (41%)
  Pallas kernels  105 us (33%)
  starting transfers between devices  68 us (21%)
  local copies, waits for them, and re-layouts  9.33 us (3%)
  other arithmetic  6.54 us (2%)
    ppermute x30, waiting for transfers between devices, within_half(): moved.append(lax.ppermute(parts[x], AXES, pairs))  98.7 us
    pallas_call x2, Pallas kernels, longitudes(): pl.pallas_call(functools.partial(longitude_kernel, fields, chunk, 1.0 / m...  53 us
    ppermute x30, starting transfers between devices, within_half(): moved.append(lax.ppermute(parts[x], AXES, pairs))  41.4 us
    all_to_all x4, waiting for transfers between devices, exchange(): lax.all_to_all(rows, AXES[::-1], split_axis=0, concat_axis=0, tiled=True)  33.7 us
    all_to_all x4, starting transfers between devices, exchange(): lax.all_to_all(rows, AXES[::-1], split_axis=0, concat_axis=0, tiled=True)  16.7 us
    pallas_call x2, Pallas kernels, synthesize(): pl.pallas_call(functools.partial(synthesis_kernel, slots, levels, fields,...  13.4 us
    ppermute x2, starting transfers between devices, across_halves(): lax.ppermute(value, 'grp', [(p, (p + planes // 2) % planes) for p in rang...  10 us
    pallas_call x1, Pallas kernels, trig_tables(): pl.pallas_call(trig_kernel, grid=(depth // rows,), in_specs=[pl.BlockSpec...  9.01 us
  transfers between devices with their start and end apart: 36, of which 22 were waited for; matrix products, arithmetic and copies ran while one was open for 4% of the time, Pallas kernels for 30%

profile of v5, /device:TPU:0, one launch (start us, length us, event | category | flops | bytes accessed | tf_op | source)
XLA Modules:
  0.0 322.0 jit_solution(6111079173872451568)
XLA Ops:
  2.1 4.1 %collective-permute-start = (bf16[384,768]{1,0:T(8,128)(2,1)}, bf16[384,768]{1,0:T(8,128)(2,1)S(1)}, u32[]{:S(2)}, u32[]{:S(2)}) collective-permute-start(bf16[384,768]{1,0:T(8,128)(2,1)} %pack.1.own_ref), channel_id=1, source_target_pairs={{0,2},{1,3},{2,0},{3,1},{4,6},{5,7},{6,4},{7,5},{8,10},{9,11},{10,... | collective-permute-start | bytes 1769480 | tf_op jit(solution)/shard_map/ppermute | solution.py:538
  7.5 7.5 %synthesis.2 = bf16[1024,1536]{1,0:T(8,128)(2,1)} custom-call(s32[1]{0:T(128)} %bitcast.1.first_ref, s32[640]{0:T(1024)} %owner_ref.3, bf16[20,128,640]{2,1,0:T(8,128)(2,1)} %bitcast.25, bf16[20,640,640]{2,1,0:T(8,128)(2,1)} %table_ref.7), custom_call_target="tpu_custom_call" | custom-call | flops 2013265920 | bytes 13631488 | tf_op jit(solution)/shard_map/synthesis/pallas_call | solution.py:81
  21.6 9.0 %trig.1 = (bf16[1280,2560]{1,0:T(8,128)(2,1)}, bf16[2560,1280]{1,0:T(8,128)(2,1)}) custom-call(f32[1280,4]{1,0:T(8,128)} %copy.38.small_ref, f32[1280,128]{1,0:T(8,128)} %get-tuple-element.60.cos_turn_ref, f32[1280,128]{1,0:T(8,128)} %get-tuple-element.61.sin_turn_ref), custom_call_target="tpu_custom_call" | custom-call | flops 39321600 | bytes 13107200 | tf_op jit(solution)/shard_map/trig/pallas_call | solution.py:596
  30.7 5.9 %synthesis.3 = bf16[1024,1024]{1,0:T(8,128)(2,1)} custom-call(s32[1]{0:T(128)} %bitcast.1.first_ref, s32[640]{0:T(1024)} %owner_ref.3, bf16[20,128,640]{2,1,0:T(8,128)(2,1)} %bitcast.26, bf16[20,640,640]{2,1,0:T(8,128)(2,1)} %table_ref.7), custom_call_target="tpu_custom_call" | custom-call | flops 1342177280 | bytes 9961472 | tf_op jit(solution)/shard_map/synthesis/pallas_call | solution.py:81
  37.4 4.1 %all-to-all-start = ((bf16[32,32,1536]{2,1,0:T(8,128)(2,1)}), bf16[32,32,1536]{2,1,0:T(8,128)(2,1)}, u32[]{:S(2)}, u32[]{:S(2)}) async-start(bf16[32,32,1536]{2,1,0:T(8,128)(2,1)} %bitcast.27), calls=%async_computation | async-start | bytes 6291456 | tf_op jit(solution)/shard_map/all_to_all | solution.py:617
  53.5 12.4 %collective-permute-done.2 = bf16[16,2560]{1,0:T(8,128)(2,1)S(1)} collective-permute-done((bf16[16,2560]{1,0:T(8,128)(2,1)}, bf16[16,2560]{1,0:T(8,128)(2,1)S(1)}, u32[]{:S(2)}, u32[]{:S(2)}) %collective-permute-start.2) | collective-permute-done | bytes 81952 | tf_op jit(solution)/shard_map/ppermute | solution.py:552
  70.9 4.5 %collective-permute-done.6 = bf16[16,2560]{1,0:T(8,128)(2,1)S(1)} collective-permute-done((bf16[16,2560]{1,0:T(8,128)(2,1)}, bf16[16,2560]{1,0:T(8,128)(2,1)S(1)}, u32[]{:S(2)}, u32[]{:S(2)}) %collective-permute-start.6) | collective-permute-done | bytes 81952 | tf_op jit(solution)/shard_map/ppermute | solution.py:552
  79.1 16.5 %collective-permute-done.8 = bf16[16,2560]{1,0:T(8,128)(2,1)S(1)} collective-permute-done((bf16[16,2560]{1,0:T(8,128)(2,1)}, bf16[16,2560]{1,0:T(8,128)(2,1)S(1)}, u32[]{:S(2)}, u32[]{:S(2)}) %collective-permute-start.8) | collective-permute-done | bytes 81952 | tf_op jit(solution)/shard_map/ppermute | solution.py:552
  104.3 4.0 %collective-permute-done.14 = bf16[16,2560]{1,0:T(8,128)(2,1)S(1)} collective-permute-done((bf16[16,2560]{1,0:T(8,128)(2,1)S(1)}, bf16[16,2560]{1,0:T(8,128)(2,1)S(1)}, u32[]{:S(2)}, u32[]{:S(2)}) %collective-permute-start.14) | collective-permute-done | bytes 81952 | tf_op jit(solution)/shard_map/ppermute | solution.py:552
  114.4 4.1 %all-to-all-start.1 = ((bf16[32,32,1024]{2,1,0:T(8,128)(2,1)}), bf16[32,32,1024]{2,1,0:T(8,128)(2,1)}, u32[]{:S(2)}, u32[]{:S(2)}) async-start(bf16[32,32,1024]{2,1,0:T(8,128)(2,1)} %bitcast.12), calls=%async_computation.1 | async-start | bytes 4194304 | tf_op jit(solution)/shard_map/all_to_all | solution.py:617
  118.6 31.0 %longitudes.3 = (bf16[1024,1536]{1,0:T(8,128)(2,1)}, bf16[256,1536]{1,0:T(8,128)(2,1)}) custom-call(bf16[1024,1536]{1,0:T(8,128)(2,1)} %bitcast.11.rows_ref, bf16[256,2560]{1,0:T(8,128)(2,1)} %copy-done.19, bf16[2560,1280]{1,0:T(8,128)(2,1)} %get-tuple-element.65.by_lon_ref, bf16[1280,2560]{1,0:T(8,128)(2,1)} %get-tuple-element.62.by_wave_ref), custom_call_target="tpu_custom_call" | custom-call | flops 20132659200 | bytes 20971520 | tf_op jit(solution)/shard_map/longitudes/pallas_call | solution.py:137
  149.6 17.9 %all-to-all-done.1 = bf16[32,32,1024]{2,1,0:T(8,128)(2,1)} async-done(((bf16[32,32,1024]{2,1,0:T(8,128)(2,1)}), bf16[32,32,1024]{2,1,0:T(8,128)(2,1)}, u32[]{:S(2)}, u32[]{:S(2)}) %all-to-all-start.1) | async-done | bytes 2097184 | tf_op jit(solution)/shard_map/all_to_all | solution.py:617
  167.4 4.1 %all-to-all-start.2 = ((bf16[32,32,1536]{2,1,0:T(8,128)(2,1)}), bf16[32,32,1536]{2,1,0:T(8,128)(2,1)}, u32[]{:S(2)}, u32[]{:S(2)}) async-start(bf16[32,32,1536]{2,1,0:T(8,128)(2,1)} %bitcast.28), calls=%async_computation.2 | async-start | bytes 6291456 | tf_op jit(solution)/shard_map/all_to_all | solution.py:617
  171.6 22.0 %longitudes.2 = (bf16[1024,1024]{1,0:T(8,128)(2,1)}, bf16[256,1024]{1,0:T(8,128)(2,1)}) custom-call(bf16[1024,1024]{1,0:T(8,128)(2,1)} %bitcast.13.rows_ref, bf16[256,2560]{1,0:T(8,128)(2,1)} %copy-done.19, bf16[2560,1280]{1,0:T(8,128)(2,1)} %get-tuple-element.65.by_lon_ref, bf16[1280,2560]{1,0:T(8,128)(2,1)} %get-tuple-element.62.by_wave_ref), custom_call_target="tpu_custom_call" | custom-call | flops 13421772800 | bytes 18350080 | tf_op jit(solution)/shard_map/longitudes/pallas_call | solution.py:137
  201.7 5.5 %collective-permute-start.22 = (bf16[16,2560]{1,0:T(8,128)(2,1)S(1)}, bf16[16,2560]{1,0:T(8,128)(2,1)S(1)}, u32[]{:S(2)}, u32[]{:S(2)}) collective-permute-start(bf16[16,2560]{1,0:T(8,128)(2,1)S(1)} %get-tuple-element.85), channel_id=1, source_target_pairs={{0,28},{1,29},{2,30},{3,31},{4,24},{5,25},{6,26},{7,27},{8,20},{9,... | collective-permute-start | bytes 245768 | tf_op jit(solution)/shard_map/ppermute | solution.py:552
  209.3 4.7 %collective-permute-start.25 = (bf16[16,2560]{1,0:T(8,128)(2,1)S(1)}, bf16[16,2560]{1,0:T(8,128)(2,1)S(1)}, u32[]{:S(2)}, u32[]{:S(2)}) collective-permute-start(bf16[16,2560]{1,0:T(8,128)(2,1)S(1)} %get-tuple-element.82), channel_id=1, source_target_pairs={{0,9},{1,8},{2,11},{3,10},{4,13},{5,12},{6,15},{7,14},{8,1},{9,0},... | collective-permute-start | bytes 245768 | tf_op jit(solution)/shard_map/ppermute | solution.py:552
  215.6 9.9 %collective-permute-done.23.refs_8_ = bf16[16,2560]{1,0:T(8,128)(2,1)S(1)} collective-permute-done((bf16[16,2560]{1,0:T(8,128)(2,1)S(1)}, bf16[16,2560]{1,0:T(8,128)(2,1)S(1)}, u32[]{:S(2)}, u32[]{:S(2)}) %collective-permute-start.23) | collective-permute-done | bytes 81952 | tf_op jit(solution)/shard_map/ppermute | solution.py:552
  230.4 12.7 %all-to-all-done.2 = bf16[32,32,1536]{2,1,0:T(8,128)(2,1)} async-done(((bf16[32,32,1536]{2,1,0:T(8,128)(2,1)}), bf16[32,32,1536]{2,1,0:T(8,128)(2,1)}, u32[]{:S(2)}, u32[]{:S(2)}) %all-to-all-start.2) | async-done | bytes 3145760 | tf_op jit(solution)/shard_map/all_to_all | solution.py:617
  243.2 4.3 %all-to-all-start.3 = ((bf16[32,32,1024]{2,1,0:T(8,128)(2,1)}), bf16[32,32,1024]{2,1,0:T(8,128)(2,1)}, u32[]{:S(2)}, u32[]{:S(2)}) async-start(bf16[32,32,1024]{2,1,0:T(8,128)(2,1)} %bitcast.29), calls=%async_computation.3 | async-start | bytes 4194304 | tf_op jit(solution)/shard_map/all_to_all | solution.py:617
  255.4 29.0 %collective-permute-done.27.refs_12_ = bf16[16,2560]{1,0:T(8,128)(2,1)S(1)} collective-permute-done((bf16[16,2560]{1,0:T(8,128)(2,1)S(1)}, bf16[16,2560]{1,0:T(8,128)(2,1)S(1)}, u32[]{:S(2)}, u32[]{:S(2)}) %collective-permute-start.27) | collective-permute-done | bytes 81952 | tf_op jit(solution)/shard_map/ppermute | solution.py:552
  294.8 5.9 %collective-permute-start.31 = (bf16[384,128]{1,0:T(8,128)(2,1)}, bf16[384,128]{1,0:T(8,128)(2,1)S(1)}, u32[]{:S(2)}, u32[]{:S(2)}) collective-permute-start(bf16[384,128]{1,0:T(8,128)(2,1)} %get-tuple-element.74), channel_id=1, source_target_pairs={{0,2},{1,3},{2,0},{3,1},{4,6},{5,7},{6,4},{7,5},{8,10},{9,11},{10,... | collective-permute-start | bytes 294920 | tf_op jit(solution)/shard_map/ppermute | solution.py:538
  300.7 5.4 %fold.1.folded_ref = bf16[16,256,384]{2,1,0:T(8,128)(2,1)} custom-call(bf16[1024,1536]{1,0:T(8,128)(2,1)} %bitcast.15.arrived_ref), custom_call_target="tpu_custom_call" | custom-call | flops 3145728 | bytes 6291456 | tf_op jit(solution)/shard_map/fold/pallas_call | solution.py:343
  306.1 8.5 %analysis.1.base_ref = f32[20,128,640]{2,1,0:T(8,128)} custom-call(bf16[16,256,384]{2,1,0:T(8,128)(2,1)} %fold.1.folded_ref, f32[20,1,640]{2,1,0:T(1,128)} %get-tuple-element.100.even_ref, f32[20,1,640]{2,1,0:T(1,128)} %get-tuple-element.99.odd_ref, bf16[20,640,640]{2,1,0:T(8,128)(2,1)} %table_ref.7, bf16[20,640,640]{2,1,0:T(8,128)(2,1)} %table_ref.7, ...), custom_call_target="tpu_custom_call" | custom-call | flops 2516582400 | bytes 20316160 | tf_op jit(solution)/shard_map/analysis/pallas_call | solution.py:386
  315.3 6.5 %closing.1 = f32[20,128,640]{2,1,0:T(8,128)} custom-call(s32[1]{0:T(128)} %bitcast.hemi_ref, bf16[1024,1024]{1,0:T(8,128)(2,1)} %bitcast.17.arrived_ref, bf16[20,640,640]{2,1,0:T(8,128)(2,1)} %table_ref.7, f32[20,128,640]{2,1,0:T(8,128)} %analysis.1.base_ref, f32[20,1,640]{2,1,0:T(1,128)} %get-tuple-element.100.even_ref, ...), custom_call_target="tpu_custom_call", output_to_operand_aliasing={{}: (3, {})} | custom-call | flops 1677721600 | bytes 15204352 | tf_op jit(solution)/shard_map/closing/pallas_call | solution.py:510
  (157 shorter events, 81.9 us)
Async XLA Ops:
  2.1 34.4 %collective-permute-start = (bf16[384,768]{1,0:T(8,128)(2,1)}, bf16[384,768]{1,0:T(8,128)(2,1)S(1)}, u32[]{:S(2)}, u32[]{:S(2)}) collective-permute-start(bf16[384,768]{1,0:T(8,128)(2,1)} %pack.1.own_ref), channel_id=1, source_target_pairs={{0,2},{1,3},{2,0},{3,1},{4,6},{5,7},{6,4},{7,5},{8,10},{9,11},{10,... | collective-permute-start | bytes 1769480 | tf_op jit(solution)/shard_map/ppermute | solution.py:538
  37.4 77.0 %all-to-all-start = ((bf16[32,32,1536]{2,1,0:T(8,128)(2,1)}), bf16[32,32,1536]{2,1,0:T(8,128)(2,1)}, u32[]{:S(2)}, u32[]{:S(2)}) async-start(bf16[32,32,1536]{2,1,0:T(8,128)(2,1)} %bitcast.27), calls=%async_computation | async-start | bytes 6291456 | tf_op jit(solution)/shard_map/all_to_all | solution.py:617
  47.5 18.5 %collective-permute-start.2 = (bf16[16,2560]{1,0:T(8,128)(2,1)}, bf16[16,2560]{1,0:T(8,128)(2,1)S(1)}, u32[]{:S(2)}, u32[]{:S(2)}) collective-permute-start(bf16[16,2560]{1,0:T(8,128)(2,1)} %get-tuple-element.44), channel_id=1, source_target_pairs={{0,8},{1,9},{2,10},{3,11},{4,12},{5,13},{6,14},{7,15},{8,0},{9,1},... | collective-permute-start | bytes 245768 | tf_op jit(solution)/shard_map/ppermute | solution.py:552
  49.1 17.7 %collective-permute-start.3 = (bf16[16,2560]{1,0:T(8,128)(2,1)}, bf16[16,2560]{1,0:T(8,128)(2,1)S(1)}, u32[]{:S(2)}, u32[]{:S(2)}) collective-permute-start(bf16[16,2560]{1,0:T(8,128)(2,1)} %get-tuple-element.45), channel_id=1, source_target_pairs={{0,12},{1,13},{2,14},{3,15},{4,8},{5,9},{6,10},{7,11},{8,4},{9,5},... | collective-permute-start | bytes 245768 | tf_op jit(solution)/shard_map/ppermute | solution.py:552
  49.3 18.0 %collective-permute-start.4 = (bf16[16,2560]{1,0:T(8,128)(2,1)}, bf16[16,2560]{1,0:T(8,128)(2,1)S(1)}, u32[]{:S(2)}, u32[]{:S(2)}) collective-permute-start(bf16[16,2560]{1,0:T(8,128)(2,1)} %get-tuple-element.46), channel_id=1, source_target_pairs={{0,16},{1,17},{2,18},{3,19},{4,20},{5,21},{6,22},{7,23},{8,24},{9,... | collective-permute-start | bytes 245768 | tf_op jit(solution)/shard_map/ppermute | solution.py:552
  50.8 18.8 %collective-permute-start.5 = (bf16[16,2560]{1,0:T(8,128)(2,1)}, bf16[16,2560]{1,0:T(8,128)(2,1)S(1)}, u32[]{:S(2)}, u32[]{:S(2)}) collective-permute-start(bf16[16,2560]{1,0:T(8,128)(2,1)} %get-tuple-element.47), channel_id=1, source_target_pairs={{0,20},{1,21},{2,22},{3,23},{4,16},{5,17},{6,18},{7,19},{8,28},{9,... | collective-permute-start | bytes 245768 | tf_op jit(solution)/shard_map/ppermute | solution.py:552
  51.0 24.4 %collective-permute-start.6 = (bf16[16,2560]{1,0:T(8,128)(2,1)}, bf16[16,2560]{1,0:T(8,128)(2,1)S(1)}, u32[]{:S(2)}, u32[]{:S(2)}) collective-permute-start(bf16[16,2560]{1,0:T(8,128)(2,1)} %get-tuple-element.48), channel_id=1, source_target_pairs={{0,24},{1,25},{2,26},{3,27},{4,28},{5,29},{6,30},{7,31},{8,16},{9,... | collective-permute-start | bytes 245768 | tf_op jit(solution)/shard_map/ppermute | solution.py:552
  66.9 28.7 %collective-permute-start.8 = (bf16[16,2560]{1,0:T(8,128)(2,1)}, bf16[16,2560]{1,0:T(8,128)(2,1)S(1)}, u32[]{:S(2)}, u32[]{:S(2)}) collective-permute-start(bf16[16,2560]{1,0:T(8,128)(2,1)} %get-tuple-element.50), channel_id=1, source_target_pairs={{0,1},{1,0},{2,3},{3,2},{4,5},{5,4},{6,7},{7,6},{8,9},{9,8},{10,11... | collective-permute-start | bytes 245768 | tf_op jit(solution)/shard_map/ppermute | solution.py:552
  67.3 30.1 %collective-permute-start.9 = (bf16[16,2560]{1,0:T(8,128)(2,1)}, bf16[16,2560]{1,0:T(8,128)(2,1)S(1)}, u32[]{:S(2)}, u32[]{:S(2)}) collective-permute-start(bf16[16,2560]{1,0:T(8,128)(2,1)} %get-tuple-element.51), channel_id=1, source_target_pairs={{0,5},{1,4},{2,7},{3,6},{4,1},{5,0},{6,3},{7,2},{8,13},{9,12},{10,... | collective-permute-start | bytes 245768 | tf_op jit(solution)/shard_map/ppermute | solution.py:552
  69.6 31.1 %collective-permute-start.10 = (bf16[16,2560]{1,0:T(8,128)(2,1)}, bf16[16,2560]{1,0:T(8,128)(2,1)S(1)}, u32[]{:S(2)}, u32[]{:S(2)}) collective-permute-start(bf16[16,2560]{1,0:T(8,128)(2,1)} %get-tuple-element.52), channel_id=1, source_target_pairs={{0,9},{1,8},{2,11},{3,10},{4,13},{5,12},{6,15},{7,14},{8,1},{9,0},... | collective-permute-start | bytes 245768 | tf_op jit(solution)/shard_map/ppermute | solution.py:552
  75.4 26.6 %collective-permute-start.11 = (bf16[16,2560]{1,0:T(8,128)(2,1)}, bf16[16,2560]{1,0:T(8,128)(2,1)S(1)}, u32[]{:S(2)}, u32[]{:S(2)}) collective-permute-start(bf16[16,2560]{1,0:T(8,128)(2,1)} %get-tuple-element.53), channel_id=1, source_target_pairs={{0,13},{1,12},{2,15},{3,14},{4,9},{5,8},{6,11},{7,10},{8,5},{9,4},... | collective-permute-start | bytes 245768 | tf_op jit(solution)/shard_map/ppermute | solution.py:552
  79.1 23.5 %collective-permute-start.12 = (bf16[16,2560]{1,0:T(8,128)(2,1)}, bf16[16,2560]{1,0:T(8,128)(2,1)S(1)}, u32[]{:S(2)}, u32[]{:S(2)}) collective-permute-start(bf16[16,2560]{1,0:T(8,128)(2,1)} %get-tuple-element.54), channel_id=1, source_target_pairs={{0,17},{1,16},{2,19},{3,18},{4,21},{5,20},{6,23},{7,22},{8,25},{9,... | collective-permute-start | bytes 245768 | tf_op jit(solution)/shard_map/ppermute | solution.py:552
  114.4 53.0 %all-to-all-start.1 = ((bf16[32,32,1024]{2,1,0:T(8,128)(2,1)}), bf16[32,32,1024]{2,1,0:T(8,128)(2,1)}, u32[]{:S(2)}, u32[]{:S(2)}) async-start(bf16[32,32,1024]{2,1,0:T(8,128)(2,1)} %bitcast.12), calls=%async_computation.1 | async-start | bytes 4194304 | tf_op jit(solution)/shard_map/all_to_all | solution.py:617
  167.4 75.6 %all-to-all-start.2 = ((bf16[32,32,1536]{2,1,0:T(8,128)(2,1)}), bf16[32,32,1536]{2,1,0:T(8,128)(2,1)}, u32[]{:S(2)}, u32[]{:S(2)}) async-start(bf16[32,32,1536]{2,1,0:T(8,128)(2,1)} %bitcast.28), calls=%async_computation.2 | async-start | bytes 6291456 | tf_op jit(solution)/shard_map/all_to_all | solution.py:617
  207.7 17.7 %collective-permute-start.23 = (bf16[16,2560]{1,0:T(8,128)(2,1)S(1)}, bf16[16,2560]{1,0:T(8,128)(2,1)S(1)}, u32[]{:S(2)}, u32[]{:S(2)}) collective-permute-start(bf16[16,2560]{1,0:T(8,128)(2,1)S(1)} %get-tuple-element.84), channel_id=1, source_target_pairs={{0,1},{1,0},{2,3},{3,2},{4,5},{5,4},{6,7},{7,6},{8,9},{9,8},{10,11... | collective-permute-start | bytes 245768 | tf_op jit(solution)/shard_map/ppermute | solution.py:552
  207.7 19.5 %collective-permute-start.24 = (bf16[16,2560]{1,0:T(8,128)(2,1)S(1)}, bf16[16,2560]{1,0:T(8,128)(2,1)S(1)}, u32[]{:S(2)}, u32[]{:S(2)}) collective-permute-start(bf16[16,2560]{1,0:T(8,128)(2,1)S(1)} %get-tuple-element.83), channel_id=1, source_target_pairs={{0,5},{1,4},{2,7},{3,6},{4,1},{5,0},{6,3},{7,2},{8,13},{9,12},{10,... | collective-permute-start | bytes 245768 | tf_op jit(solution)/shard_map/ppermute | solution.py:552
  209.3 19.6 %collective-permute-start.25 = (bf16[16,2560]{1,0:T(8,128)(2,1)S(1)}, bf16[16,2560]{1,0:T(8,128)(2,1)S(1)}, u32[]{:S(2)}, u32[]{:S(2)}) collective-permute-start(bf16[16,2560]{1,0:T(8,128)(2,1)S(1)} %get-tuple-element.82), channel_id=1, source_target_pairs={{0,9},{1,8},{2,11},{3,10},{4,13},{5,12},{6,15},{7,14},{8,1},{9,0},... | collective-permute-start | bytes 245768 | tf_op jit(solution)/shard_map/ppermute | solution.py:552
  214.0 16.4 %collective-permute-start.26 = (bf16[16,2560]{1,0:T(8,128)(2,1)S(1)}, bf16[16,2560]{1,0:T(8,128)(2,1)S(1)}, u32[]{:S(2)}, u32[]{:S(2)}) collective-permute-start(bf16[16,2560]{1,0:T(8,128)(2,1)S(1)} %get-tuple-element.81), channel_id=1, source_target_pairs={{0,13},{1,12},{2,15},{3,14},{4,9},{5,8},{6,11},{7,10},{8,5},{9,4},... | collective-permute-start | bytes 245768 | tf_op jit(solution)/shard_map/ppermute | solution.py:552
  243.2 71.5 %all-to-all-start.3 = ((bf16[32,32,1024]{2,1,0:T(8,128)(2,1)}), bf16[32,32,1024]{2,1,0:T(8,128)(2,1)}, u32[]{:S(2)}, u32[]{:S(2)}) async-start(bf16[32,32,1024]{2,1,0:T(8,128)(2,1)} %bitcast.29), calls=%async_computation.3 | async-start | bytes 4194304 | tf_op jit(solution)/shard_map/all_to_all | solution.py:617
  248.2 36.2 %collective-permute-start.27 = (bf16[16,2560]{1,0:T(8,128)(2,1)S(1)}, bf16[16,2560]{1,0:T(8,128)(2,1)S(1)}, u32[]{:S(2)}, u32[]{:S(2)}) collective-permute-start(bf16[16,2560]{1,0:T(8,128)(2,1)S(1)} %get-tuple-element.80), channel_id=1, source_target_pairs={{0,17},{1,16},{2,19},{3,18},{4,21},{5,20},{6,23},{7,22},{8,25},{9,... | collective-permute-start | bytes 245768 | tf_op jit(solution)/shard_map/ppermute | solution.py:552
  250.6 35.6 %collective-permute-start.28 = (bf16[16,2560]{1,0:T(8,128)(2,1)S(1)}, bf16[16,2560]{1,0:T(8,128)(2,1)S(1)}, u32[]{:S(2)}, u32[]{:S(2)}) collective-permute-start(bf16[16,2560]{1,0:T(8,128)(2,1)S(1)} %get-tuple-element.79), channel_id=1, source_target_pairs={{0,21},{1,20},{2,23},{3,22},{4,17},{5,16},{6,19},{7,18},{8,29},{9,... | collective-permute-start | bytes 245768 | tf_op jit(solution)/shard_map/ppermute | solution.py:552
  250.6 37.8 %collective-permute-start.29 = (bf16[16,2560]{1,0:T(8,128)(2,1)S(1)}, bf16[16,2560]{1,0:T(8,128)(2,1)S(1)}, u32[]{:S(2)}, u32[]{:S(2)}) collective-permute-start(bf16[16,2560]{1,0:T(8,128)(2,1)S(1)} %get-tuple-element.78), channel_id=1, source_target_pairs={{0,25},{1,24},{2,27},{3,26},{4,29},{5,28},{6,31},{7,30},{8,17},{9,... | collective-permute-start | bytes 245768 | tf_op jit(solution)/shard_map/ppermute | solution.py:552
  253.9 36.8 %collective-permute-start.30 = (bf16[16,2560]{1,0:T(8,128)(2,1)S(1)}, bf16[16,2560]{1,0:T(8,128)(2,1)S(1)}, u32[]{:S(2)}, u32[]{:S(2)}) collective-permute-start(bf16[16,2560]{1,0:T(8,128)(2,1)S(1)} %get-tuple-element.77), channel_id=1, source_target_pairs={{0,29},{1,28},{2,31},{3,30},{4,25},{5,24},{6,27},{7,26},{8,21},{9,... | collective-permute-start | bytes 245768 | tf_op jit(solution)/shard_map/ppermute | solution.py:552
  294.8 19.8 %collective-permute-start.31 = (bf16[384,128]{1,0:T(8,128)(2,1)}, bf16[384,128]{1,0:T(8,128)(2,1)S(1)}, u32[]{:S(2)}, u32[]{:S(2)}) collective-permute-start(bf16[384,128]{1,0:T(8,128)(2,1)} %get-tuple-element.74), channel_id=1, source_target_pairs={{0,2},{1,3},{2,0},{3,1},{4,6},{5,7},{6,4},{7,5},{8,10},{9,11},{10,... | collective-permute-start | bytes 294920 | tf_op jit(solution)/shard_map/ppermute | solution.py:538
  (36 other events, 608.4 us)

commit v6 on v5

--- a/solution.py
+++ b/solution.py
@@ -653,8 +653,8 @@
     waves = jnp.concatenate([by_device[:, :, :near].reshape(-1), far_waves.reshape(-1)])
 
     small = send(after(spec_rows, large), chunks[1])
-    by_wave, by_lon = trig_tables(after(waves, own_pack), lon_count, large)
-    arrived = [exchange(after(large, small, by_wave, partner_pack))]
+    by_wave, by_lon = trig_tables(after(waves, large), lon_count, small)
+    arrived = [exchange(after(large, small, partner_pack))]
     far_rows = far_synthesize(
         place, far_waves[0] - far_least, own_pack, partner_pack, levels, fields, 1.0 / math.sqrt(degrees)
     )
@@ -666,7 +666,7 @@
     returned = [exchange(zonal[0][0])]
     far_zonal = jnp.concatenate([zonal[0][1], zonal[1][1]], axis=1)
     far_zonal = within_half([far_zonal[16 * x : 16 * x + 16] for x in range(levels)])
-    returned.append(exchange(after(zonal[1][0], *far_zonal[: levels - 4], *returned)))
+    returned.append(exchange(after(zonal[1][0], *far_zonal, *returned)))
     own_sums, partner_sums = far_analyze(place, own_pack, partner_pack, far_zonal, levels, fields, chunks)
     other_sums = across_halves(partner_sums)
     wavenumber = lax.dynamic_slice_in_dim(after(owner_table, by_wave), first, slots)

time: 323 us -> 308 us (0.954)
  waiting for transfers between devices: 132 us -> 115 us
    ppermute x30, waiting for transfers between devices: 98.7 us -> 64.8 us  [within_half(): moved.append(lax.ppermute(parts[x], AXES, pairs))]
    ppermute x2, waiting for transfers between devices: 0.01 us -> 13.4 us  [across_halves(): lax.ppermute(value, 'grp', [(p, (p + planes // 2) % planes) for p in rang...]
    ppermute x30, starting transfers between devices: 41.4 us -> 45.9 us  [within_half(): moved.append(lax.ppermute(parts[x], AXES, pairs))]
    ppermute x2, starting transfers between devices: 10 us -> 6.43 us  [across_halves(): lax.ppermute(value, 'grp', [(p, (p + planes // 2) % planes) for p in rang...]
  transfers between devices with their start and end apart: 36 -> 36, of which waited for: 22 -> 23; matrix products, arithmetic and copies ran while one was open for 4% -> 4% of each run, Pallas kernels for 30% -> 32%
where the time goes in v6:
time: 308 us; the launch traced here: 307 us
  waiting for transfers between devices  115 us (37%)
  Pallas kernels  105 us (34%)
  starting transfers between devices  70.9 us (23%)
  local copies, waits for them, and re-layouts  8.68 us (3%)
  other arithmetic  6.48 us (2%)
    ppermute x30, waiting for transfers between devices, within_half(): moved.append(lax.ppermute(parts[x], AXES, pairs))  64.8 us
    pallas_call x2, Pallas kernels, longitudes(): pl.pallas_call(functools.partial(longitude_kernel, fields, chunk, 1.0 / m...  53.2 us
    ppermute x30, starting transfers between devices, within_half(): moved.append(lax.ppermute(parts[x], AXES, pairs))  45.9 us
    all_to_all x4, waiting for transfers between devices, exchange(): lax.all_to_all(rows, AXES[::-1], split_axis=0, concat_axis=0, tiled=True)  36.7 us
    all_to_all x4, starting transfers between devices, exchange(): lax.all_to_all(rows, AXES[::-1], split_axis=0, concat_axis=0, tiled=True)  18.6 us
    pallas_call x2, Pallas kernels, synthesize(): pl.pallas_call(functools.partial(synthesis_kernel, slots, levels, fields,...  13.4 us
    ppermute x2, waiting for transfers between devices, across_halves(): lax.ppermute(value, 'grp', [(p, (p + planes // 2) % planes) for p in rang...  13.4 us
    pallas_call x1, Pallas kernels, trig_tables(): pl.pallas_call(trig_kernel, grid=(depth // rows,), in_specs=[pl.BlockSpec...  9.01 us
  transfers between devices with their start and end apart: 36, of which 23 were waited for; matrix products, arithmetic and copies ran while one was open for 4% of the time, Pallas kernels for 32%

profile of v6, /device:TPU:0, one launch (start us, length us, event | category | flops | bytes accessed | tf_op | source)
XLA Modules:
  0.0 306.9 jit_solution(15109765782799942947)
XLA Ops:
  2.1 4.1 %collective-permute-start = (bf16[384,768]{1,0:T(8,128)(2,1)}, bf16[384,768]{1,0:T(8,128)(2,1)S(1)}, u32[]{:S(2)}, u32[]{:S(2)}) collective-permute-start(bf16[384,768]{1,0:T(8,128)(2,1)} %pack.1.own_ref), channel_id=1, source_target_pairs={{0,2},{1,3},{2,0},{3,1},{4,6},{5,7},{6,4},{7,5},{8,10},{9,11},{10,... | collective-permute-start | bytes 1769480 | tf_op jit(solution)/shard_map/ppermute | solution.py:538
  6.2 7.5 %synthesis.2 = bf16[1024,1536]{1,0:T(8,128)(2,1)} custom-call(s32[1]{0:T(128)} %bitcast.1.first_ref, s32[640]{0:T(1024)} %owner_ref.3, bf16[20,128,640]{2,1,0:T(8,128)(2,1)} %bitcast.25, bf16[20,640,640]{2,1,0:T(8,128)(2,1)} %table_ref.7), custom_call_target="tpu_custom_call" | custom-call | flops 2013265920 | bytes 13631488 | tf_op jit(solution)/shard_map/synthesis/pallas_call | solution.py:81
  14.6 5.9 %synthesis.3 = bf16[1024,1024]{1,0:T(8,128)(2,1)} custom-call(s32[1]{0:T(128)} %bitcast.1.first_ref, s32[640]{0:T(1024)} %owner_ref.3, bf16[20,128,640]{2,1,0:T(8,128)(2,1)} %bitcast.26, bf16[20,640,640]{2,1,0:T(8,128)(2,1)} %table_ref.7), custom_call_target="tpu_custom_call" | custom-call | flops 1342177280 | bytes 9961472 | tf_op jit(solution)/shard_map/synthesis/pallas_call | solution.py:81
  20.6 11.8 %collective-permute-done.partner_ref = bf16[384,768]{1,0:T(8,128)(2,1)S(1)} collective-permute-done((bf16[384,768]{1,0:T(8,128)(2,1)}, bf16[384,768]{1,0:T(8,128)(2,1)S(1)}, u32[]{:S(2)}, u32[]{:S(2)}) %collective-permute-start) | collective-permute-done | bytes 589856 | tf_op jit(solution)/shard_map/ppermute | solution.py:538
  33.2 5.9 %all-to-all-start = ((bf16[32,32,1536]{2,1,0:T(8,128)(2,1)}), bf16[32,32,1536]{2,1,0:T(8,128)(2,1)}, u32[]{:S(2)}, u32[]{:S(2)}) async-start(bf16[32,32,1536]{2,1,0:T(8,128)(2,1)} %bitcast.27), calls=%async_computation | async-start | bytes 6291456 | tf_op jit(solution)/shard_map/all_to_all | solution.py:617
  51.4 12.4 %collective-permute-done.2 = bf16[16,2560]{1,0:T(8,128)(2,1)S(1)} collective-permute-done((bf16[16,2560]{1,0:T(8,128)(2,1)}, bf16[16,2560]{1,0:T(8,128)(2,1)S(1)}, u32[]{:S(2)}, u32[]{:S(2)}) %collective-permute-start.2) | collective-permute-done | bytes 81952 | tf_op jit(solution)/shard_map/ppermute | solution.py:552
  68.6 4.6 %collective-permute-done.6 = bf16[16,2560]{1,0:T(8,128)(2,1)S(1)} collective-permute-done((bf16[16,2560]{1,0:T(8,128)(2,1)}, bf16[16,2560]{1,0:T(8,128)(2,1)S(1)}, u32[]{:S(2)}, u32[]{:S(2)}) %collective-permute-start.6) | collective-permute-done | bytes 81952 | tf_op jit(solution)/shard_map/ppermute | solution.py:552
  76.9 16.5 %collective-permute-done.8 = bf16[16,2560]{1,0:T(8,128)(2,1)S(1)} collective-permute-done((bf16[16,2560]{1,0:T(8,128)(2,1)}, bf16[16,2560]{1,0:T(8,128)(2,1)S(1)}, u32[]{:S(2)}, u32[]{:S(2)}) %collective-permute-start.8) | collective-permute-done | bytes 81952 | tf_op jit(solution)/shard_map/ppermute | solution.py:552
  102.1 4.1 %collective-permute-done.14 = bf16[16,2560]{1,0:T(8,128)(2,1)S(1)} collective-permute-done((bf16[16,2560]{1,0:T(8,128)(2,1)S(1)}, bf16[16,2560]{1,0:T(8,128)(2,1)S(1)}, u32[]{:S(2)}, u32[]{:S(2)}) %collective-permute-start.14) | collective-permute-done | bytes 81952 | tf_op jit(solution)/shard_map/ppermute | solution.py:552
  111.9 4.6 %all-to-all-start.1 = ((bf16[32,32,1024]{2,1,0:T(8,128)(2,1)}), bf16[32,32,1024]{2,1,0:T(8,128)(2,1)}, u32[]{:S(2)}, u32[]{:S(2)}) async-start(bf16[32,32,1024]{2,1,0:T(8,128)(2,1)} %bitcast.12), calls=%async_computation.1 | async-start | bytes 4194304 | tf_op jit(solution)/shard_map/all_to_all | solution.py:617
  118.5 3.8 %fusion = (f32[1280,128]{1,0:T(8,128)}, f32[1280,128]{1,0:T(8,128)}) fusion(f32[1280]{0:T(1024)S(1)} %convert_element_type.24), kind=kLoop, calls=%fused_computation.2 | loop fusion | flops 983040 | bytes 1315840 | tf_op jit(solution)/shard_map/sin | solution.py:592
  123.5 9.0 %trig.1 = (bf16[1280,2560]{1,0:T(8,128)(2,1)}, bf16[2560,1280]{1,0:T(8,128)(2,1)}) custom-call(f32[1280,4]{1,0:T(8,128)} %copy.38.small_ref, f32[1280,128]{1,0:T(8,128)} %get-tuple-element.62.cos_turn_ref, f32[1280,128]{1,0:T(8,128)} %get-tuple-element.63.sin_turn_ref), custom_call_target="tpu_custom_call" | custom-call | flops 39321600 | bytes 13107200 | tf_op jit(solution)/shard_map/trig/pallas_call | solution.py:596
  132.5 31.1 %longitudes.3 = (bf16[1024,1536]{1,0:T(8,128)(2,1)}, bf16[256,1536]{1,0:T(8,128)(2,1)}) custom-call(bf16[1024,1536]{1,0:T(8,128)(2,1)} %bitcast.11.rows_ref, bf16[256,2560]{1,0:T(8,128)(2,1)} %copy-done.19, bf16[2560,1280]{1,0:T(8,128)(2,1)} %get-tuple-element.64.by_lon_ref, bf16[1280,2560]{1,0:T(8,128)(2,1)} %get-tuple-element.65.by_wave_ref), custom_call_target="tpu_custom_call" | custom-call | flops 20132659200 | bytes 20971520 | tf_op jit(solution)/shard_map/longitudes/pallas_call | solution.py:137
  165.3 4.3 %all-to-all-start.2 = ((bf16[32,32,1536]{2,1,0:T(8,128)(2,1)}), bf16[32,32,1536]{2,1,0:T(8,128)(2,1)}, u32[]{:S(2)}, u32[]{:S(2)}) async-start(bf16[32,32,1536]{2,1,0:T(8,128)(2,1)} %bitcast.28), calls=%async_computation.2 | async-start | bytes 6291456 | tf_op jit(solution)/shard_map/all_to_all | solution.py:617
  169.7 22.1 %longitudes.2 = (bf16[1024,1024]{1,0:T(8,128)(2,1)}, bf16[256,1024]{1,0:T(8,128)(2,1)}) custom-call(bf16[1024,1024]{1,0:T(8,128)(2,1)} %bitcast.13.rows_ref, bf16[256,2560]{1,0:T(8,128)(2,1)} %copy-done.19, bf16[2560,1280]{1,0:T(8,128)(2,1)} %get-tuple-element.64.by_lon_ref, bf16[1280,2560]{1,0:T(8,128)(2,1)} %get-tuple-element.65.by_wave_ref), custom_call_target="tpu_custom_call" | custom-call | flops 13421772800 | bytes 18350080 | tf_op jit(solution)/shard_map/longitudes/pallas_call | solution.py:137
  199.6 5.4 %collective-permute-start.22 = (bf16[16,2560]{1,0:T(8,128)(2,1)S(1)}, bf16[16,2560]{1,0:T(8,128)(2,1)S(1)}, u32[]{:S(2)}, u32[]{:S(2)}) collective-permute-start(bf16[16,2560]{1,0:T(8,128)(2,1)S(1)} %get-tuple-element.85), channel_id=1, source_target_pairs={{0,28},{1,29},{2,30},{3,31},{4,24},{5,25},{6,26},{7,27},{8,20},{9,... | collective-permute-start | bytes 245768 | tf_op jit(solution)/shard_map/ppermute | solution.py:552
  207.2 4.6 %collective-permute-start.25 = (bf16[16,2560]{1,0:T(8,128)(2,1)S(1)}, bf16[16,2560]{1,0:T(8,128)(2,1)S(1)}, u32[]{:S(2)}, u32[]{:S(2)}) collective-permute-start(bf16[16,2560]{1,0:T(8,128)(2,1)S(1)} %get-tuple-element.82), channel_id=1, source_target_pairs={{0,9},{1,8},{2,11},{3,10},{4,13},{5,12},{6,15},{7,14},{8,1},{9,0},... | collective-permute-start | bytes 245768 | tf_op jit(solution)/shard_map/ppermute | solution.py:552
  213.4 4.4 %collective-permute-start.27 = (bf16[16,2560]{1,0:T(8,128)(2,1)S(1)}, bf16[16,2560]{1,0:T(8,128)(2,1)S(1)}, u32[]{:S(2)}, u32[]{:S(2)}) collective-permute-start(bf16[16,2560]{1,0:T(8,128)(2,1)S(1)} %get-tuple-element.80), channel_id=1, source_target_pairs={{0,17},{1,16},{2,19},{3,18},{4,21},{5,20},{6,23},{7,22},{8,25},{9,... | collective-permute-start | bytes 245768 | tf_op jit(solution)/shard_map/ppermute | solution.py:552
  217.7 5.6 %collective-permute-done.23.refs_8_ = bf16[16,2560]{1,0:T(8,128)(2,1)S(1)} collective-permute-done((bf16[16,2560]{1,0:T(8,128)(2,1)S(1)}, bf16[16,2560]{1,0:T(8,128)(2,1)S(1)}, u32[]{:S(2)}, u32[]{:S(2)}) %collective-permute-start.23) | collective-permute-done | bytes 81952 | tf_op jit(solution)/shard_map/ppermute | solution.py:552
  232.1 4.6 %collective-permute-done.29.refs_14_ = bf16[16,2560]{1,0:T(8,128)(2,1)S(1)} collective-permute-done((bf16[16,2560]{1,0:T(8,128)(2,1)S(1)}, bf16[16,2560]{1,0:T(8,128)(2,1)S(1)}, u32[]{:S(2)}, u32[]{:S(2)}) %collective-permute-start.29) | collective-permute-done | bytes 81952 | tf_op jit(solution)/shard_map/ppermute | solution.py:552
  254.2 5.4 %fold.1.folded_ref = bf16[16,256,384]{2,1,0:T(8,128)(2,1)} custom-call(bf16[1024,1536]{1,0:T(8,128)(2,1)} %bitcast.15.arrived_ref), custom_call_target="tpu_custom_call" | custom-call | flops 3145728 | bytes 6291456 | tf_op jit(solution)/shard_map/fold/pallas_call | solution.py:343
  259.5 8.5 %analysis.1.base_ref = f32[20,128,640]{2,1,0:T(8,128)} custom-call(bf16[16,256,384]{2,1,0:T(8,128)(2,1)} %fold.1.folded_ref, f32[20,1,640]{2,1,0:T(1,128)} %get-tuple-element.100.even_ref, f32[20,1,640]{2,1,0:T(1,128)} %get-tuple-element.99.odd_ref, bf16[20,640,640]{2,1,0:T(8,128)(2,1)} %table_ref.7, bf16[20,640,640]{2,1,0:T(8,128)(2,1)} %table_ref.7, ...), custom_call_target="tpu_custom_call" | custom-call | flops 2516582400 | bytes 20316160 | tf_op jit(solution)/shard_map/analysis/pallas_call | solution.py:386
  268.1 29.9 %all-to-all-done.3 = bf16[32,32,1024]{2,1,0:T(8,128)(2,1)} async-done(((bf16[32,32,1024]{2,1,0:T(8,128)(2,1)}), bf16[32,32,1024]{2,1,0:T(8,128)(2,1)}, u32[]{:S(2)}, u32[]{:S(2)}) %all-to-all-start.3) | async-done | bytes 2097184 | tf_op jit(solution)/shard_map/all_to_all | solution.py:617
  300.2 6.5 %closing.1 = f32[20,128,640]{2,1,0:T(8,128)} custom-call(s32[1]{0:T(128)} %bitcast.hemi_ref, bf16[1024,1024]{1,0:T(8,128)(2,1)} %bitcast.17.arrived_ref, bf16[20,640,640]{2,1,0:T(8,128)(2,1)} %table_ref.7, f32[20,128,640]{2,1,0:T(8,128)} %analysis.1.base_ref, f32[20,1,640]{2,1,0:T(1,128)} %get-tuple-element.100.even_ref, ...), custom_call_target="tpu_custom_call", output_to_operand_aliasing={{}: (3, {})} | custom-call | flops 1677721600 | bytes 15204352 | tf_op jit(solution)/shard_map/closing/pallas_call | solution.py:510
  (157 shorter events, 83.6 us)
Async XLA Ops:
  2.1 30.3 %collective-permute-start = (bf16[384,768]{1,0:T(8,128)(2,1)}, bf16[384,768]{1,0:T(8,128)(2,1)S(1)}, u32[]{:S(2)}, u32[]{:S(2)}) collective-permute-start(bf16[384,768]{1,0:T(8,128)(2,1)} %pack.1.own_ref), channel_id=1, source_target_pairs={{0,2},{1,3},{2,0},{3,1},{4,6},{5,7},{6,4},{7,5},{8,10},{9,11},{10,... | collective-permute-start | bytes 1769480 | tf_op jit(solution)/shard_map/ppermute | solution.py:538
  33.2 78.7 %all-to-all-start = ((bf16[32,32,1536]{2,1,0:T(8,128)(2,1)}), bf16[32,32,1536]{2,1,0:T(8,128)(2,1)}, u32[]{:S(2)}, u32[]{:S(2)}) async-start(bf16[32,32,1536]{2,1,0:T(8,128)(2,1)} %bitcast.27), calls=%async_computation | async-start | bytes 6291456 | tf_op jit(solution)/shard_map/all_to_all | solution.py:617
  45.3 18.5 %collective-permute-start.2 = (bf16[16,2560]{1,0:T(8,128)(2,1)}, bf16[16,2560]{1,0:T(8,128)(2,1)S(1)}, u32[]{:S(2)}, u32[]{:S(2)}) collective-permute-start(bf16[16,2560]{1,0:T(8,128)(2,1)} %get-tuple-element.44), channel_id=1, source_target_pairs={{0,8},{1,9},{2,10},{3,11},{4,12},{5,13},{6,14},{7,15},{8,0},{9,1},... | collective-permute-start | bytes 245768 | tf_op jit(solution)/shard_map/ppermute | solution.py:552
  46.9 17.7 %collective-permute-start.3 = (bf16[16,2560]{1,0:T(8,128)(2,1)}, bf16[16,2560]{1,0:T(8,128)(2,1)S(1)}, u32[]{:S(2)}, u32[]{:S(2)}) collective-permute-start(bf16[16,2560]{1,0:T(8,128)(2,1)} %get-tuple-element.45), channel_id=1, source_target_pairs={{0,12},{1,13},{2,14},{3,15},{4,8},{5,9},{6,10},{7,11},{8,4},{9,5},... | collective-permute-start | bytes 245768 | tf_op jit(solution)/shard_map/ppermute | solution.py:552
  47.0 18.1 %collective-permute-start.4 = (bf16[16,2560]{1,0:T(8,128)(2,1)}, bf16[16,2560]{1,0:T(8,128)(2,1)S(1)}, u32[]{:S(2)}, u32[]{:S(2)}) collective-permute-start(bf16[16,2560]{1,0:T(8,128)(2,1)} %get-tuple-element.46), channel_id=1, source_target_pairs={{0,16},{1,17},{2,18},{3,19},{4,20},{5,21},{6,22},{7,23},{8,24},{9,... | collective-permute-start | bytes 245768 | tf_op jit(solution)/shard_map/ppermute | solution.py:552
  48.6 18.7 %collective-permute-start.5 = (bf16[16,2560]{1,0:T(8,128)(2,1)}, bf16[16,2560]{1,0:T(8,128)(2,1)S(1)}, u32[]{:S(2)}, u32[]{:S(2)}) collective-permute-start(bf16[16,2560]{1,0:T(8,128)(2,1)} %get-tuple-element.47), channel_id=1, source_target_pairs={{0,20},{1,21},{2,22},{3,23},{4,16},{5,17},{6,18},{7,19},{8,28},{9,... | collective-permute-start | bytes 245768 | tf_op jit(solution)/shard_map/ppermute | solution.py:552
  48.8 24.4 %collective-permute-start.6 = (bf16[16,2560]{1,0:T(8,128)(2,1)}, bf16[16,2560]{1,0:T(8,128)(2,1)S(1)}, u32[]{:S(2)}, u32[]{:S(2)}) collective-permute-start(bf16[16,2560]{1,0:T(8,128)(2,1)} %get-tuple-element.48), channel_id=1, source_target_pairs={{0,24},{1,25},{2,26},{3,27},{4,28},{5,29},{6,30},{7,31},{8,16},{9,... | collective-permute-start | bytes 245768 | tf_op jit(solution)/shard_map/ppermute | solution.py:552
  63.8 13.1 %collective-permute-start.7 = (bf16[16,2560]{1,0:T(8,128)(2,1)}, bf16[16,2560]{1,0:T(8,128)(2,1)S(1)}, u32[]{:S(2)}, u32[]{:S(2)}) collective-permute-start(bf16[16,2560]{1,0:T(8,128)(2,1)} %get-tuple-element.49), channel_id=1, source_target_pairs={{0,28},{1,29},{2,30},{3,31},{4,24},{5,25},{6,26},{7,27},{8,20},{9,... | collective-permute-start | bytes 245768 | tf_op jit(solution)/shard_map/ppermute | solution.py:552
  64.7 28.7 %collective-permute-start.8 = (bf16[16,2560]{1,0:T(8,128)(2,1)}, bf16[16,2560]{1,0:T(8,128)(2,1)S(1)}, u32[]{:S(2)}, u32[]{:S(2)}) collective-permute-start(bf16[16,2560]{1,0:T(8,128)(2,1)} %get-tuple-element.50), channel_id=1, source_target_pairs={{0,1},{1,0},{2,3},{3,2},{4,5},{5,4},{6,7},{7,6},{8,9},{9,8},{10,11... | collective-permute-start | bytes 245768 | tf_op jit(solution)/shard_map/ppermute | solution.py:552
  65.1 30.1 %collective-permute-start.9 = (bf16[16,2560]{1,0:T(8,128)(2,1)}, bf16[16,2560]{1,0:T(8,128)(2,1)S(1)}, u32[]{:S(2)}, u32[]{:S(2)}) collective-permute-start(bf16[16,2560]{1,0:T(8,128)(2,1)} %get-tuple-element.51), channel_id=1, source_target_pairs={{0,5},{1,4},{2,7},{3,6},{4,1},{5,0},{6,3},{7,2},{8,13},{9,12},{10,... | collective-permute-start | bytes 245768 | tf_op jit(solution)/shard_map/ppermute | solution.py:552
  67.4 31.1 %collective-permute-start.10 = (bf16[16,2560]{1,0:T(8,128)(2,1)}, bf16[16,2560]{1,0:T(8,128)(2,1)S(1)}, u32[]{:S(2)}, u32[]{:S(2)}) collective-permute-start(bf16[16,2560]{1,0:T(8,128)(2,1)} %get-tuple-element.52), channel_id=1, source_target_pairs={{0,9},{1,8},{2,11},{3,10},{4,13},{5,12},{6,15},{7,14},{8,1},{9,0},... | collective-permute-start | bytes 245768 | tf_op jit(solution)/shard_map/ppermute | solution.py:552
  73.2 26.6 %collective-permute-start.11 = (bf16[16,2560]{1,0:T(8,128)(2,1)}, bf16[16,2560]{1,0:T(8,128)(2,1)S(1)}, u32[]{:S(2)}, u32[]{:S(2)}) collective-permute-start(bf16[16,2560]{1,0:T(8,128)(2,1)} %get-tuple-element.53), channel_id=1, source_target_pairs={{0,13},{1,12},{2,15},{3,14},{4,9},{5,8},{6,11},{7,10},{8,5},{9,4},... | collective-permute-start | bytes 245768 | tf_op jit(solution)/shard_map/ppermute | solution.py:552
  76.9 23.5 %collective-permute-start.12 = (bf16[16,2560]{1,0:T(8,128)(2,1)}, bf16[16,2560]{1,0:T(8,128)(2,1)S(1)}, u32[]{:S(2)}, u32[]{:S(2)}) collective-permute-start(bf16[16,2560]{1,0:T(8,128)(2,1)} %get-tuple-element.54), channel_id=1, source_target_pairs={{0,17},{1,16},{2,19},{3,18},{4,21},{5,20},{6,23},{7,22},{8,25},{9,... | collective-permute-start | bytes 245768 | tf_op jit(solution)/shard_map/ppermute | solution.py:552
  111.9 53.4 %all-to-all-start.1 = ((bf16[32,32,1024]{2,1,0:T(8,128)(2,1)}), bf16[32,32,1024]{2,1,0:T(8,128)(2,1)}, u32[]{:S(2)}, u32[]{:S(2)}) async-start(bf16[32,32,1024]{2,1,0:T(8,128)(2,1)} %bitcast.12), calls=%async_computation.1 | async-start | bytes 4194304 | tf_op jit(solution)/shard_map/all_to_all | solution.py:617
  165.3 77.4 %all-to-all-start.2 = ((bf16[32,32,1536]{2,1,0:T(8,128)(2,1)}), bf16[32,32,1536]{2,1,0:T(8,128)(2,1)}, u32[]{:S(2)}, u32[]{:S(2)}) async-start(bf16[32,32,1536]{2,1,0:T(8,128)(2,1)} %bitcast.28), calls=%async_computation.2 | async-start | bytes 6291456 | tf_op jit(solution)/shard_map/all_to_all | solution.py:617
  197.0 14.8 %collective-permute-start.21 = (bf16[16,2560]{1,0:T(8,128)(2,1)S(1)}, bf16[16,2560]{1,0:T(8,128)(2,1)S(1)}, u32[]{:S(2)}, u32[]{:S(2)}) collective-permute-start(bf16[16,2560]{1,0:T(8,128)(2,1)S(1)} %get-tuple-element.86), channel_id=1, source_target_pairs={{0,24},{1,25},{2,26},{3,27},{4,28},{5,29},{6,30},{7,31},{8,16},{9,... | collective-permute-start | bytes 245768 | tf_op jit(solution)/shard_map/ppermute | solution.py:552
  199.6 13.8 %collective-permute-start.22 = (bf16[16,2560]{1,0:T(8,128)(2,1)S(1)}, bf16[16,2560]{1,0:T(8,128)(2,1)S(1)}, u32[]{:S(2)}, u32[]{:S(2)}) collective-permute-start(bf16[16,2560]{1,0:T(8,128)(2,1)S(1)} %get-tuple-element.85), channel_id=1, source_target_pairs={{0,28},{1,29},{2,30},{3,31},{4,24},{5,25},{6,26},{7,27},{8,20},{9,... | collective-permute-start | bytes 245768 | tf_op jit(solution)/shard_map/ppermute | solution.py:552
  205.5 17.8 %collective-permute-start.23 = (bf16[16,2560]{1,0:T(8,128)(2,1)S(1)}, bf16[16,2560]{1,0:T(8,128)(2,1)S(1)}, u32[]{:S(2)}, u32[]{:S(2)}) collective-permute-start(bf16[16,2560]{1,0:T(8,128)(2,1)S(1)} %get-tuple-element.84), channel_id=1, source_target_pairs={{0,1},{1,0},{2,3},{3,2},{4,5},{5,4},{6,7},{7,6},{8,9},{9,8},{10,11... | collective-permute-start | bytes 245768 | tf_op jit(solution)/shard_map/ppermute | solution.py:552
  205.5 19.9 %collective-permute-start.24 = (bf16[16,2560]{1,0:T(8,128)(2,1)S(1)}, bf16[16,2560]{1,0:T(8,128)(2,1)S(1)}, u32[]{:S(2)}, u32[]{:S(2)}) collective-permute-start(bf16[16,2560]{1,0:T(8,128)(2,1)S(1)} %get-tuple-element.83), channel_id=1, source_target_pairs={{0,5},{1,4},{2,7},{3,6},{4,1},{5,0},{6,3},{7,2},{8,13},{9,12},{10,... | collective-permute-start | bytes 245768 | tf_op jit(solution)/shard_map/ppermute | solution.py:552
  207.2 21.6 %collective-permute-start.25 = (bf16[16,2560]{1,0:T(8,128)(2,1)S(1)}, bf16[16,2560]{1,0:T(8,128)(2,1)S(1)}, u32[]{:S(2)}, u32[]{:S(2)}) collective-permute-start(bf16[16,2560]{1,0:T(8,128)(2,1)S(1)} %get-tuple-element.82), channel_id=1, source_target_pairs={{0,9},{1,8},{2,11},{3,10},{4,13},{5,12},{6,15},{7,14},{8,1},{9,0},... | collective-permute-start | bytes 245768 | tf_op jit(solution)/shard_map/ppermute | solution.py:552
  211.8 18.1 %collective-permute-start.26 = (bf16[16,2560]{1,0:T(8,128)(2,1)S(1)}, bf16[16,2560]{1,0:T(8,128)(2,1)S(1)}, u32[]{:S(2)}, u32[]{:S(2)}) collective-permute-start(bf16[16,2560]{1,0:T(8,128)(2,1)S(1)} %get-tuple-element.81), channel_id=1, source_target_pairs={{0,13},{1,12},{2,15},{3,14},{4,9},{5,8},{6,11},{7,10},{8,5},{9,4},... | collective-permute-start | bytes 245768 | tf_op jit(solution)/shard_map/ppermute | solution.py:552
  213.4 17.0 %collective-permute-start.27 = (bf16[16,2560]{1,0:T(8,128)(2,1)S(1)}, bf16[16,2560]{1,0:T(8,128)(2,1)S(1)}, u32[]{:S(2)}, u32[]{:S(2)}) collective-permute-start(bf16[16,2560]{1,0:T(8,128)(2,1)S(1)} %get-tuple-element.80), channel_id=1, source_target_pairs={{0,17},{1,16},{2,19},{3,18},{4,21},{5,20},{6,23},{7,22},{8,25},{9,... | collective-permute-start | bytes 245768 | tf_op jit(solution)/shard_map/ppermute | solution.py:552
  242.8 55.2 %all-to-all-start.3 = ((bf16[32,32,1024]{2,1,0:T(8,128)(2,1)}), bf16[32,32,1024]{2,1,0:T(8,128)(2,1)}, u32[]{:S(2)}, u32[]{:S(2)}) async-start(bf16[32,32,1024]{2,1,0:T(8,128)(2,1)} %bitcast.29), calls=%async_computation.3 | async-start | bytes 4194304 | tf_op jit(solution)/shard_map/all_to_all | solution.py:617
  251.9 47.7 %collective-permute-start.31 = (bf16[384,128]{1,0:T(8,128)(2,1)}, bf16[384,128]{1,0:T(8,128)(2,1)S(1)}, u32[]{:S(2)}, u32[]{:S(2)}) collective-permute-start(bf16[384,128]{1,0:T(8,128)(2,1)} %get-tuple-element.74), channel_id=1, source_target_pairs={{0,2},{1,3},{2,0},{3,1},{4,6},{5,7},{6,4},{7,5},{8,10},{9,11},{10,... | collective-permute-start | bytes 294920 | tf_op jit(solution)/shard_map/ppermute | solution.py:538
  (36 other events, 632.2 us)

commit v7 on v6

--- a/solution.py
+++ b/solution.py
@@ -156,7 +156,7 @@
     )(rows, far, by_lon, by_wave)
 
 
-def pack_kernel(near, spec_ref, table_ref, out_ref, tail_ref, sems):
+def pack_kernel(near, spec_ref, table_ref, out_ref, last_ref, tail_ref, sems):
     degrees, half_lat = table_ref.shape[1:]
     half = LANES // 2
     copies = []
@@ -171,43 +171,44 @@
         fetch(table_ref.at[near + slot, pl.ds(degrees - LANES, LANES), :], out_ref.at[rows, lanes])
         fetch(spec_ref.at[near + slot, :, pl.ds(degrees - LANES, LANES)], out_ref.at[rows, sides])
     for slot in range(2):
-        rows = pl.ds(2 * LANES + slot * half, half)
-        fetch(table_ref.at[near + 2 + slot, pl.ds(degrees - half, half), :], out_ref.at[rows, lanes])
+        rows = pl.ds(slot * half, half)
+        fetch(table_ref.at[near + 2 + slot, pl.ds(degrees - half, half), :], last_ref.at[rows, lanes])
         fetch(spec_ref.at[near + 2 + slot, :, pl.ds(degrees - LANES, LANES)], tail_ref.at[slot])
     for copy in copies:
         copy.wait()
     third = pltpu.roll(tail_ref[0].astype(jnp.float32), half, 1)
     lower = lax.broadcasted_iota(jnp.int32, third.shape, 1) < half
     both = jnp.where(lower, third, tail_ref[1].astype(jnp.float32))
-    out_ref[pl.ds(2 * LANES, LANES), sides] = both.astype(out_ref.dtype)
+    last_ref[:, sides] = both.astype(last_ref.dtype)
 
 
 def pack(spec_rows, legendre, near):
-    shape = (3 * LANES, legendre.shape[2] + LANES)
+    shapes = [(rows * LANES, legendre.shape[2] + LANES) for rows in (2, 1)]
     return pl.pallas_call(
         functools.partial(pack_kernel, near),
         in_specs=[pl.BlockSpec(memory_space=pl.ANY)] * 2,
-        out_specs=pl.BlockSpec(shape, lambda: (0, 0)),
-        out_shape=jax.ShapeDtypeStruct(shape, jnp.bfloat16),
+        out_specs=[pl.BlockSpec(shape, lambda: (0, 0)) for shape in shapes],
+        out_shape=[jax.ShapeDtypeStruct(shape, jnp.bfloat16) for shape in shapes],
         scratch_shapes=[
             pltpu.VMEM((2, spec_rows.shape[1], LANES), jnp.bfloat16),
             pltpu.SemaphoreType.DMA((8,)),
         ],
         compiler_params=pltpu.CompilerParams(vmem_limit_bytes=VMEM_BYTES),
-        cost_estimate=pl.CostEstimate(flops=0, bytes_accessed=4 * shape[0] * shape[1], transcendentals=0),
+        cost_estimate=pl.CostEstimate(flops=0, bytes_accessed=12 * LANES * shapes[0][1], transcendentals=0),
         name="pack",
     )(spec_rows, legendre)
 
 
-def far_synthesis_kernel(levels, fields, scale, place_ref, waves_ref, own_ref, partner_ref, *refs):
-    out_refs, rows_ref = refs[:-1], refs[-1]
+def far_synthesis_kernel(levels, fields, scale, place_ref, waves_ref, *refs):
+    pack_refs, out_refs, rows_ref = refs[:4], refs[4:-1], refs[-1]
     tiles = rows_ref.shape[1]
     half_lat = tiles * LANES
     stride = rows_ref.shape[2] // levels
     degree = lax.broadcasted_iota(jnp.int32, (1, LANES), 1)
     for slot in range(8):
-        pack_ref, local = (own_ref, slot) if slot < 4 else (partner_ref, slot - 4)
-        rows = pl.ds(min(local, 2) * LANES, LANES)
+        local = slot % 4
+        pack_ref = pack_refs[slot // 4 * 2 + local // 2]
+        rows = pl.ds(local % 2 * LANES if local < 2 else 0, LANES)
         distance = degree - waves_ref[slot] + (LANES // 2 if local == 2 else 0)
         keep = jnp.where(distance >= 0, 1.0, 0.0)
         if local >= 2:
@@ -231,26 +232,26 @@
                 out_ref[:, lanes] = rows_ref[field, tile, rows, :].astype(out_ref.dtype)
 
 
-def far_synthesize(place, waves, own, partner, levels, fields, scale):
-    tiles = own.shape[1] // LANES - 1
+def far_synthesize(place, waves, packs, levels, fields, scale):
+    tiles = packs[0].shape[1] // LANES - 1
     shape = (16, fields * tiles * LANES)
-    whole = pl.BlockSpec(own.shape, lambda: (0, 0))
     return pl.pallas_call(
         functools.partial(far_synthesis_kernel, levels, fields, scale),
-        in_specs=[pl.BlockSpec(memory_space=pltpu.SMEM)] * 2 + [whole, whole],
+        in_specs=[pl.BlockSpec(memory_space=pltpu.SMEM)] * 2 + [pl.BlockSpec(x.shape, lambda: (0, 0)) for x in packs],
         out_specs=[pl.BlockSpec(shape, lambda: (0, 0))] * levels,
         out_shape=[jax.ShapeDtypeStruct(shape, jnp.bfloat16)] * levels,
         scratch_shapes=[pltpu.VMEM((fields, tiles, 16 * levels, LANES), jnp.float32)],
         compiler_params=pltpu.CompilerParams(vmem_limit_bytes=VMEM_BYTES),
         cost_estimate=pl.CostEstimate(
-            flops=16 * 2 * fields * levels * LANES * tiles * LANES, bytes_accessed=4 * own.size, transcendentals=0
+            flops=16 * 2 * fields * levels * LANES * tiles * LANES, bytes_accessed=12 * packs[0].size, transcendentals=0
         ),
         name="far_synthesis",
-    )(place, waves, own, partner)
-
-
-def far_analysis_kernel(levels, fields, chunks, place_ref, own_ref, partner_ref, *refs):
-    zonal_refs, own_out_ref, partner_out_ref, rows_ref = refs[:levels], refs[-3], refs[-2], refs[-1]
+    )(place, waves, *packs)
+
+
+def far_analysis_kernel(levels, fields, chunks, place_ref, *refs):
+    pack_refs, zonal_refs = refs[:4], refs[4:-3]
+    own_out_ref, partner_out_ref, rows_ref = refs[-3:]
     tiles = rows_ref.shape[1]
     stride = rows_ref.shape[2] // levels
     for apart, zonal_ref in enumerate(zonal_refs):
@@ -262,10 +263,11 @@
                     rows_ref[field, tile, rows, :] = zonal_ref[:, pl.ds(offset, LANES)].astype(jnp.float32)
                     offset += LANES
     lower = lax.broadcasted_iota(jnp.int32, (1, LANES), 1) < LANES // 2
-    for pack_ref, out_ref, base in ((own_ref, own_out_ref, 0), (partner_ref, partner_out_ref, 4)):
+    for out_ref, base in ((own_out_ref, 0), (partner_out_ref, 4)):
         sums = []
         for local in range(4):
-            rows = pl.ds(min(local, 2) * LANES, LANES)
+            pack_ref = pack_refs[base // 2 + local // 2]
+            rows = pl.ds(local % 2 * LANES if local < 2 else 0, LANES)
             zonal = jnp.concatenate(
                 [
                     jnp.concatenate(
@@ -290,24 +292,23 @@
             out_ref[pl.ds(block * size, size), :] = sums[block].astype(out_ref.dtype)
 
 
-def far_analyze(place, own, partner, zonal, levels, fields, chunks):
-    tiles = own.shape[1] // LANES - 1
+def far_analyze(place, packs, zonal, levels, fields, chunks):
+    tiles = packs[0].shape[1] // LANES - 1
     shape = (3 * 2 * fields * levels, LANES)
-    whole = pl.BlockSpec(own.shape, lambda: (0, 0))
     out_spec = pl.BlockSpec(shape, lambda: (0, 0))
     return pl.pallas_call(
         functools.partial(far_analysis_kernel, levels, fields, chunks),
-        in_specs=[pl.BlockSpec(memory_space=pltpu.SMEM), whole, whole]
-        + [pl.BlockSpec(x.shape, lambda: (0, 0)) for x in zonal],
+        in_specs=[pl.BlockSpec(memory_space=pltpu.SMEM)]
+        + [pl.BlockSpec(x.shape, lambda: (0, 0)) for x in (*packs, *zonal)],
         out_specs=[out_spec, out_spec],
         out_shape=[jax.ShapeDtypeStruct(shape, jnp.float32), jax.ShapeDtypeStruct(shape, jnp.bfloat16)],
         scratch_shapes=[pltpu.VMEM((fields, tiles, 16 * levels, LANES), jnp.float32)],
         compiler_params=pltpu.CompilerParams(vmem_limit_bytes=VMEM_BYTES),
         cost_estimate=pl.CostEstimate(
-            flops=16 * 2 * fields * levels * LANES * tiles * LANES, bytes_accessed=4 * own.size, transcendentals=0
+            flops=16 * 2 * fields * levels * LANES * tiles * LANES, bytes_accessed=12 * packs[0].size, transcendentals=0
         ),
         name="far_analysis",
-    )(place, own, partner, *zonal)
+    )(place, *packs, *zonal)
 
 
 def fold_kernel(slots, levels, fields, arrived_ref, out_ref, rows_ref):
@@ -635,9 +636,9 @@
     def send(spec, chunk):
         return synthesize(first.reshape(1), owner_table, spec, legendre, chunk, fields, levels, least)
 
-    own_pack = pack(spec_rows, legendre, near)
-    partner_pack = across_halves(own_pack)
-    large = send(after(spec_rows, own_pack), chunks[0])
+    packs = list(pack(spec_rows, legendre, near))
+    packs += [across_halves(packs[0]), across_halves(packs[1])]
+    large = send(after(spec_rows, packs[0]), chunks[0])
 
     bands, planes = lax.axis_size("band"), lax.axis_size("grp")
     by_device = jnp.swapaxes(owner_table.reshape(bands, planes, slots), 0, 1).reshape(2, levels, slots)
@@ -654,9 +655,9 @@
 
     small = send(after(spec_rows, large), chunks[1])
     by_wave, by_lon = trig_tables(after(waves, large), lon_count, small)
-    arrived = [exchange(after(large, small, partner_pack))]
+    arrived = [exchange(after(large, small, packs[2]))]
     far_rows = far_synthesize(
-        place, far_waves[0] - far_least, own_pack, partner_pack, levels, fields, 1.0 / math.sqrt(degrees)
+        place, far_waves[0] - far_least, packs, levels, fields, 1.0 / math.sqrt(degrees)
     )
     far_rows = jnp.concatenate(within_half(far_rows))
     arrived.append(exchange(after(small, far_rows, *arrived)))
@@ -667,7 +668,7 @@
     far_zonal = jnp.concatenate([zonal[0][1], zonal[1][1]], axis=1)
     far_zonal = within_half([far_zonal[16 * x : 16 * x + 16] for x in range(levels)])
     returned.append(exchange(after(zonal[1][0], *far_zonal, *returned)))
-    own_sums, partner_sums = far_analyze(place, own_pack, partner_pack, far_zonal, levels, fields, chunks)
+    own_sums, partner_sums = far_analyze(place, packs, far_zonal, levels, fields, chunks)
     other_sums = across_halves(partner_sums)
     wavenumber = lax.dynamic_slice_in_dim(after(owner_table, by_wave), first, slots)
     distance = jnp.arange(degrees, dtype=jnp.int32)[None, :] - wavenumber[:, None]

time: 308 us -> 303 us (0.984)
  waiting for transfers between devices: 115 us -> 111 us
    ppermute x2 -> x3, waiting for transfers between devices: 13.4 us -> 10.1 us  [across_halves(): lax.ppermute(value, 'grp', [(p, (p + planes // 2) % planes) for p in rang...]
    ppermute x2 -> x3, starting transfers between devices: 6.43 us -> 6.51 us  [across_halves(): lax.ppermute(value, 'grp', [(p, (p + planes // 2) % planes) for p in rang...]
  transfers between devices with their start and end apart: 36 -> 37, of which waited for: 23 -> 22; matrix products, arithmetic and copies ran while one was open for 4% -> 4% of each run, Pallas kernels for 32% -> 32%
where the time goes in v7:
time: 303 us
  waiting for transfers between devices  111 us (37%)
  Pallas kernels  105 us (35%)
  starting transfers between devices  70.3 us (23%)
  local copies, waits for them, and re-layouts  9.25 us (3%)
  other arithmetic  6.4 us (2%)
    ppermute x30, waiting for transfers between devices, within_half(): moved.append(lax.ppermute(parts[x], AXES, pairs))  64.3 us
    pallas_call x2, Pallas kernels, longitudes(): pl.pallas_call(functools.partial(longitude_kernel, fields, chunk, 1.0 / m...  53.1 us
    ppermute x30, starting transfers between devices, within_half(): moved.append(lax.ppermute(parts[x], AXES, pairs))  46 us
    all_to_all x4, waiting for transfers between devices, exchange(): lax.all_to_all(rows, AXES[::-1], split_axis=0, concat_axis=0, tiled=True)  36.5 us
    all_to_all x4, starting transfers between devices, exchange(): lax.all_to_all(rows, AXES[::-1], split_axis=0, concat_axis=0, tiled=True)  17.8 us
    pallas_call x2, Pallas kernels, synthesize(): pl.pallas_call(functools.partial(synthesis_kernel, slots, levels, fields,...  13.3 us
    ppermute x3, waiting for transfers between devices, across_halves(): lax.ppermute(value, 'grp', [(p, (p + planes // 2) % planes) for p in rang...  10.1 us
    pallas_call x1, Pallas kernels, trig_tables(): pl.pallas_call(trig_kernel, grid=(depth // rows,), in_specs=[pl.BlockSpec...  9.06 us
  transfers between devices with their start and end apart: 37, of which 22 were waited for; matrix products, arithmetic and copies ran while one was open for 4% of the time, Pallas kernels for 32%

profile of v7, /device:TPU:0, one launch (start us, length us, event | category | flops | bytes accessed | tf_op | source)
XLA Modules:
  0.0 302.5 jit_solution(14362246891539776053)
XLA Ops:
  2.0 4.1 %collective-permute-start = (bf16[256,768]{1,0:T(8,128)(2,1)}, bf16[256,768]{1,0:T(8,128)(2,1)S(1)}, u32[]{:S(2)}, u32[]{:S(2)}) collective-permute-start(bf16[256,768]{1,0:T(8,128)(2,1)} %get-tuple-element.42.refs_0_), channel_id=1, source_target_pairs={{0,2},{1,3},{2,0},{3,1},{4,6},{5,7},{6,4},{7,5},{8,10},{9,11},{10,... | collective-permute-start | bytes 1179656 | tf_op jit(solution)/shard_map/ppermute | solution.py:539
  6.4 7.4 %synthesis.2 = bf16[1024,1536]{1,0:T(8,128)(2,1)} custom-call(s32[1]{0:T(128)} %bitcast.1.first_ref, s32[640]{0:T(1024)} %owner_ref.3, bf16[20,128,640]{2,1,0:T(8,128)(2,1)} %bitcast.25, bf16[20,640,640]{2,1,0:T(8,128)(2,1)} %table_ref.7), custom_call_target="tpu_custom_call" | custom-call | flops 2013265920 | bytes 13631488 | tf_op jit(solution)/shard_map/synthesis/pallas_call | solution.py:81
  14.5 5.9 %synthesis.3 = bf16[1024,1024]{1,0:T(8,128)(2,1)} custom-call(s32[1]{0:T(128)} %bitcast.1.first_ref, s32[640]{0:T(1024)} %owner_ref.3, bf16[20,128,640]{2,1,0:T(8,128)(2,1)} %bitcast.26, bf16[20,640,640]{2,1,0:T(8,128)(2,1)} %table_ref.7), custom_call_target="tpu_custom_call" | custom-call | flops 1342177280 | bytes 9961472 | tf_op jit(solution)/shard_map/synthesis/pallas_call | solution.py:81
  20.4 8.5 %collective-permute-done.refs_2_ = bf16[256,768]{1,0:T(8,128)(2,1)S(1)} collective-permute-done((bf16[256,768]{1,0:T(8,128)(2,1)}, bf16[256,768]{1,0:T(8,128)(2,1)S(1)}, u32[]{:S(2)}, u32[]{:S(2)}) %collective-permute-start) | collective-permute-done | bytes 393248 | tf_op jit(solution)/shard_map/ppermute | solution.py:539
  29.7 5.2 %all-to-all-start = ((bf16[32,32,1536]{2,1,0:T(8,128)(2,1)}), bf16[32,32,1536]{2,1,0:T(8,128)(2,1)}, u32[]{:S(2)}, u32[]{:S(2)}) async-start(bf16[32,32,1536]{2,1,0:T(8,128)(2,1)} %bitcast.27), calls=%async_computation | async-start | bytes 6291456 | tf_op jit(solution)/shard_map/all_to_all | solution.py:618
  47.7 11.8 %collective-permute-done.3 = bf16[16,2560]{1,0:T(8,128)(2,1)S(1)} collective-permute-done((bf16[16,2560]{1,0:T(8,128)(2,1)}, bf16[16,2560]{1,0:T(8,128)(2,1)S(1)}, u32[]{:S(2)}, u32[]{:S(2)}) %collective-permute-start.3) | collective-permute-done | bytes 81952 | tf_op jit(solution)/shard_map/ppermute | solution.py:553
  64.3 4.6 %collective-permute-done.7 = bf16[16,2560]{1,0:T(8,128)(2,1)S(1)} collective-permute-done((bf16[16,2560]{1,0:T(8,128)(2,1)}, bf16[16,2560]{1,0:T(8,128)(2,1)S(1)}, u32[]{:S(2)}, u32[]{:S(2)}) %collective-permute-start.7) | collective-permute-done | bytes 81952 | tf_op jit(solution)/shard_map/ppermute | solution.py:553
  72.6 16.5 %collective-permute-done.9 = bf16[16,2560]{1,0:T(8,128)(2,1)S(1)} collective-permute-done((bf16[16,2560]{1,0:T(8,128)(2,1)}, bf16[16,2560]{1,0:T(8,128)(2,1)S(1)}, u32[]{:S(2)}, u32[]{:S(2)}) %collective-permute-start.9) | collective-permute-done | bytes 81952 | tf_op jit(solution)/shard_map/ppermute | solution.py:553
  97.8 4.1 %collective-permute-done.15 = bf16[16,2560]{1,0:T(8,128)(2,1)S(1)} collective-permute-done((bf16[16,2560]{1,0:T(8,128)(2,1)S(1)}, bf16[16,2560]{1,0:T(8,128)(2,1)S(1)}, u32[]{:S(2)}, u32[]{:S(2)}) %collective-permute-start.15) | collective-permute-done | bytes 81952 | tf_op jit(solution)/shard_map/ppermute | solution.py:553
  107.6 4.6 %all-to-all-start.1 = ((bf16[32,32,1024]{2,1,0:T(8,128)(2,1)}), bf16[32,32,1024]{2,1,0:T(8,128)(2,1)}, u32[]{:S(2)}, u32[]{:S(2)}) async-start(bf16[32,32,1024]{2,1,0:T(8,128)(2,1)} %bitcast.12), calls=%async_computation.1 | async-start | bytes 4194304 | tf_op jit(solution)/shard_map/all_to_all | solution.py:618
  114.2 3.8 %fusion = (f32[1280,128]{1,0:T(8,128)}, f32[1280,128]{1,0:T(8,128)}) fusion(f32[1280]{0:T(1024)S(1)} %convert_element_type.24), kind=kLoop, calls=%fused_computation.2 | loop fusion | flops 983040 | bytes 1315840 | tf_op jit(solution)/shard_map/sin | solution.py:593
  119.1 9.1 %trig.1 = (bf16[1280,2560]{1,0:T(8,128)(2,1)}, bf16[2560,1280]{1,0:T(8,128)(2,1)}) custom-call(f32[1280,4]{1,0:T(8,128)} %copy.38.small_ref, f32[1280,128]{1,0:T(8,128)} %get-tuple-element.66.cos_turn_ref, f32[1280,128]{1,0:T(8,128)} %get-tuple-element.67.sin_turn_ref), custom_call_target="tpu_custom_call" | custom-call | flops 39321600 | bytes 13107200 | tf_op jit(solution)/shard_map/trig/pallas_call | solution.py:597
  128.2 31.1 %longitudes.3 = (bf16[1024,1536]{1,0:T(8,128)(2,1)}, bf16[256,1536]{1,0:T(8,128)(2,1)}) custom-call(bf16[1024,1536]{1,0:T(8,128)(2,1)} %bitcast.11.rows_ref, bf16[256,2560]{1,0:T(8,128)(2,1)} %copy-done.20, bf16[2560,1280]{1,0:T(8,128)(2,1)} %get-tuple-element.68.by_lon_ref, bf16[1280,2560]{1,0:T(8,128)(2,1)} %get-tuple-element.69.by_wave_ref), custom_call_target="tpu_custom_call" | custom-call | flops 20132659200 | bytes 20971520 | tf_op jit(solution)/shard_map/longitudes/pallas_call | solution.py:137
  161.0 4.3 %all-to-all-start.2 = ((bf16[32,32,1536]{2,1,0:T(8,128)(2,1)}), bf16[32,32,1536]{2,1,0:T(8,128)(2,1)}, u32[]{:S(2)}, u32[]{:S(2)}) async-start(bf16[32,32,1536]{2,1,0:T(8,128)(2,1)} %bitcast.28), calls=%async_computation.2 | async-start | bytes 6291456 | tf_op jit(solution)/shard_map/all_to_all | solution.py:618
  165.3 22.0 %longitudes.2 = (bf16[1024,1024]{1,0:T(8,128)(2,1)}, bf16[256,1024]{1,0:T(8,128)(2,1)}) custom-call(bf16[1024,1024]{1,0:T(8,128)(2,1)} %bitcast.13.rows_ref, bf16[256,2560]{1,0:T(8,128)(2,1)} %copy-done.20, bf16[2560,1280]{1,0:T(8,128)(2,1)} %get-tuple-element.68.by_lon_ref, bf16[1280,2560]{1,0:T(8,128)(2,1)} %get-tuple-element.69.by_wave_ref), custom_call_target="tpu_custom_call" | custom-call | flops 13421772800 | bytes 18350080 | tf_op jit(solution)/shard_map/longitudes/pallas_call | solution.py:137
  195.2 5.4 %collective-permute-start.23 = (bf16[16,2560]{1,0:T(8,128)(2,1)S(1)}, bf16[16,2560]{1,0:T(8,128)(2,1)S(1)}, u32[]{:S(2)}, u32[]{:S(2)}) collective-permute-start(bf16[16,2560]{1,0:T(8,128)(2,1)S(1)} %get-tuple-element.89), channel_id=1, source_target_pairs={{0,28},{1,29},{2,30},{3,31},{4,24},{5,25},{6,26},{7,27},{8,20},{9,... | collective-permute-start | bytes 245768 | tf_op jit(solution)/shard_map/ppermute | solution.py:553
  202.8 4.6 %collective-permute-start.26 = (bf16[16,2560]{1,0:T(8,128)(2,1)S(1)}, bf16[16,2560]{1,0:T(8,128)(2,1)S(1)}, u32[]{:S(2)}, u32[]{:S(2)}) collective-permute-start(bf16[16,2560]{1,0:T(8,128)(2,1)S(1)} %get-tuple-element.86), channel_id=1, source_target_pairs={{0,9},{1,8},{2,11},{3,10},{4,13},{5,12},{6,15},{7,14},{8,1},{9,0},... | collective-permute-start | bytes 245768 | tf_op jit(solution)/shard_map/ppermute | solution.py:553
  209.0 4.3 %collective-permute-start.28 = (bf16[16,2560]{1,0:T(8,128)(2,1)S(1)}, bf16[16,2560]{1,0:T(8,128)(2,1)S(1)}, u32[]{:S(2)}, u32[]{:S(2)}) collective-permute-start(bf16[16,2560]{1,0:T(8,128)(2,1)S(1)} %get-tuple-element.84), channel_id=1, source_target_pairs={{0,17},{1,16},{2,19},{3,18},{4,21},{5,20},{6,23},{7,22},{8,25},{9,... | collective-permute-start | bytes 245768 | tf_op jit(solution)/shard_map/ppermute | solution.py:553
  213.4 5.6 %collective-permute-done.24.refs_12_ = bf16[16,2560]{1,0:T(8,128)(2,1)S(1)} collective-permute-done((bf16[16,2560]{1,0:T(8,128)(2,1)S(1)}, bf16[16,2560]{1,0:T(8,128)(2,1)S(1)}, u32[]{:S(2)}, u32[]{:S(2)}) %collective-permute-start.24) | collective-permute-done | bytes 81952 | tf_op jit(solution)/shard_map/ppermute | solution.py:553
  227.7 5.9 %collective-permute-done.30.refs_18_ = bf16[16,2560]{1,0:T(8,128)(2,1)S(1)} collective-permute-done((bf16[16,2560]{1,0:T(8,128)(2,1)S(1)}, bf16[16,2560]{1,0:T(8,128)(2,1)S(1)}, u32[]{:S(2)}, u32[]{:S(2)}) %collective-permute-start.30) | collective-permute-done | bytes 81952 | tf_op jit(solution)/shard_map/ppermute | solution.py:553
  249.9 5.3 %fold.1.folded_ref = bf16[16,256,384]{2,1,0:T(8,128)(2,1)} custom-call(bf16[1024,1536]{1,0:T(8,128)(2,1)} %bitcast.15.arrived_ref), custom_call_target="tpu_custom_call" | custom-call | flops 3145728 | bytes 6291456 | tf_op jit(solution)/shard_map/fold/pallas_call | solution.py:344
  255.3 8.5 %analysis.1.base_ref = f32[20,128,640]{2,1,0:T(8,128)} custom-call(bf16[16,256,384]{2,1,0:T(8,128)(2,1)} %fold.1.folded_ref, f32[20,1,640]{2,1,0:T(1,128)} %get-tuple-element.104.even_ref, f32[20,1,640]{2,1,0:T(1,128)} %get-tuple-element.103.odd_ref, bf16[20,640,640]{2,1,0:T(8,128)(2,1)} %table_ref.7, bf16[20,640,640]{2,1,0:T(8,128)(2,1)} %table_ref.7, ...), custom_call_target="tpu_custom_call" | custom-call | flops 2516582400 | bytes 20316160 | tf_op jit(solution)/shard_map/analysis/pallas_call | solution.py:387
  263.8 29.8 %all-to-all-done.3 = bf16[32,32,1024]{2,1,0:T(8,128)(2,1)} async-done(((bf16[32,32,1024]{2,1,0:T(8,128)(2,1)}), bf16[32,32,1024]{2,1,0:T(8,128)(2,1)}, u32[]{:S(2)}, u32[]{:S(2)}) %all-to-all-start.3) | async-done | bytes 2097184 | tf_op jit(solution)/shard_map/all_to_all | solution.py:618
  295.8 6.5 %closing.1 = f32[20,128,640]{2,1,0:T(8,128)} custom-call(s32[1]{0:T(128)} %bitcast.hemi_ref, bf16[1024,1024]{1,0:T(8,128)(2,1)} %bitcast.17.arrived_ref, bf16[20,640,640]{2,1,0:T(8,128)(2,1)} %table_ref.7, f32[20,128,640]{2,1,0:T(8,128)} %analysis.1.base_ref, f32[20,1,640]{2,1,0:T(1,128)} %get-tuple-element.104.even_ref, ...), custom_call_target="tpu_custom_call", output_to_operand_aliasing={{}: (3, {})} | custom-call | flops 1677721600 | bytes 15204352 | tf_op jit(solution)/shard_map/closing/pallas_call | solution.py:511
  (161 shorter events, 82.9 us)
Async XLA Ops:
  2.0 26.9 %collective-permute-start = (bf16[256,768]{1,0:T(8,128)(2,1)}, bf16[256,768]{1,0:T(8,128)(2,1)S(1)}, u32[]{:S(2)}, u32[]{:S(2)}) collective-permute-start(bf16[256,768]{1,0:T(8,128)(2,1)} %get-tuple-element.42.refs_0_), channel_id=1, source_target_pairs={{0,2},{1,3},{2,0},{3,1},{4,6},{5,7},{6,4},{7,5},{8,10},{9,11},{10,... | collective-permute-start | bytes 1179656 | tf_op jit(solution)/shard_map/ppermute | solution.py:539
  6.1 29.9 %collective-permute-start.1 = (bf16[128,768]{1,0:T(8,128)(2,1)}, bf16[128,768]{1,0:T(8,128)(2,1)S(1)}, u32[]{:S(2)}, u32[]{:S(2)}) collective-permute-start(bf16[128,768]{1,0:T(8,128)(2,1)} %get-tuple-element.45.refs_1_), channel_id=1, source_target_pairs={{0,2},{1,3},{2,0},{3,1},{4,6},{5,7},{6,4},{7,5},{8,10},{9,11},{10,... | collective-permute-start | bytes 589832 | tf_op jit(solution)/shard_map/ppermute | solution.py:539
  29.7 77.9 %all-to-all-start = ((bf16[32,32,1536]{2,1,0:T(8,128)(2,1)}), bf16[32,32,1536]{2,1,0:T(8,128)(2,1)}, u32[]{:S(2)}, u32[]{:S(2)}) async-start(bf16[32,32,1536]{2,1,0:T(8,128)(2,1)} %bitcast.27), calls=%async_computation | async-start | bytes 6291456 | tf_op jit(solution)/shard_map/all_to_all | solution.py:618
  41.6 17.8 %collective-permute-start.3 = (bf16[16,2560]{1,0:T(8,128)(2,1)}, bf16[16,2560]{1,0:T(8,128)(2,1)S(1)}, u32[]{:S(2)}, u32[]{:S(2)}) collective-permute-start(bf16[16,2560]{1,0:T(8,128)(2,1)} %get-tuple-element.48), channel_id=1, source_target_pairs={{0,8},{1,9},{2,10},{3,11},{4,12},{5,13},{6,14},{7,15},{8,0},{9,1},... | collective-permute-start | bytes 245768 | tf_op jit(solution)/shard_map/ppermute | solution.py:553
  43.3 17.1 %collective-permute-start.4 = (bf16[16,2560]{1,0:T(8,128)(2,1)}, bf16[16,2560]{1,0:T(8,128)(2,1)S(1)}, u32[]{:S(2)}, u32[]{:S(2)}) collective-permute-start(bf16[16,2560]{1,0:T(8,128)(2,1)} %get-tuple-element.49), channel_id=1, source_target_pairs={{0,12},{1,13},{2,14},{3,15},{4,8},{5,9},{6,10},{7,11},{8,4},{9,5},... | collective-permute-start | bytes 245768 | tf_op jit(solution)/shard_map/ppermute | solution.py:553
  43.3 17.5 %collective-permute-start.5 = (bf16[16,2560]{1,0:T(8,128)(2,1)}, bf16[16,2560]{1,0:T(8,128)(2,1)S(1)}, u32[]{:S(2)}, u32[]{:S(2)}) collective-permute-start(bf16[16,2560]{1,0:T(8,128)(2,1)} %get-tuple-element.50), channel_id=1, source_target_pairs={{0,16},{1,17},{2,18},{3,19},{4,20},{5,21},{6,22},{7,23},{8,24},{9,... | collective-permute-start | bytes 245768 | tf_op jit(solution)/shard_map/ppermute | solution.py:553
  45.0 18.1 %collective-permute-start.6 = (bf16[16,2560]{1,0:T(8,128)(2,1)}, bf16[16,2560]{1,0:T(8,128)(2,1)S(1)}, u32[]{:S(2)}, u32[]{:S(2)}) collective-permute-start(bf16[16,2560]{1,0:T(8,128)(2,1)} %get-tuple-element.51), channel_id=1, source_target_pairs={{0,20},{1,21},{2,22},{3,23},{4,16},{5,17},{6,18},{7,19},{8,28},{9,... | collective-permute-start | bytes 245768 | tf_op jit(solution)/shard_map/ppermute | solution.py:553
  45.1 23.8 %collective-permute-start.7 = (bf16[16,2560]{1,0:T(8,128)(2,1)}, bf16[16,2560]{1,0:T(8,128)(2,1)S(1)}, u32[]{:S(2)}, u32[]{:S(2)}) collective-permute-start(bf16[16,2560]{1,0:T(8,128)(2,1)} %get-tuple-element.52), channel_id=1, source_target_pairs={{0,24},{1,25},{2,26},{3,27},{4,28},{5,29},{6,30},{7,31},{8,16},{9,... | collective-permute-start | bytes 245768 | tf_op jit(solution)/shard_map/ppermute | solution.py:553
  60.4 28.7 %collective-permute-start.9 = (bf16[16,2560]{1,0:T(8,128)(2,1)}, bf16[16,2560]{1,0:T(8,128)(2,1)S(1)}, u32[]{:S(2)}, u32[]{:S(2)}) collective-permute-start(bf16[16,2560]{1,0:T(8,128)(2,1)} %get-tuple-element.54), channel_id=1, source_target_pairs={{0,1},{1,0},{2,3},{3,2},{4,5},{5,4},{6,7},{7,6},{8,9},{9,8},{10,11... | collective-permute-start | bytes 245768 | tf_op jit(solution)/shard_map/ppermute | solution.py:553
  60.8 30.1 %collective-permute-start.10 = (bf16[16,2560]{1,0:T(8,128)(2,1)}, bf16[16,2560]{1,0:T(8,128)(2,1)S(1)}, u32[]{:S(2)}, u32[]{:S(2)}) collective-permute-start(bf16[16,2560]{1,0:T(8,128)(2,1)} %get-tuple-element.55), channel_id=1, source_target_pairs={{0,5},{1,4},{2,7},{3,6},{4,1},{5,0},{6,3},{7,2},{8,13},{9,12},{10,... | collective-permute-start | bytes 245768 | tf_op jit(solution)/shard_map/ppermute | solution.py:553
  63.1 31.1 %collective-permute-start.11 = (bf16[16,2560]{1,0:T(8,128)(2,1)}, bf16[16,2560]{1,0:T(8,128)(2,1)S(1)}, u32[]{:S(2)}, u32[]{:S(2)}) collective-permute-start(bf16[16,2560]{1,0:T(8,128)(2,1)} %get-tuple-element.56), channel_id=1, source_target_pairs={{0,9},{1,8},{2,11},{3,10},{4,13},{5,12},{6,15},{7,14},{8,1},{9,0},... | collective-permute-start | bytes 245768 | tf_op jit(solution)/shard_map/ppermute | solution.py:553
  68.9 26.6 %collective-permute-start.12 = (bf16[16,2560]{1,0:T(8,128)(2,1)}, bf16[16,2560]{1,0:T(8,128)(2,1)S(1)}, u32[]{:S(2)}, u32[]{:S(2)}) collective-permute-start(bf16[16,2560]{1,0:T(8,128)(2,1)} %get-tuple-element.57), channel_id=1, source_target_pairs={{0,13},{1,12},{2,15},{3,14},{4,9},{5,8},{6,11},{7,10},{8,5},{9,4},... | collective-permute-start | bytes 245768 | tf_op jit(solution)/shard_map/ppermute | solution.py:553
  72.6 23.5 %collective-permute-start.13 = (bf16[16,2560]{1,0:T(8,128)(2,1)}, bf16[16,2560]{1,0:T(8,128)(2,1)S(1)}, u32[]{:S(2)}, u32[]{:S(2)}) collective-permute-start(bf16[16,2560]{1,0:T(8,128)(2,1)} %get-tuple-element.58), channel_id=1, source_target_pairs={{0,17},{1,16},{2,19},{3,18},{4,21},{5,20},{6,23},{7,22},{8,25},{9,... | collective-permute-start | bytes 245768 | tf_op jit(solution)/shard_map/ppermute | solution.py:553
  107.6 53.3 %all-to-all-start.1 = ((bf16[32,32,1024]{2,1,0:T(8,128)(2,1)}), bf16[32,32,1024]{2,1,0:T(8,128)(2,1)}, u32[]{:S(2)}, u32[]{:S(2)}) async-start(bf16[32,32,1024]{2,1,0:T(8,128)(2,1)} %bitcast.12), calls=%async_computation.1 | async-start | bytes 4194304 | tf_op jit(solution)/shard_map/all_to_all | solution.py:618
  161.0 77.3 %all-to-all-start.2 = ((bf16[32,32,1536]{2,1,0:T(8,128)(2,1)}), bf16[32,32,1536]{2,1,0:T(8,128)(2,1)}, u32[]{:S(2)}, u32[]{:S(2)}) async-start(bf16[32,32,1536]{2,1,0:T(8,128)(2,1)} %bitcast.28), calls=%async_computation.2 | async-start | bytes 6291456 | tf_op jit(solution)/shard_map/all_to_all | solution.py:618
  192.6 14.8 %collective-permute-start.22 = (bf16[16,2560]{1,0:T(8,128)(2,1)S(1)}, bf16[16,2560]{1,0:T(8,128)(2,1)S(1)}, u32[]{:S(2)}, u32[]{:S(2)}) collective-permute-start(bf16[16,2560]{1,0:T(8,128)(2,1)S(1)} %get-tuple-element.90), channel_id=1, source_target_pairs={{0,24},{1,25},{2,26},{3,27},{4,28},{5,29},{6,30},{7,31},{8,16},{9,... | collective-permute-start | bytes 245768 | tf_op jit(solution)/shard_map/ppermute | solution.py:553
  195.2 13.8 %collective-permute-start.23 = (bf16[16,2560]{1,0:T(8,128)(2,1)S(1)}, bf16[16,2560]{1,0:T(8,128)(2,1)S(1)}, u32[]{:S(2)}, u32[]{:S(2)}) collective-permute-start(bf16[16,2560]{1,0:T(8,128)(2,1)S(1)} %get-tuple-element.89), channel_id=1, source_target_pairs={{0,28},{1,29},{2,30},{3,31},{4,24},{5,25},{6,26},{7,27},{8,20},{9,... | collective-permute-start | bytes 245768 | tf_op jit(solution)/shard_map/ppermute | solution.py:553
  201.2 17.8 %collective-permute-start.24 = (bf16[16,2560]{1,0:T(8,128)(2,1)S(1)}, bf16[16,2560]{1,0:T(8,128)(2,1)S(1)}, u32[]{:S(2)}, u32[]{:S(2)}) collective-permute-start(bf16[16,2560]{1,0:T(8,128)(2,1)S(1)} %get-tuple-element.88), channel_id=1, source_target_pairs={{0,1},{1,0},{2,3},{3,2},{4,5},{5,4},{6,7},{7,6},{8,9},{9,8},{10,11... | collective-permute-start | bytes 245768 | tf_op jit(solution)/shard_map/ppermute | solution.py:553
  201.2 19.9 %collective-permute-start.25 = (bf16[16,2560]{1,0:T(8,128)(2,1)S(1)}, bf16[16,2560]{1,0:T(8,128)(2,1)S(1)}, u32[]{:S(2)}, u32[]{:S(2)}) collective-permute-start(bf16[16,2560]{1,0:T(8,128)(2,1)S(1)} %get-tuple-element.87), channel_id=1, source_target_pairs={{0,5},{1,4},{2,7},{3,6},{4,1},{5,0},{6,3},{7,2},{8,13},{9,12},{10,... | collective-permute-start | bytes 245768 | tf_op jit(solution)/shard_map/ppermute | solution.py:553
  202.8 21.6 %collective-permute-start.26 = (bf16[16,2560]{1,0:T(8,128)(2,1)S(1)}, bf16[16,2560]{1,0:T(8,128)(2,1)S(1)}, u32[]{:S(2)}, u32[]{:S(2)}) collective-permute-start(bf16[16,2560]{1,0:T(8,128)(2,1)S(1)} %get-tuple-element.86), channel_id=1, source_target_pairs={{0,9},{1,8},{2,11},{3,10},{4,13},{5,12},{6,15},{7,14},{8,1},{9,0},... | collective-permute-start | bytes 245768 | tf_op jit(solution)/shard_map/ppermute | solution.py:553
  207.4 18.1 %collective-permute-start.27 = (bf16[16,2560]{1,0:T(8,128)(2,1)S(1)}, bf16[16,2560]{1,0:T(8,128)(2,1)S(1)}, u32[]{:S(2)}, u32[]{:S(2)}) collective-permute-start(bf16[16,2560]{1,0:T(8,128)(2,1)S(1)} %get-tuple-element.85), channel_id=1, source_target_pairs={{0,13},{1,12},{2,15},{3,14},{4,9},{5,8},{6,11},{7,10},{8,5},{9,4},... | collective-permute-start | bytes 245768 | tf_op jit(solution)/shard_map/ppermute | solution.py:553
  209.0 17.0 %collective-permute-start.28 = (bf16[16,2560]{1,0:T(8,128)(2,1)S(1)}, bf16[16,2560]{1,0:T(8,128)(2,1)S(1)}, u32[]{:S(2)}, u32[]{:S(2)}) collective-permute-start(bf16[16,2560]{1,0:T(8,128)(2,1)S(1)} %get-tuple-element.84), channel_id=1, source_target_pairs={{0,17},{1,16},{2,19},{3,18},{4,21},{5,20},{6,23},{7,22},{8,25},{9,... | collective-permute-start | bytes 245768 | tf_op jit(solution)/shard_map/ppermute | solution.py:553
  238.4 55.2 %all-to-all-start.3 = ((bf16[32,32,1024]{2,1,0:T(8,128)(2,1)}), bf16[32,32,1024]{2,1,0:T(8,128)(2,1)}, u32[]{:S(2)}, u32[]{:S(2)}) async-start(bf16[32,32,1024]{2,1,0:T(8,128)(2,1)} %bitcast.29), calls=%async_computation.3 | async-start | bytes 4194304 | tf_op jit(solution)/shard_map/all_to_all | solution.py:618
  247.6 47.6 %collective-permute-start.32 = (bf16[384,128]{1,0:T(8,128)(2,1)}, bf16[384,128]{1,0:T(8,128)(2,1)S(1)}, u32[]{:S(2)}, u32[]{:S(2)}) collective-permute-start(bf16[384,128]{1,0:T(8,128)(2,1)} %get-tuple-element.78), channel_id=1, source_target_pairs={{0,2},{1,3},{2,0},{3,1},{4,6},{5,7},{6,4},{7,5},{8,10},{9,11},{10,... | collective-permute-start | bytes 294920 | tf_op jit(solution)/shard_map/ppermute | solution.py:539
  (38 other events, 642.9 us)

commit v8 on v7

--- a/solution.py
+++ b/solution.py
@@ -637,8 +637,9 @@
         return synthesize(first.reshape(1), owner_table, spec, legendre, chunk, fields, levels, least)
 
     packs = list(pack(spec_rows, legendre, near))
-    packs += [across_halves(packs[0]), across_halves(packs[1])]
+    packs.append(across_halves(packs[0]))
     large = send(after(spec_rows, packs[0]), chunks[0])
+    packs.append(across_halves(after(packs[1], large)))
 
     bands, planes = lax.axis_size("band"), lax.axis_size("grp")
     by_device = jnp.swapaxes(owner_table.reshape(bands, planes, slots), 0, 1).reshape(2, levels, slots)

time: 303 us -> 303 us (level)
  transfers between devices with their start and end apart: 37 -> 37, of which waited for: 22 -> 22; matrix products, arithmetic and copies ran while one was open for 4% -> 5% of each run, Pallas kernels for 32% -> 32%
where the time goes in v8:
time: 303 us
  waiting for transfers between devices  111 us (37%)
  Pallas kernels  105 us (35%)
  starting transfers between devices  70.3 us (23%)
  local copies, waits for them, and re-layouts  9.26 us (3%)
  other arithmetic  6.51 us (2%)
    ppermute x30, waiting for transfers between devices, within_half(): moved.append(lax.ppermute(parts[x], AXES, pairs))  64.1 us
    pallas_call x2, Pallas kernels, longitudes(): pl.pallas_call(functools.partial(longitude_kernel, fields, chunk, 1.0 / m...  53.1 us
    ppermute x30, starting transfers between devices, within_half(): moved.append(lax.ppermute(parts[x], AXES, pairs))  45.9 us
    all_to_all x4, waiting for transfers between devices, exchange(): lax.all_to_all(rows, AXES[::-1], split_axis=0, concat_axis=0, tiled=True)  36.6 us
    all_to_all x4, starting transfers between devices, exchange(): lax.all_to_all(rows, AXES[::-1], split_axis=0, concat_axis=0, tiled=True)  17.8 us
    pallas_call x2, Pallas kernels, synthesize(): pl.pallas_call(functools.partial(synthesis_kernel, slots, levels, fields,...  13.4 us
    ppermute x3, waiting for transfers between devices, across_halves(): lax.ppermute(value, 'grp', [(p, (p + planes // 2) % planes) for p in rang...  9.91 us
    pallas_call x1, Pallas kernels, trig_tables(): pl.pallas_call(trig_kernel, grid=(depth // rows,), in_specs=[pl.BlockSpec...  9.04 us
  transfers between devices with their start and end apart: 37, of which 22 were waited for; matrix products, arithmetic and copies ran while one was open for 5% of the time, Pallas kernels for 32%

profile of v8, /device:TPU:0, one launch (start us, length us, event | category | flops | bytes accessed | tf_op | source)
XLA Modules:
  0.0 302.5 jit_solution(7955517048409127884)
XLA Ops:
  2.0 4.1 %collective-permute-start = (bf16[256,768]{1,0:T(8,128)(2,1)}, bf16[256,768]{1,0:T(8,128)(2,1)S(1)}, u32[]{:S(2)}, u32[]{:S(2)}) collective-permute-start(bf16[256,768]{1,0:T(8,128)(2,1)} %get-tuple-element.43.refs_0_), channel_id=1, source_target_pairs={{0,2},{1,3},{2,0},{3,1},{4,6},{5,7},{6,4},{7,5},{8,10},{9,11},{10,... | collective-permute-start | bytes 1179656 | tf_op jit(solution)/shard_map/ppermute | solution.py:539
  6.1 7.5 %synthesis.2 = bf16[1024,1536]{1,0:T(8,128)(2,1)} custom-call(s32[1]{0:T(128)} %bitcast.1.first_ref, s32[640]{0:T(1024)} %owner_ref.3, bf16[20,128,640]{2,1,0:T(8,128)(2,1)} %bitcast.25, bf16[20,640,640]{2,1,0:T(8,128)(2,1)} %table_ref.7), custom_call_target="tpu_custom_call" | custom-call | flops 2013265920 | bytes 13631488 | tf_op jit(solution)/shard_map/synthesis/pallas_call | solution.py:81
  14.6 5.9 %synthesis.3 = bf16[1024,1024]{1,0:T(8,128)(2,1)} custom-call(s32[1]{0:T(128)} %bitcast.1.first_ref, s32[640]{0:T(1024)} %owner_ref.3, bf16[20,128,640]{2,1,0:T(8,128)(2,1)} %bitcast.26, bf16[20,640,640]{2,1,0:T(8,128)(2,1)} %table_ref.7), custom_call_target="tpu_custom_call" | custom-call | flops 1342177280 | bytes 9961472 | tf_op jit(solution)/shard_map/synthesis/pallas_call | solution.py:81
  20.5 8.4 %collective-permute-done.refs_2_ = bf16[256,768]{1,0:T(8,128)(2,1)S(1)} collective-permute-done((bf16[256,768]{1,0:T(8,128)(2,1)}, bf16[256,768]{1,0:T(8,128)(2,1)S(1)}, u32[]{:S(2)}, u32[]{:S(2)}) %collective-permute-start) | collective-permute-done | bytes 393248 | tf_op jit(solution)/shard_map/ppermute | solution.py:539
  29.6 5.2 %all-to-all-start = ((bf16[32,32,1536]{2,1,0:T(8,128)(2,1)}), bf16[32,32,1536]{2,1,0:T(8,128)(2,1)}, u32[]{:S(2)}, u32[]{:S(2)}) async-start(bf16[32,32,1536]{2,1,0:T(8,128)(2,1)} %bitcast.27), calls=%async_computation | async-start | bytes 6291456 | tf_op jit(solution)/shard_map/all_to_all | solution.py:618
  47.8 11.7 %collective-permute-done.3 = bf16[16,2560]{1,0:T(8,128)(2,1)S(1)} collective-permute-done((bf16[16,2560]{1,0:T(8,128)(2,1)}, bf16[16,2560]{1,0:T(8,128)(2,1)S(1)}, u32[]{:S(2)}, u32[]{:S(2)}) %collective-permute-start.3) | collective-permute-done | bytes 81952 | tf_op jit(solution)/shard_map/ppermute | solution.py:553
  64.3 4.6 %collective-permute-done.7 = bf16[16,2560]{1,0:T(8,128)(2,1)S(1)} collective-permute-done((bf16[16,2560]{1,0:T(8,128)(2,1)}, bf16[16,2560]{1,0:T(8,128)(2,1)S(1)}, u32[]{:S(2)}, u32[]{:S(2)}) %collective-permute-start.7) | collective-permute-done | bytes 81952 | tf_op jit(solution)/shard_map/ppermute | solution.py:553
  72.6 16.5 %collective-permute-done.9 = bf16[16,2560]{1,0:T(8,128)(2,1)S(1)} collective-permute-done((bf16[16,2560]{1,0:T(8,128)(2,1)}, bf16[16,2560]{1,0:T(8,128)(2,1)S(1)}, u32[]{:S(2)}, u32[]{:S(2)}) %collective-permute-start.9) | collective-permute-done | bytes 81952 | tf_op jit(solution)/shard_map/ppermute | solution.py:553
  97.8 4.1 %collective-permute-done.15 = bf16[16,2560]{1,0:T(8,128)(2,1)S(1)} collective-permute-done((bf16[16,2560]{1,0:T(8,128)(2,1)S(1)}, bf16[16,2560]{1,0:T(8,128)(2,1)S(1)}, u32[]{:S(2)}, u32[]{:S(2)}) %collective-permute-start.15) | collective-permute-done | bytes 81952 | tf_op jit(solution)/shard_map/ppermute | solution.py:553
  107.6 4.6 %all-to-all-start.1 = ((bf16[32,32,1024]{2,1,0:T(8,128)(2,1)}), bf16[32,32,1024]{2,1,0:T(8,128)(2,1)}, u32[]{:S(2)}, u32[]{:S(2)}) async-start(bf16[32,32,1024]{2,1,0:T(8,128)(2,1)} %bitcast.12), calls=%async_computation.1 | async-start | bytes 4194304 | tf_op jit(solution)/shard_map/all_to_all | solution.py:618
  114.2 3.8 %fusion = (f32[1280,128]{1,0:T(8,128)}, f32[1280,128]{1,0:T(8,128)}) fusion(f32[1280]{0:T(1024)S(1)} %convert_element_type.24), kind=kLoop, calls=%fused_computation.2 | loop fusion | flops 983040 | bytes 1315840 | tf_op jit(solution)/shard_map/sin | solution.py:593
  119.1 9.0 %trig.1 = (bf16[1280,2560]{1,0:T(8,128)(2,1)}, bf16[2560,1280]{1,0:T(8,128)(2,1)}) custom-call(f32[1280,4]{1,0:T(8,128)} %copy.38.small_ref, f32[1280,128]{1,0:T(8,128)} %get-tuple-element.68.cos_turn_ref, f32[1280,128]{1,0:T(8,128)} %get-tuple-element.69.sin_turn_ref), custom_call_target="tpu_custom_call" | custom-call | flops 39321600 | bytes 13107200 | tf_op jit(solution)/shard_map/trig/pallas_call | solution.py:597
  128.2 31.1 %longitudes.3 = (bf16[1024,1536]{1,0:T(8,128)(2,1)}, bf16[256,1536]{1,0:T(8,128)(2,1)}) custom-call(bf16[1024,1536]{1,0:T(8,128)(2,1)} %bitcast.11.rows_ref, bf16[256,2560]{1,0:T(8,128)(2,1)} %copy-done.21, bf16[2560,1280]{1,0:T(8,128)(2,1)} %get-tuple-element.70.by_lon_ref, bf16[1280,2560]{1,0:T(8,128)(2,1)} %get-tuple-element.71.by_wave_ref), custom_call_target="tpu_custom_call" | custom-call | flops 20132659200 | bytes 20971520 | tf_op jit(solution)/shard_map/longitudes/pallas_call | solution.py:137
  160.9 4.3 %all-to-all-start.2 = ((bf16[32,32,1536]{2,1,0:T(8,128)(2,1)}), bf16[32,32,1536]{2,1,0:T(8,128)(2,1)}, u32[]{:S(2)}, u32[]{:S(2)}) async-start(bf16[32,32,1536]{2,1,0:T(8,128)(2,1)} %bitcast.28), calls=%async_computation.2 | async-start | bytes 6291456 | tf_op jit(solution)/shard_map/all_to_all | solution.py:618
  165.3 22.0 %longitudes.2 = (bf16[1024,1024]{1,0:T(8,128)(2,1)}, bf16[256,1024]{1,0:T(8,128)(2,1)}) custom-call(bf16[1024,1024]{1,0:T(8,128)(2,1)} %bitcast.13.rows_ref, bf16[256,2560]{1,0:T(8,128)(2,1)} %copy-done.21, bf16[2560,1280]{1,0:T(8,128)(2,1)} %get-tuple-element.70.by_lon_ref, bf16[1280,2560]{1,0:T(8,128)(2,1)} %get-tuple-element.71.by_wave_ref), custom_call_target="tpu_custom_call" | custom-call | flops 13421772800 | bytes 18350080 | tf_op jit(solution)/shard_map/longitudes/pallas_call | solution.py:137
  195.2 5.4 %collective-permute-start.23 = (bf16[16,2560]{1,0:T(8,128)(2,1)S(1)}, bf16[16,2560]{1,0:T(8,128)(2,1)S(1)}, u32[]{:S(2)}, u32[]{:S(2)}) collective-permute-start(bf16[16,2560]{1,0:T(8,128)(2,1)S(1)} %get-tuple-element.91), channel_id=1, source_target_pairs={{0,28},{1,29},{2,30},{3,31},{4,24},{5,25},{6,26},{7,27},{8,20},{9,... | collective-permute-start | bytes 245768 | tf_op jit(solution)/shard_map/ppermute | solution.py:553
  202.8 4.7 %collective-permute-start.26 = (bf16[16,2560]{1,0:T(8,128)(2,1)S(1)}, bf16[16,2560]{1,0:T(8,128)(2,1)S(1)}, u32[]{:S(2)}, u32[]{:S(2)}) collective-permute-start(bf16[16,2560]{1,0:T(8,128)(2,1)S(1)} %get-tuple-element.88), channel_id=1, source_target_pairs={{0,9},{1,8},{2,11},{3,10},{4,13},{5,12},{6,15},{7,14},{8,1},{9,0},... | collective-permute-start | bytes 245768 | tf_op jit(solution)/shard_map/ppermute | solution.py:553
  209.0 4.3 %collective-permute-start.28 = (bf16[16,2560]{1,0:T(8,128)(2,1)S(1)}, bf16[16,2560]{1,0:T(8,128)(2,1)S(1)}, u32[]{:S(2)}, u32[]{:S(2)}) collective-permute-start(bf16[16,2560]{1,0:T(8,128)(2,1)S(1)} %get-tuple-element.86), channel_id=1, source_target_pairs={{0,17},{1,16},{2,19},{3,18},{4,21},{5,20},{6,23},{7,22},{8,25},{9,... | collective-permute-start | bytes 245768 | tf_op jit(solution)/shard_map/ppermute | solution.py:553
  213.4 5.6 %collective-permute-done.24.refs_12_ = bf16[16,2560]{1,0:T(8,128)(2,1)S(1)} collective-permute-done((bf16[16,2560]{1,0:T(8,128)(2,1)S(1)}, bf16[16,2560]{1,0:T(8,128)(2,1)S(1)}, u32[]{:S(2)}, u32[]{:S(2)}) %collective-permute-start.24) | collective-permute-done | bytes 81952 | tf_op jit(solution)/shard_map/ppermute | solution.py:553
  227.7 4.6 %collective-permute-done.30.refs_18_ = bf16[16,2560]{1,0:T(8,128)(2,1)S(1)} collective-permute-done((bf16[16,2560]{1,0:T(8,128)(2,1)S(1)}, bf16[16,2560]{1,0:T(8,128)(2,1)S(1)}, u32[]{:S(2)}, u32[]{:S(2)}) %collective-permute-start.30) | collective-permute-done | bytes 81952 | tf_op jit(solution)/shard_map/ppermute | solution.py:553
  250.0 5.4 %fold.1.folded_ref = bf16[16,256,384]{2,1,0:T(8,128)(2,1)} custom-call(bf16[1024,1536]{1,0:T(8,128)(2,1)} %bitcast.15.arrived_ref), custom_call_target="tpu_custom_call" | custom-call | flops 3145728 | bytes 6291456 | tf_op jit(solution)/shard_map/fold/pallas_call | solution.py:344
  255.3 8.5 %analysis.1.base_ref = f32[20,128,640]{2,1,0:T(8,128)} custom-call(bf16[16,256,384]{2,1,0:T(8,128)(2,1)} %fold.1.folded_ref, f32[20,1,640]{2,1,0:T(1,128)} %get-tuple-element.106.even_ref, f32[20,1,640]{2,1,0:T(1,128)} %get-tuple-element.105.odd_ref, bf16[20,640,640]{2,1,0:T(8,128)(2,1)} %table_ref.7, bf16[20,640,640]{2,1,0:T(8,128)(2,1)} %table_ref.7, ...), custom_call_target="tpu_custom_call" | custom-call | flops 2516582400 | bytes 20316160 | tf_op jit(solution)/shard_map/analysis/pallas_call | solution.py:387
  263.8 29.8 %all-to-all-done.3 = bf16[32,32,1024]{2,1,0:T(8,128)(2,1)} async-done(((bf16[32,32,1024]{2,1,0:T(8,128)(2,1)}), bf16[32,32,1024]{2,1,0:T(8,128)(2,1)}, u32[]{:S(2)}, u32[]{:S(2)}) %all-to-all-start.3) | async-done | bytes 2097184 | tf_op jit(solution)/shard_map/all_to_all | solution.py:618
  295.8 6.5 %closing.1 = f32[20,128,640]{2,1,0:T(8,128)} custom-call(s32[1]{0:T(128)} %bitcast.hemi_ref, bf16[1024,1024]{1,0:T(8,128)(2,1)} %bitcast.17.arrived_ref, bf16[20,640,640]{2,1,0:T(8,128)(2,1)} %table_ref.7, f32[20,128,640]{2,1,0:T(8,128)} %analysis.1.base_ref, f32[20,1,640]{2,1,0:T(1,128)} %get-tuple-element.106.even_ref, ...), custom_call_target="tpu_custom_call", output_to_operand_aliasing={{}: (3, {})} | custom-call | flops 1677721600 | bytes 15204352 | tf_op jit(solution)/shard_map/closing/pallas_call | solution.py:511
  (163 shorter events, 84.4 us)
Async XLA Ops:
  2.0 26.9 %collective-permute-start = (bf16[256,768]{1,0:T(8,128)(2,1)}, bf16[256,768]{1,0:T(8,128)(2,1)S(1)}, u32[]{:S(2)}, u32[]{:S(2)}) collective-permute-start(bf16[256,768]{1,0:T(8,128)(2,1)} %get-tuple-element.43.refs_0_), channel_id=1, source_target_pairs={{0,2},{1,3},{2,0},{3,1},{4,6},{5,7},{6,4},{7,5},{8,10},{9,11},{10,... | collective-permute-start | bytes 1179656 | tf_op jit(solution)/shard_map/ppermute | solution.py:539
  13.7 22.5 %collective-permute-start.1 = (bf16[128,768]{1,0:T(8,128)(2,1)S(1)}, bf16[128,768]{1,0:T(8,128)(2,1)S(1)}, u32[]{:S(2)}, u32[]{:S(2)}) collective-permute-start(bf16[128,768]{1,0:T(8,128)(2,1)S(1)} %copy-done.2), channel_id=1, source_target_pairs={{0,2},{1,3},{2,0},{3,1},{4,6},{5,7},{6,4},{7,5},{8,10},{9,11},{10,... | collective-permute-start | bytes 589832 | tf_op jit(solution)/shard_map/ppermute | solution.py:539
  29.6 77.9 %all-to-all-start = ((bf16[32,32,1536]{2,1,0:T(8,128)(2,1)}), bf16[32,32,1536]{2,1,0:T(8,128)(2,1)}, u32[]{:S(2)}, u32[]{:S(2)}) async-start(bf16[32,32,1536]{2,1,0:T(8,128)(2,1)} %bitcast.27), calls=%async_computation | async-start | bytes 6291456 | tf_op jit(solution)/shard_map/all_to_all | solution.py:618
  41.7 17.8 %collective-permute-start.3 = (bf16[16,2560]{1,0:T(8,128)(2,1)}, bf16[16,2560]{1,0:T(8,128)(2,1)S(1)}, u32[]{:S(2)}, u32[]{:S(2)}) collective-permute-start(bf16[16,2560]{1,0:T(8,128)(2,1)} %get-tuple-element.50), channel_id=1, source_target_pairs={{0,8},{1,9},{2,10},{3,11},{4,12},{5,13},{6,14},{7,15},{8,0},{9,1},... | collective-permute-start | bytes 245768 | tf_op jit(solution)/shard_map/ppermute | solution.py:553
  43.4 17.0 %collective-permute-start.4 = (bf16[16,2560]{1,0:T(8,128)(2,1)}, bf16[16,2560]{1,0:T(8,128)(2,1)S(1)}, u32[]{:S(2)}, u32[]{:S(2)}) collective-permute-start(bf16[16,2560]{1,0:T(8,128)(2,1)} %get-tuple-element.51), channel_id=1, source_target_pairs={{0,12},{1,13},{2,14},{3,15},{4,8},{5,9},{6,10},{7,11},{8,4},{9,5},... | collective-permute-start | bytes 245768 | tf_op jit(solution)/shard_map/ppermute | solution.py:553
  43.4 17.4 %collective-permute-start.5 = (bf16[16,2560]{1,0:T(8,128)(2,1)}, bf16[16,2560]{1,0:T(8,128)(2,1)S(1)}, u32[]{:S(2)}, u32[]{:S(2)}) collective-permute-start(bf16[16,2560]{1,0:T(8,128)(2,1)} %get-tuple-element.52), channel_id=1, source_target_pairs={{0,16},{1,17},{2,18},{3,19},{4,20},{5,21},{6,22},{7,23},{8,24},{9,... | collective-permute-start | bytes 245768 | tf_op jit(solution)/shard_map/ppermute | solution.py:553
  45.1 18.0 %collective-permute-start.6 = (bf16[16,2560]{1,0:T(8,128)(2,1)}, bf16[16,2560]{1,0:T(8,128)(2,1)S(1)}, u32[]{:S(2)}, u32[]{:S(2)}) collective-permute-start(bf16[16,2560]{1,0:T(8,128)(2,1)} %get-tuple-element.53), channel_id=1, source_target_pairs={{0,20},{1,21},{2,22},{3,23},{4,16},{5,17},{6,18},{7,19},{8,28},{9,... | collective-permute-start | bytes 245768 | tf_op jit(solution)/shard_map/ppermute | solution.py:553
  45.2 23.7 %collective-permute-start.7 = (bf16[16,2560]{1,0:T(8,128)(2,1)}, bf16[16,2560]{1,0:T(8,128)(2,1)S(1)}, u32[]{:S(2)}, u32[]{:S(2)}) collective-permute-start(bf16[16,2560]{1,0:T(8,128)(2,1)} %get-tuple-element.54), channel_id=1, source_target_pairs={{0,24},{1,25},{2,26},{3,27},{4,28},{5,29},{6,30},{7,31},{8,16},{9,... | collective-permute-start | bytes 245768 | tf_op jit(solution)/shard_map/ppermute | solution.py:553
  60.3 28.7 %collective-permute-start.9 = (bf16[16,2560]{1,0:T(8,128)(2,1)}, bf16[16,2560]{1,0:T(8,128)(2,1)S(1)}, u32[]{:S(2)}, u32[]{:S(2)}) collective-permute-start(bf16[16,2560]{1,0:T(8,128)(2,1)} %get-tuple-element.56), channel_id=1, source_target_pairs={{0,1},{1,0},{2,3},{3,2},{4,5},{5,4},{6,7},{7,6},{8,9},{9,8},{10,11... | collective-permute-start | bytes 245768 | tf_op jit(solution)/shard_map/ppermute | solution.py:553
  60.8 30.1 %collective-permute-start.10 = (bf16[16,2560]{1,0:T(8,128)(2,1)}, bf16[16,2560]{1,0:T(8,128)(2,1)S(1)}, u32[]{:S(2)}, u32[]{:S(2)}) collective-permute-start(bf16[16,2560]{1,0:T(8,128)(2,1)} %get-tuple-element.57), channel_id=1, source_target_pairs={{0,5},{1,4},{2,7},{3,6},{4,1},{5,0},{6,3},{7,2},{8,13},{9,12},{10,... | collective-permute-start | bytes 245768 | tf_op jit(solution)/shard_map/ppermute | solution.py:553
  63.1 31.1 %collective-permute-start.11 = (bf16[16,2560]{1,0:T(8,128)(2,1)}, bf16[16,2560]{1,0:T(8,128)(2,1)S(1)}, u32[]{:S(2)}, u32[]{:S(2)}) collective-permute-start(bf16[16,2560]{1,0:T(8,128)(2,1)} %get-tuple-element.58), channel_id=1, source_target_pairs={{0,9},{1,8},{2,11},{3,10},{4,13},{5,12},{6,15},{7,14},{8,1},{9,0},... | collective-permute-start | bytes 245768 | tf_op jit(solution)/shard_map/ppermute | solution.py:553
  68.9 26.6 %collective-permute-start.12 = (bf16[16,2560]{1,0:T(8,128)(2,1)}, bf16[16,2560]{1,0:T(8,128)(2,1)S(1)}, u32[]{:S(2)}, u32[]{:S(2)}) collective-permute-start(bf16[16,2560]{1,0:T(8,128)(2,1)} %get-tuple-element.59), channel_id=1, source_target_pairs={{0,13},{1,12},{2,15},{3,14},{4,9},{5,8},{6,11},{7,10},{8,5},{9,4},... | collective-permute-start | bytes 245768 | tf_op jit(solution)/shard_map/ppermute | solution.py:553
  72.6 23.5 %collective-permute-start.13 = (bf16[16,2560]{1,0:T(8,128)(2,1)}, bf16[16,2560]{1,0:T(8,128)(2,1)S(1)}, u32[]{:S(2)}, u32[]{:S(2)}) collective-permute-start(bf16[16,2560]{1,0:T(8,128)(2,1)} %get-tuple-element.60), channel_id=1, source_target_pairs={{0,17},{1,16},{2,19},{3,18},{4,21},{5,20},{6,23},{7,22},{8,25},{9,... | collective-permute-start | bytes 245768 | tf_op jit(solution)/shard_map/ppermute | solution.py:553
  107.6 53.3 %all-to-all-start.1 = ((bf16[32,32,1024]{2,1,0:T(8,128)(2,1)}), bf16[32,32,1024]{2,1,0:T(8,128)(2,1)}, u32[]{:S(2)}, u32[]{:S(2)}) async-start(bf16[32,32,1024]{2,1,0:T(8,128)(2,1)} %bitcast.12), calls=%async_computation.1 | async-start | bytes 4194304 | tf_op jit(solution)/shard_map/all_to_all | solution.py:618
  160.9 77.4 %all-to-all-start.2 = ((bf16[32,32,1536]{2,1,0:T(8,128)(2,1)}), bf16[32,32,1536]{2,1,0:T(8,128)(2,1)}, u32[]{:S(2)}, u32[]{:S(2)}) async-start(bf16[32,32,1536]{2,1,0:T(8,128)(2,1)} %bitcast.28), calls=%async_computation.2 | async-start | bytes 6291456 | tf_op jit(solution)/shard_map/all_to_all | solution.py:618
  192.6 14.8 %collective-permute-start.22 = (bf16[16,2560]{1,0:T(8,128)(2,1)S(1)}, bf16[16,2560]{1,0:T(8,128)(2,1)S(1)}, u32[]{:S(2)}, u32[]{:S(2)}) collective-permute-start(bf16[16,2560]{1,0:T(8,128)(2,1)S(1)} %get-tuple-element.92), channel_id=1, source_target_pairs={{0,24},{1,25},{2,26},{3,27},{4,28},{5,29},{6,30},{7,31},{8,16},{9,... | collective-permute-start | bytes 245768 | tf_op jit(solution)/shard_map/ppermute | solution.py:553
  195.2 13.8 %collective-permute-start.23 = (bf16[16,2560]{1,0:T(8,128)(2,1)S(1)}, bf16[16,2560]{1,0:T(8,128)(2,1)S(1)}, u32[]{:S(2)}, u32[]{:S(2)}) collective-permute-start(bf16[16,2560]{1,0:T(8,128)(2,1)S(1)} %get-tuple-element.91), channel_id=1, source_target_pairs={{0,28},{1,29},{2,30},{3,31},{4,24},{5,25},{6,26},{7,27},{8,20},{9,... | collective-permute-start | bytes 245768 | tf_op jit(solution)/shard_map/ppermute | solution.py:553
  201.2 17.8 %collective-permute-start.24 = (bf16[16,2560]{1,0:T(8,128)(2,1)S(1)}, bf16[16,2560]{1,0:T(8,128)(2,1)S(1)}, u32[]{:S(2)}, u32[]{:S(2)}) collective-permute-start(bf16[16,2560]{1,0:T(8,128)(2,1)S(1)} %get-tuple-element.90), channel_id=1, source_target_pairs={{0,1},{1,0},{2,3},{3,2},{4,5},{5,4},{6,7},{7,6},{8,9},{9,8},{10,11... | collective-permute-start | bytes 245768 | tf_op jit(solution)/shard_map/ppermute | solution.py:553
  201.2 19.9 %collective-permute-start.25 = (bf16[16,2560]{1,0:T(8,128)(2,1)S(1)}, bf16[16,2560]{1,0:T(8,128)(2,1)S(1)}, u32[]{:S(2)}, u32[]{:S(2)}) collective-permute-start(bf16[16,2560]{1,0:T(8,128)(2,1)S(1)} %get-tuple-element.89), channel_id=1, source_target_pairs={{0,5},{1,4},{2,7},{3,6},{4,1},{5,0},{6,3},{7,2},{8,13},{9,12},{10,... | collective-permute-start | bytes 245768 | tf_op jit(solution)/shard_map/ppermute | solution.py:553
  202.8 21.6 %collective-permute-start.26 = (bf16[16,2560]{1,0:T(8,128)(2,1)S(1)}, bf16[16,2560]{1,0:T(8,128)(2,1)S(1)}, u32[]{:S(2)}, u32[]{:S(2)}) collective-permute-start(bf16[16,2560]{1,0:T(8,128)(2,1)S(1)} %get-tuple-element.88), channel_id=1, source_target_pairs={{0,9},{1,8},{2,11},{3,10},{4,13},{5,12},{6,15},{7,14},{8,1},{9,0},... | collective-permute-start | bytes 245768 | tf_op jit(solution)/shard_map/ppermute | solution.py:553
  207.4 18.1 %collective-permute-start.27 = (bf16[16,2560]{1,0:T(8,128)(2,1)S(1)}, bf16[16,2560]{1,0:T(8,128)(2,1)S(1)}, u32[]{:S(2)}, u32[]{:S(2)}) collective-permute-start(bf16[16,2560]{1,0:T(8,128)(2,1)S(1)} %get-tuple-element.87), channel_id=1, source_target_pairs={{0,13},{1,12},{2,15},{3,14},{4,9},{5,8},{6,11},{7,10},{8,5},{9,4},... | collective-permute-start | bytes 245768 | tf_op jit(solution)/shard_map/ppermute | solution.py:553
  209.0 16.9 %collective-permute-start.28 = (bf16[16,2560]{1,0:T(8,128)(2,1)S(1)}, bf16[16,2560]{1,0:T(8,128)(2,1)S(1)}, u32[]{:S(2)}, u32[]{:S(2)}) collective-permute-start(bf16[16,2560]{1,0:T(8,128)(2,1)S(1)} %get-tuple-element.86), channel_id=1, source_target_pairs={{0,17},{1,16},{2,19},{3,18},{4,21},{5,20},{6,23},{7,22},{8,25},{9,... | collective-permute-start | bytes 245768 | tf_op jit(solution)/shard_map/ppermute | solution.py:553
  238.4 55.2 %all-to-all-start.3 = ((bf16[32,32,1024]{2,1,0:T(8,128)(2,1)}), bf16[32,32,1024]{2,1,0:T(8,128)(2,1)}, u32[]{:S(2)}, u32[]{:S(2)}) async-start(bf16[32,32,1024]{2,1,0:T(8,128)(2,1)} %bitcast.29), calls=%async_computation.3 | async-start | bytes 4194304 | tf_op jit(solution)/shard_map/all_to_all | solution.py:618
  247.6 47.6 %collective-permute-start.32 = (bf16[384,128]{1,0:T(8,128)(2,1)}, bf16[384,128]{1,0:T(8,128)(2,1)S(1)}, u32[]{:S(2)}, u32[]{:S(2)}) collective-permute-start(bf16[384,128]{1,0:T(8,128)(2,1)} %get-tuple-element.80), channel_id=1, source_target_pairs={{0,2},{1,3},{2,0},{3,1},{4,6},{5,7},{6,4},{7,5},{8,10},{9,11},{10,... | collective-permute-start | bytes 294920 | tf_op jit(solution)/shard_map/ppermute | solution.py:539
  (39 other events, 651.8 us)

commit v9 on v7

--- a/solution.py
+++ b/solution.py
@@ -63,7 +63,7 @@
     for field in range(fields):
         for tile in range(tiles):
             lanes = pl.ds((field * tiles + tile) * LANES, LANES)
-            rows = rows_ref[field, tile].reshape(2 * levels, stride, LANES)[:, : 2 * slots]
+            rows = rows_ref[field, tile, : 2 * levels * stride].reshape(2 * levels, stride, LANES)[:, : 2 * slots]
             out_ref[:, lanes] = rows.reshape(out_ref.shape[0], LANES).astype(out_ref.dtype)
 
 
@@ -84,7 +84,7 @@
         out_specs=pl.BlockSpec(shape, lambda: (0, 0)),
         out_shape=jax.ShapeDtypeStruct(shape, jnp.bfloat16),
         scratch_shapes=[
-            pltpu.VMEM((fields, tiles, 2 * levels * padded(slots), LANES), jnp.float32),
+            pltpu.VMEM((fields, tiles, (2 * levels + 1) * padded(slots), LANES), jnp.float32),
             pltpu.SemaphoreType.DMA((2 * len(least),)),
             *held,
         ],
@@ -203,7 +203,7 @@
     pack_refs, out_refs, rows_ref = refs[:4], refs[4:-1], refs[-1]
     tiles = rows_ref.shape[1]
     half_lat = tiles * LANES
-    stride = rows_ref.shape[2] // levels
+    stride = out_refs[0].shape[0]
     degree = lax.broadcasted_iota(jnp.int32, (1, LANES), 1)
     for slot in range(8):
         local = slot % 4
@@ -240,7 +240,7 @@
         in_specs=[pl.BlockSpec(memory_space=pltpu.SMEM)] * 2 + [pl.BlockSpec(x.shape, lambda: (0, 0)) for x in packs],
         out_specs=[pl.BlockSpec(shape, lambda: (0, 0))] * levels,
         out_shape=[jax.ShapeDtypeStruct(shape, jnp.bfloat16)] * levels,
-        scratch_shapes=[pltpu.VMEM((fields, tiles, 16 * levels, LANES), jnp.float32)],
+        scratch_shapes=[pltpu.VMEM((fields, tiles, 16 * (levels + 1), LANES), jnp.float32)],
         compiler_params=pltpu.CompilerParams(vmem_limit_bytes=VMEM_BYTES),
         cost_estimate=pl.CostEstimate(
             flops=16 * 2 * fields * levels * LANES * tiles * LANES, bytes_accessed=12 * packs[0].size, transcendentals=0
@@ -253,7 +253,7 @@
     pack_refs, zonal_refs = refs[:4], refs[4:-3]
     own_out_ref, partner_out_ref, rows_ref = refs[-3:]
     tiles = rows_ref.shape[1]
-    stride = rows_ref.shape[2] // levels
+    stride = zonal_refs[0].shape[0]
     for apart, zonal_ref in enumerate(zonal_refs):
         rows = pl.ds(pl.multiple_of((place_ref[1] ^ apart) * stride, stride), stride)
         offset = 0
@@ -302,7 +302,7 @@
         + [pl.BlockSpec(x.shape, lambda: (0, 0)) for x in (*packs, *zonal)],
         out_specs=[out_spec, out_spec],
         out_shape=[jax.ShapeDtypeStruct(shape, jnp.float32), jax.ShapeDtypeStruct(shape, jnp.bfloat16)],
-        scratch_shapes=[pltpu.VMEM((fields, tiles, 16 * levels, LANES), jnp.float32)],
+        scratch_shapes=[pltpu.VMEM((fields, tiles, 16 * (levels + 1), LANES), jnp.float32)],
         compiler_params=pltpu.CompilerParams(vmem_limit_bytes=VMEM_BYTES),
         cost_estimate=pl.CostEstimate(
             flops=16 * 2 * fields * levels * LANES * tiles * LANES, bytes_accessed=12 * packs[0].size, transcendentals=0
@@ -346,7 +346,7 @@
         in_specs=[pl.BlockSpec((rows, width), lambda: (0, 0))],
         out_specs=pl.BlockSpec(shape, lambda: (0, 0, 0)),
         out_shape=jax.ShapeDtypeStruct(shape, jnp.bfloat16),
-        scratch_shapes=[pltpu.VMEM((fields, tiles, 2 * levels * padded(slots), LANES), jnp.float32)],
+        scratch_shapes=[pltpu.VMEM((fields, tiles, (2 * levels + 1) * padded(slots), LANES), jnp.float32)],
         compiler_params=pltpu.CompilerParams(vmem_limit_bytes=VMEM_BYTES),
         cost_estimate=pl.CostEstimate(flops=2 * rows * width, bytes_accessed=4 * rows * width, transcendentals=0),
         name="fold",
@@ -502,7 +502,7 @@
     block = 4
     rows, width = arrived.shape
     tiles = chunk[1]
-    half = pltpu.VMEM((fields, tiles, levels * padded(block * len(least)), LANES), jnp.float32)
+    half = pltpu.VMEM((fields, tiles, (levels + 1) * padded(block * len(least)), LANES), jnp.float32)
     held = []
     for start in least:
         held.append(pltpu.VMEM((block, degrees - start, tiles * LANES), jnp.bfloat16))

time: 303 us -> 303 us (level)
  no operation moved by 1% of the time
where the time goes in v9:
time: 303 us
  waiting for transfers between devices  111 us (37%)
  Pallas kernels  105 us (35%)
  starting transfers between devices  70.3 us (23%)
  local copies, waits for them, and re-layouts  9.25 us (3%)
  other arithmetic  6.4 us (2%)
    ppermute x30, waiting for transfers between devices, within_half(): moved.append(lax.ppermute(parts[x], AXES, pairs))  64.3 us
    pallas_call x2, Pallas kernels, longitudes(): pl.pallas_call(functools.partial(longitude_kernel, fields, chunk, 1.0 / m...  53.1 us
    ppermute x30, starting transfers between devices, within_half(): moved.append(lax.ppermute(parts[x], AXES, pairs))  45.9 us
    all_to_all x4, waiting for transfers between devices, exchange(): lax.all_to_all(rows, AXES[::-1], split_axis=0, concat_axis=0, tiled=True)  36.5 us
    all_to_all x4, starting transfers between devices, exchange(): lax.all_to_all(rows, AXES[::-1], split_axis=0, concat_axis=0, tiled=True)  17.8 us
    pallas_call x2, Pallas kernels, synthesize(): pl.pallas_call(functools.partial(synthesis_kernel, slots, levels, fields,...  13.3 us
    ppermute x3, waiting for transfers between devices, across_halves(): lax.ppermute(value, 'grp', [(p, (p + planes // 2) % planes) for p in rang...  10.1 us
    pallas_call x1, Pallas kernels, trig_tables(): pl.pallas_call(trig_kernel, grid=(depth // rows,), in_specs=[pl.BlockSpec...  9.06 us
  transfers between devices with their start and end apart: 37, of which 22 were waited for; matrix products, arithmetic and copies ran while one was open for 4% of the time, Pallas kernels for 32%

profile of v9, /device:TPU:0, one launch (start us, length us, event | category | flops | bytes accessed | tf_op | source)
XLA Modules:
  0.0 302.5 jit_solution(2172764585945559839)
XLA Ops:
  2.0 4.1 %collective-permute-start = (bf16[256,768]{1,0:T(8,128)(2,1)}, bf16[256,768]{1,0:T(8,128)(2,1)S(1)}, u32[]{:S(2)}, u32[]{:S(2)}) collective-permute-start(bf16[256,768]{1,0:T(8,128)(2,1)} %get-tuple-element.42.refs_0_), channel_id=1, source_target_pairs={{0,2},{1,3},{2,0},{3,1},{4,6},{5,7},{6,4},{7,5},{8,10},{9,11},{10,... | collective-permute-start | bytes 1179656 | tf_op jit(solution)/shard_map/ppermute | solution.py:539
  6.4 7.4 %synthesis.2 = bf16[1024,1536]{1,0:T(8,128)(2,1)} custom-call(s32[1]{0:T(128)} %bitcast.1.first_ref, s32[640]{0:T(1024)} %owner_ref.3, bf16[20,128,640]{2,1,0:T(8,128)(2,1)} %bitcast.25, bf16[20,640,640]{2,1,0:T(8,128)(2,1)} %table_ref.7), custom_call_target="tpu_custom_call" | custom-call | flops 2013265920 | bytes 13631488 | tf_op jit(solution)/shard_map/synthesis/pallas_call | solution.py:81
  14.5 5.9 %synthesis.3 = bf16[1024,1024]{1,0:T(8,128)(2,1)} custom-call(s32[1]{0:T(128)} %bitcast.1.first_ref, s32[640]{0:T(1024)} %owner_ref.3, bf16[20,128,640]{2,1,0:T(8,128)(2,1)} %bitcast.26, bf16[20,640,640]{2,1,0:T(8,128)(2,1)} %table_ref.7), custom_call_target="tpu_custom_call" | custom-call | flops 1342177280 | bytes 9961472 | tf_op jit(solution)/shard_map/synthesis/pallas_call | solution.py:81
  20.4 8.5 %collective-permute-done.refs_2_ = bf16[256,768]{1,0:T(8,128)(2,1)S(1)} collective-permute-done((bf16[256,768]{1,0:T(8,128)(2,1)}, bf16[256,768]{1,0:T(8,128)(2,1)S(1)}, u32[]{:S(2)}, u32[]{:S(2)}) %collective-permute-start) | collective-permute-done | bytes 393248 | tf_op jit(solution)/shard_map/ppermute | solution.py:539
  29.7 5.2 %all-to-all-start = ((bf16[32,32,1536]{2,1,0:T(8,128)(2,1)}), bf16[32,32,1536]{2,1,0:T(8,128)(2,1)}, u32[]{:S(2)}, u32[]{:S(2)}) async-start(bf16[32,32,1536]{2,1,0:T(8,128)(2,1)} %bitcast.27), calls=%async_computation | async-start | bytes 6291456 | tf_op jit(solution)/shard_map/all_to_all | solution.py:618
  47.7 11.8 %collective-permute-done.3 = bf16[16,2560]{1,0:T(8,128)(2,1)S(1)} collective-permute-done((bf16[16,2560]{1,0:T(8,128)(2,1)}, bf16[16,2560]{1,0:T(8,128)(2,1)S(1)}, u32[]{:S(2)}, u32[]{:S(2)}) %collective-permute-start.3) | collective-permute-done | bytes 81952 | tf_op jit(solution)/shard_map/ppermute | solution.py:553
  64.3 4.6 %collective-permute-done.7 = bf16[16,2560]{1,0:T(8,128)(2,1)S(1)} collective-permute-done((bf16[16,2560]{1,0:T(8,128)(2,1)}, bf16[16,2560]{1,0:T(8,128)(2,1)S(1)}, u32[]{:S(2)}, u32[]{:S(2)}) %collective-permute-start.7) | collective-permute-done | bytes 81952 | tf_op jit(solution)/shard_map/ppermute | solution.py:553
  72.6 16.5 %collective-permute-done.9 = bf16[16,2560]{1,0:T(8,128)(2,1)S(1)} collective-permute-done((bf16[16,2560]{1,0:T(8,128)(2,1)}, bf16[16,2560]{1,0:T(8,128)(2,1)S(1)}, u32[]{:S(2)}, u32[]{:S(2)}) %collective-permute-start.9) | collective-permute-done | bytes 81952 | tf_op jit(solution)/shard_map/ppermute | solution.py:553
  97.8 4.1 %collective-permute-done.15 = bf16[16,2560]{1,0:T(8,128)(2,1)S(1)} collective-permute-done((bf16[16,2560]{1,0:T(8,128)(2,1)S(1)}, bf16[16,2560]{1,0:T(8,128)(2,1)S(1)}, u32[]{:S(2)}, u32[]{:S(2)}) %collective-permute-start.15) | collective-permute-done | bytes 81952 | tf_op jit(solution)/shard_map/ppermute | solution.py:553
  107.6 4.6 %all-to-all-start.1 = ((bf16[32,32,1024]{2,1,0:T(8,128)(2,1)}), bf16[32,32,1024]{2,1,0:T(8,128)(2,1)}, u32[]{:S(2)}, u32[]{:S(2)}) async-start(bf16[32,32,1024]{2,1,0:T(8,128)(2,1)} %bitcast.12), calls=%async_computation.1 | async-start | bytes 4194304 | tf_op jit(solution)/shard_map/all_to_all | solution.py:618
  114.2 3.8 %fusion = (f32[1280,128]{1,0:T(8,128)}, f32[1280,128]{1,0:T(8,128)}) fusion(f32[1280]{0:T(1024)S(1)} %convert_element_type.24), kind=kLoop, calls=%fused_computation.2 | loop fusion | flops 983040 | bytes 1315840 | tf_op jit(solution)/shard_map/sin | solution.py:593
  119.1 9.1 %trig.1 = (bf16[1280,2560]{1,0:T(8,128)(2,1)}, bf16[2560,1280]{1,0:T(8,128)(2,1)}) custom-call(f32[1280,4]{1,0:T(8,128)} %copy.38.small_ref, f32[1280,128]{1,0:T(8,128)} %get-tuple-element.66.cos_turn_ref, f32[1280,128]{1,0:T(8,128)} %get-tuple-element.67.sin_turn_ref), custom_call_target="tpu_custom_call" | custom-call | flops 39321600 | bytes 13107200 | tf_op jit(solution)/shard_map/trig/pallas_call | solution.py:597
  128.2 31.1 %longitudes.3 = (bf16[1024,1536]{1,0:T(8,128)(2,1)}, bf16[256,1536]{1,0:T(8,128)(2,1)}) custom-call(bf16[1024,1536]{1,0:T(8,128)(2,1)} %bitcast.11.rows_ref, bf16[256,2560]{1,0:T(8,128)(2,1)} %copy-done.20, bf16[2560,1280]{1,0:T(8,128)(2,1)} %get-tuple-element.68.by_lon_ref, bf16[1280,2560]{1,0:T(8,128)(2,1)} %get-tuple-element.69.by_wave_ref), custom_call_target="tpu_custom_call" | custom-call | flops 20132659200 | bytes 20971520 | tf_op jit(solution)/shard_map/longitudes/pallas_call | solution.py:137
  161.0 4.3 %all-to-all-start.2 = ((bf16[32,32,1536]{2,1,0:T(8,128)(2,1)}), bf16[32,32,1536]{2,1,0:T(8,128)(2,1)}, u32[]{:S(2)}, u32[]{:S(2)}) async-start(bf16[32,32,1536]{2,1,0:T(8,128)(2,1)} %bitcast.28), calls=%async_computation.2 | async-start | bytes 6291456 | tf_op jit(solution)/shard_map/all_to_all | solution.py:618
  165.3 22.0 %longitudes.2 = (bf16[1024,1024]{1,0:T(8,128)(2,1)}, bf16[256,1024]{1,0:T(8,128)(2,1)}) custom-call(bf16[1024,1024]{1,0:T(8,128)(2,1)} %bitcast.13.rows_ref, bf16[256,2560]{1,0:T(8,128)(2,1)} %copy-done.20, bf16[2560,1280]{1,0:T(8,128)(2,1)} %get-tuple-element.68.by_lon_ref, bf16[1280,2560]{1,0:T(8,128)(2,1)} %get-tuple-element.69.by_wave_ref), custom_call_target="tpu_custom_call" | custom-call | flops 13421772800 | bytes 18350080 | tf_op jit(solution)/shard_map/longitudes/pallas_call | solution.py:137
  195.2 5.4 %collective-permute-start.23 = (bf16[16,2560]{1,0:T(8,128)(2,1)S(1)}, bf16[16,2560]{1,0:T(8,128)(2,1)S(1)}, u32[]{:S(2)}, u32[]{:S(2)}) collective-permute-start(bf16[16,2560]{1,0:T(8,128)(2,1)S(1)} %get-tuple-element.89), channel_id=1, source_target_pairs={{0,28},{1,29},{2,30},{3,31},{4,24},{5,25},{6,26},{7,27},{8,20},{9,... | collective-permute-start | bytes 245768 | tf_op jit(solution)/shard_map/ppermute | solution.py:553
  202.8 4.6 %collective-permute-start.26 = (bf16[16,2560]{1,0:T(8,128)(2,1)S(1)}, bf16[16,2560]{1,0:T(8,128)(2,1)S(1)}, u32[]{:S(2)}, u32[]{:S(2)}) collective-permute-start(bf16[16,2560]{1,0:T(8,128)(2,1)S(1)} %get-tuple-element.86), channel_id=1, source_target_pairs={{0,9},{1,8},{2,11},{3,10},{4,13},{5,12},{6,15},{7,14},{8,1},{9,0},... | collective-permute-start | bytes 245768 | tf_op jit(solution)/shard_map/ppermute | solution.py:553
  209.0 4.3 %collective-permute-start.28 = (bf16[16,2560]{1,0:T(8,128)(2,1)S(1)}, bf16[16,2560]{1,0:T(8,128)(2,1)S(1)}, u32[]{:S(2)}, u32[]{:S(2)}) collective-permute-start(bf16[16,2560]{1,0:T(8,128)(2,1)S(1)} %get-tuple-element.84), channel_id=1, source_target_pairs={{0,17},{1,16},{2,19},{3,18},{4,21},{5,20},{6,23},{7,22},{8,25},{9,... | collective-permute-start | bytes 245768 | tf_op jit(solution)/shard_map/ppermute | solution.py:553
  213.4 5.6 %collective-permute-done.24.refs_12_ = bf16[16,2560]{1,0:T(8,128)(2,1)S(1)} collective-permute-done((bf16[16,2560]{1,0:T(8,128)(2,1)S(1)}, bf16[16,2560]{1,0:T(8,128)(2,1)S(1)}, u32[]{:S(2)}, u32[]{:S(2)}) %collective-permute-start.24) | collective-permute-done | bytes 81952 | tf_op jit(solution)/shard_map/ppermute | solution.py:553
  227.7 5.9 %collective-permute-done.30.refs_18_ = bf16[16,2560]{1,0:T(8,128)(2,1)S(1)} collective-permute-done((bf16[16,2560]{1,0:T(8,128)(2,1)S(1)}, bf16[16,2560]{1,0:T(8,128)(2,1)S(1)}, u32[]{:S(2)}, u32[]{:S(2)}) %collective-permute-start.30) | collective-permute-done | bytes 81952 | tf_op jit(solution)/shard_map/ppermute | solution.py:553
  249.9 5.3 %fold.1.folded_ref = bf16[16,256,384]{2,1,0:T(8,128)(2,1)} custom-call(bf16[1024,1536]{1,0:T(8,128)(2,1)} %bitcast.15.arrived_ref), custom_call_target="tpu_custom_call" | custom-call | flops 3145728 | bytes 6291456 | tf_op jit(solution)/shard_map/fold/pallas_call | solution.py:344
  255.3 8.5 %analysis.1.base_ref = f32[20,128,640]{2,1,0:T(8,128)} custom-call(bf16[16,256,384]{2,1,0:T(8,128)(2,1)} %fold.1.folded_ref, f32[20,1,640]{2,1,0:T(1,128)} %get-tuple-element.104.even_ref, f32[20,1,640]{2,1,0:T(1,128)} %get-tuple-element.103.odd_ref, bf16[20,640,640]{2,1,0:T(8,128)(2,1)} %table_ref.7, bf16[20,640,640]{2,1,0:T(8,128)(2,1)} %table_ref.7, ...), custom_call_target="tpu_custom_call" | custom-call | flops 2516582400 | bytes 20316160 | tf_op jit(solution)/shard_map/analysis/pallas_call | solution.py:387
  263.8 29.8 %all-to-all-done.3 = bf16[32,32,1024]{2,1,0:T(8,128)(2,1)} async-done(((bf16[32,32,1024]{2,1,0:T(8,128)(2,1)}), bf16[32,32,1024]{2,1,0:T(8,128)(2,1)}, u32[]{:S(2)}, u32[]{:S(2)}) %all-to-all-start.3) | async-done | bytes 2097184 | tf_op jit(solution)/shard_map/all_to_all | solution.py:618
  295.8 6.5 %closing.1 = f32[20,128,640]{2,1,0:T(8,128)} custom-call(s32[1]{0:T(128)} %bitcast.hemi_ref, bf16[1024,1024]{1,0:T(8,128)(2,1)} %bitcast.17.arrived_ref, bf16[20,640,640]{2,1,0:T(8,128)(2,1)} %table_ref.7, f32[20,128,640]{2,1,0:T(8,128)} %analysis.1.base_ref, f32[20,1,640]{2,1,0:T(1,128)} %get-tuple-element.104.even_ref, ...), custom_call_target="tpu_custom_call", output_to_operand_aliasing={{}: (3, {})} | custom-call | flops 1677721600 | bytes 15204352 | tf_op jit(solution)/shard_map/closing/pallas_call | solution.py:511
  (161 shorter events, 82.9 us)
Async XLA Ops:
  2.0 26.9 %collective-permute-start = (bf16[256,768]{1,0:T(8,128)(2,1)}, bf16[256,768]{1,0:T(8,128)(2,1)S(1)}, u32[]{:S(2)}, u32[]{:S(2)}) collective-permute-start(bf16[256,768]{1,0:T(8,128)(2,1)} %get-tuple-element.42.refs_0_), channel_id=1, source_target_pairs={{0,2},{1,3},{2,0},{3,1},{4,6},{5,7},{6,4},{7,5},{8,10},{9,11},{10,... | collective-permute-start | bytes 1179656 | tf_op jit(solution)/shard_map/ppermute | solution.py:539
  6.1 29.9 %collective-permute-start.1 = (bf16[128,768]{1,0:T(8,128)(2,1)}, bf16[128,768]{1,0:T(8,128)(2,1)S(1)}, u32[]{:S(2)}, u32[]{:S(2)}) collective-permute-start(bf16[128,768]{1,0:T(8,128)(2,1)} %get-tuple-element.45.refs_1_), channel_id=1, source_target_pairs={{0,2},{1,3},{2,0},{3,1},{4,6},{5,7},{6,4},{7,5},{8,10},{9,11},{10,... | collective-permute-start | bytes 589832 | tf_op jit(solution)/shard_map/ppermute | solution.py:539
  29.7 77.9 %all-to-all-start = ((bf16[32,32,1536]{2,1,0:T(8,128)(2,1)}), bf16[32,32,1536]{2,1,0:T(8,128)(2,1)}, u32[]{:S(2)}, u32[]{:S(2)}) async-start(bf16[32,32,1536]{2,1,0:T(8,128)(2,1)} %bitcast.27), calls=%async_computation | async-start | bytes 6291456 | tf_op jit(solution)/shard_map/all_to_all | solution.py:618
  41.6 17.8 %collective-permute-start.3 = (bf16[16,2560]{1,0:T(8,128)(2,1)}, bf16[16,2560]{1,0:T(8,128)(2,1)S(1)}, u32[]{:S(2)}, u32[]{:S(2)}) collective-permute-start(bf16[16,2560]{1,0:T(8,128)(2,1)} %get-tuple-element.48), channel_id=1, source_target_pairs={{0,8},{1,9},{2,10},{3,11},{4,12},{5,13},{6,14},{7,15},{8,0},{9,1},... | collective-permute-start | bytes 245768 | tf_op jit(solution)/shard_map/ppermute | solution.py:553
  43.3 17.1 %collective-permute-start.4 = (bf16[16,2560]{1,0:T(8,128)(2,1)}, bf16[16,2560]{1,0:T(8,128)(2,1)S(1)}, u32[]{:S(2)}, u32[]{:S(2)}) collective-permute-start(bf16[16,2560]{1,0:T(8,128)(2,1)} %get-tuple-element.49), channel_id=1, source_target_pairs={{0,12},{1,13},{2,14},{3,15},{4,8},{5,9},{6,10},{7,11},{8,4},{9,5},... | collective-permute-start | bytes 245768 | tf_op jit(solution)/shard_map/ppermute | solution.py:553
  43.3 17.5 %collective-permute-start.5 = (bf16[16,2560]{1,0:T(8,128)(2,1)}, bf16[16,2560]{1,0:T(8,128)(2,1)S(1)}, u32[]{:S(2)}, u32[]{:S(2)}) collective-permute-start(bf16[16,2560]{1,0:T(8,128)(2,1)} %get-tuple-element.50), channel_id=1, source_target_pairs={{0,16},{1,17},{2,18},{3,19},{4,20},{5,21},{6,22},{7,23},{8,24},{9,... | collective-permute-start | bytes 245768 | tf_op jit(solution)/shard_map/ppermute | solution.py:553
  45.0 18.1 %collective-permute-start.6 = (bf16[16,2560]{1,0:T(8,128)(2,1)}, bf16[16,2560]{1,0:T(8,128)(2,1)S(1)}, u32[]{:S(2)}, u32[]{:S(2)}) collective-permute-start(bf16[16,2560]{1,0:T(8,128)(2,1)} %get-tuple-element.51), channel_id=1, source_target_pairs={{0,20},{1,21},{2,22},{3,23},{4,16},{5,17},{6,18},{7,19},{8,28},{9,... | collective-permute-start | bytes 245768 | tf_op jit(solution)/shard_map/ppermute | solution.py:553
  45.1 23.8 %collective-permute-start.7 = (bf16[16,2560]{1,0:T(8,128)(2,1)}, bf16[16,2560]{1,0:T(8,128)(2,1)S(1)}, u32[]{:S(2)}, u32[]{:S(2)}) collective-permute-start(bf16[16,2560]{1,0:T(8,128)(2,1)} %get-tuple-element.52), channel_id=1, source_target_pairs={{0,24},{1,25},{2,26},{3,27},{4,28},{5,29},{6,30},{7,31},{8,16},{9,... | collective-permute-start | bytes 245768 | tf_op jit(solution)/shard_map/ppermute | solution.py:553
  60.4 28.7 %collective-permute-start.9 = (bf16[16,2560]{1,0:T(8,128)(2,1)}, bf16[16,2560]{1,0:T(8,128)(2,1)S(1)}, u32[]{:S(2)}, u32[]{:S(2)}) collective-permute-start(bf16[16,2560]{1,0:T(8,128)(2,1)} %get-tuple-element.54), channel_id=1, source_target_pairs={{0,1},{1,0},{2,3},{3,2},{4,5},{5,4},{6,7},{7,6},{8,9},{9,8},{10,11... | collective-permute-start | bytes 245768 | tf_op jit(solution)/shard_map/ppermute | solution.py:553
  60.8 30.1 %collective-permute-start.10 = (bf16[16,2560]{1,0:T(8,128)(2,1)}, bf16[16,2560]{1,0:T(8,128)(2,1)S(1)}, u32[]{:S(2)}, u32[]{:S(2)}) collective-permute-start(bf16[16,2560]{1,0:T(8,128)(2,1)} %get-tuple-element.55), channel_id=1, source_target_pairs={{0,5},{1,4},{2,7},{3,6},{4,1},{5,0},{6,3},{7,2},{8,13},{9,12},{10,... | collective-permute-start | bytes 245768 | tf_op jit(solution)/shard_map/ppermute | solution.py:553
  63.1 31.1 %collective-permute-start.11 = (bf16[16,2560]{1,0:T(8,128)(2,1)}, bf16[16,2560]{1,0:T(8,128)(2,1)S(1)}, u32[]{:S(2)}, u32[]{:S(2)}) collective-permute-start(bf16[16,2560]{1,0:T(8,128)(2,1)} %get-tuple-element.56), channel_id=1, source_target_pairs={{0,9},{1,8},{2,11},{3,10},{4,13},{5,12},{6,15},{7,14},{8,1},{9,0},... | collective-permute-start | bytes 245768 | tf_op jit(solution)/shard_map/ppermute | solution.py:553
  68.9 26.6 %collective-permute-start.12 = (bf16[16,2560]{1,0:T(8,128)(2,1)}, bf16[16,2560]{1,0:T(8,128)(2,1)S(1)}, u32[]{:S(2)}, u32[]{:S(2)}) collective-permute-start(bf16[16,2560]{1,0:T(8,128)(2,1)} %get-tuple-element.57), channel_id=1, source_target_pairs={{0,13},{1,12},{2,15},{3,14},{4,9},{5,8},{6,11},{7,10},{8,5},{9,4},... | collective-permute-start | bytes 245768 | tf_op jit(solution)/shard_map/ppermute | solution.py:553
  72.6 23.5 %collective-permute-start.13 = (bf16[16,2560]{1,0:T(8,128)(2,1)}, bf16[16,2560]{1,0:T(8,128)(2,1)S(1)}, u32[]{:S(2)}, u32[]{:S(2)}) collective-permute-start(bf16[16,2560]{1,0:T(8,128)(2,1)} %get-tuple-element.58), channel_id=1, source_target_pairs={{0,17},{1,16},{2,19},{3,18},{4,21},{5,20},{6,23},{7,22},{8,25},{9,... | collective-permute-start | bytes 245768 | tf_op jit(solution)/shard_map/ppermute | solution.py:553
  107.6 53.3 %all-to-all-start.1 = ((bf16[32,32,1024]{2,1,0:T(8,128)(2,1)}), bf16[32,32,1024]{2,1,0:T(8,128)(2,1)}, u32[]{:S(2)}, u32[]{:S(2)}) async-start(bf16[32,32,1024]{2,1,0:T(8,128)(2,1)} %bitcast.12), calls=%async_computation.1 | async-start | bytes 4194304 | tf_op jit(solution)/shard_map/all_to_all | solution.py:618
  161.0 77.3 %all-to-all-start.2 = ((bf16[32,32,1536]{2,1,0:T(8,128)(2,1)}), bf16[32,32,1536]{2,1,0:T(8,128)(2,1)}, u32[]{:S(2)}, u32[]{:S(2)}) async-start(bf16[32,32,1536]{2,1,0:T(8,128)(2,1)} %bitcast.28), calls=%async_computation.2 | async-start | bytes 6291456 | tf_op jit(solution)/shard_map/all_to_all | solution.py:618
  192.6 14.8 %collective-permute-start.22 = (bf16[16,2560]{1,0:T(8,128)(2,1)S(1)}, bf16[16,2560]{1,0:T(8,128)(2,1)S(1)}, u32[]{:S(2)}, u32[]{:S(2)}) collective-permute-start(bf16[16,2560]{1,0:T(8,128)(2,1)S(1)} %get-tuple-element.90), channel_id=1, source_target_pairs={{0,24},{1,25},{2,26},{3,27},{4,28},{5,29},{6,30},{7,31},{8,16},{9,... | collective-permute-start | bytes 245768 | tf_op jit(solution)/shard_map/ppermute | solution.py:553
  195.2 13.8 %collective-permute-start.23 = (bf16[16,2560]{1,0:T(8,128)(2,1)S(1)}, bf16[16,2560]{1,0:T(8,128)(2,1)S(1)}, u32[]{:S(2)}, u32[]{:S(2)}) collective-permute-start(bf16[16,2560]{1,0:T(8,128)(2,1)S(1)} %get-tuple-element.89), channel_id=1, source_target_pairs={{0,28},{1,29},{2,30},{3,31},{4,24},{5,25},{6,26},{7,27},{8,20},{9,... | collective-permute-start | bytes 245768 | tf_op jit(solution)/shard_map/ppermute | solution.py:553
  201.2 17.8 %collective-permute-start.24 = (bf16[16,2560]{1,0:T(8,128)(2,1)S(1)}, bf16[16,2560]{1,0:T(8,128)(2,1)S(1)}, u32[]{:S(2)}, u32[]{:S(2)}) collective-permute-start(bf16[16,2560]{1,0:T(8,128)(2,1)S(1)} %get-tuple-element.88), channel_id=1, source_target_pairs={{0,1},{1,0},{2,3},{3,2},{4,5},{5,4},{6,7},{7,6},{8,9},{9,8},{10,11... | collective-permute-start | bytes 245768 | tf_op jit(solution)/shard_map/ppermute | solution.py:553
  201.2 19.9 %collective-permute-start.25 = (bf16[16,2560]{1,0:T(8,128)(2,1)S(1)}, bf16[16,2560]{1,0:T(8,128)(2,1)S(1)}, u32[]{:S(2)}, u32[]{:S(2)}) collective-permute-start(bf16[16,2560]{1,0:T(8,128)(2,1)S(1)} %get-tuple-element.87), channel_id=1, source_target_pairs={{0,5},{1,4},{2,7},{3,6},{4,1},{5,0},{6,3},{7,2},{8,13},{9,12},{10,... | collective-permute-start | bytes 245768 | tf_op jit(solution)/shard_map/ppermute | solution.py:553
  202.8 21.6 %collective-permute-start.26 = (bf16[16,2560]{1,0:T(8,128)(2,1)S(1)}, bf16[16,2560]{1,0:T(8,128)(2,1)S(1)}, u32[]{:S(2)}, u32[]{:S(2)}) collective-permute-start(bf16[16,2560]{1,0:T(8,128)(2,1)S(1)} %get-tuple-element.86), channel_id=1, source_target_pairs={{0,9},{1,8},{2,11},{3,10},{4,13},{5,12},{6,15},{7,14},{8,1},{9,0},... | collective-permute-start | bytes 245768 | tf_op jit(solution)/shard_map/ppermute | solution.py:553
  207.4 18.1 %collective-permute-start.27 = (bf16[16,2560]{1,0:T(8,128)(2,1)S(1)}, bf16[16,2560]{1,0:T(8,128)(2,1)S(1)}, u32[]{:S(2)}, u32[]{:S(2)}) collective-permute-start(bf16[16,2560]{1,0:T(8,128)(2,1)S(1)} %get-tuple-element.85), channel_id=1, source_target_pairs={{0,13},{1,12},{2,15},{3,14},{4,9},{5,8},{6,11},{7,10},{8,5},{9,4},... | collective-permute-start | bytes 245768 | tf_op jit(solution)/shard_map/ppermute | solution.py:553
  209.0 17.0 %collective-permute-start.28 = (bf16[16,2560]{1,0:T(8,128)(2,1)S(1)}, bf16[16,2560]{1,0:T(8,128)(2,1)S(1)}, u32[]{:S(2)}, u32[]{:S(2)}) collective-permute-start(bf16[16,2560]{1,0:T(8,128)(2,1)S(1)} %get-tuple-element.84), channel_id=1, source_target_pairs={{0,17},{1,16},{2,19},{3,18},{4,21},{5,20},{6,23},{7,22},{8,25},{9,... | collective-permute-start | bytes 245768 | tf_op jit(solution)/shard_map/ppermute | solution.py:553
  238.4 55.2 %all-to-all-start.3 = ((bf16[32,32,1024]{2,1,0:T(8,128)(2,1)}), bf16[32,32,1024]{2,1,0:T(8,128)(2,1)}, u32[]{:S(2)}, u32[]{:S(2)}) async-start(bf16[32,32,1024]{2,1,0:T(8,128)(2,1)} %bitcast.29), calls=%async_computation.3 | async-start | bytes 4194304 | tf_op jit(solution)/shard_map/all_to_all | solution.py:618
  247.6 47.6 %collective-permute-start.32 = (bf16[384,128]{1,0:T(8,128)(2,1)}, bf16[384,128]{1,0:T(8,128)(2,1)S(1)}, u32[]{:S(2)}, u32[]{:S(2)}) collective-permute-start(bf16[384,128]{1,0:T(8,128)(2,1)} %get-tuple-element.78), channel_id=1, source_target_pairs={{0,2},{1,3},{2,0},{3,1},{4,6},{5,7},{6,4},{7,5},{8,10},{9,11},{10,... | collective-permute-start | bytes 294920 | tf_op jit(solution)/shard_map/ppermute | solution.py:539
  (38 other events, 642.9 us)

commit v10 on v9

--- a/solution.py
+++ b/solution.py
@@ -655,7 +655,7 @@
 
     small = send(after(spec_rows, large), chunks[1])
     by_wave, by_lon = trig_tables(after(waves, large), lon_count, small)
-    arrived = [exchange(after(large, small, packs[2]))]
+    arrived = [exchange(after(large, small))]
     far_rows = far_synthesize(
         place, far_waves[0] - far_least, packs, levels, fields, 1.0 / math.sqrt(degrees)
     )

time: 303 us -> 298 us (0.983)
  waiting for transfers between devices: 111 us -> 89.6 us
  starting transfers between devices: 70.3 us -> 86.9 us
    ppermute x30, waiting for transfers between devices: 64.3 us -> 41.1 us  [within_half(): moved.append(lax.ppermute(parts[x], AXES, pairs))]
    ppermute x30, starting transfers between devices: 45.9 us -> 60.8 us  [within_half(): moved.append(lax.ppermute(parts[x], AXES, pairs))]
    all_to_all x4, waiting for transfers between devices: 36.5 us -> 39.5 us  [exchange(): lax.all_to_all(rows, AXES[::-1], split_axis=0, concat_axis=0, tiled=True)]
  transfers between devices with their start and end apart: 37 -> 37, of which waited for: 22 -> 22; matrix products, arithmetic and copies ran while one was open for 4% -> 4% of each run, Pallas kernels for 32% -> 33%
where the time goes in v10:
time: 298 us; the launch traced here: 297 us
  Pallas kernels  105 us (35%)
  waiting for transfers between devices  89.6 us (30%)
  starting transfers between devices  86.9 us (29%)
  local copies, waits for them, and re-layouts  8.59 us (3%)
  other arithmetic  6.4 us (2%)
    ppermute x30, starting transfers between devices, within_half(): moved.append(lax.ppermute(parts[x], AXES, pairs))  60.8 us
    pallas_call x2, Pallas kernels, longitudes(): pl.pallas_call(functools.partial(longitude_kernel, fields, chunk, 1.0 / m...  53.1 us
    ppermute x30, waiting for transfers between devices, within_half(): moved.append(lax.ppermute(parts[x], AXES, pairs))  41.1 us
    all_to_all x4, waiting for transfers between devices, exchange(): lax.all_to_all(rows, AXES[::-1], split_axis=0, concat_axis=0, tiled=True)  39.5 us
    all_to_all x4, starting transfers between devices, exchange(): lax.all_to_all(rows, AXES[::-1], split_axis=0, concat_axis=0, tiled=True)  19.6 us
    pallas_call x2, Pallas kernels, synthesize(): pl.pallas_call(functools.partial(synthesis_kernel, slots, levels, fields,...  13.3 us
    pallas_call x1, Pallas kernels, trig_tables(): pl.pallas_call(trig_kernel, grid=(depth // rows,), in_specs=[pl.BlockSpec...  9.06 us
    ppermute x3, waiting for transfers between devices, across_halves(): lax.ppermute(value, 'grp', [(p, (p + planes // 2) % planes) for p in rang...  8.98 us
  transfers between devices with their start and end apart: 37, of which 22 were waited for; matrix products, arithmetic and copies ran while one was open for 4% of the time, Pallas kernels for 33%

profile of v10, /device:TPU:0, one launch (start us, length us, event | category | flops | bytes accessed | tf_op | source)
XLA Modules:
  0.0 297.3 jit_solution(11118293040565962141)
XLA Ops:
  2.0 4.1 %collective-permute-start = (bf16[256,768]{1,0:T(8,128)(2,1)}, bf16[256,768]{1,0:T(8,128)(2,1)S(1)}, u32[]{:S(2)}, u32[]{:S(2)}) collective-permute-start(bf16[256,768]{1,0:T(8,128)(2,1)} %get-tuple-element.42.refs_0_), channel_id=1, source_target_pairs={{0,2},{1,3},{2,0},{3,1},{4,6},{5,7},{6,4},{7,5},{8,10},{9,11},{10,... | collective-permute-start | bytes 1179656 | tf_op jit(solution)/shard_map/ppermute | solution.py:539
  6.2 7.4 %synthesis.2 = bf16[1024,1536]{1,0:T(8,128)(2,1)} custom-call(s32[1]{0:T(128)} %bitcast.1.first_ref, s32[640]{0:T(1024)} %owner_ref.3, bf16[20,128,640]{2,1,0:T(8,128)(2,1)} %bitcast.25, bf16[20,640,640]{2,1,0:T(8,128)(2,1)} %table_ref.7), custom_call_target="tpu_custom_call" | custom-call | flops 2013265920 | bytes 13631488 | tf_op jit(solution)/shard_map/synthesis/pallas_call | solution.py:81
  13.6 5.9 %synthesis.3 = bf16[1024,1024]{1,0:T(8,128)(2,1)} custom-call(s32[1]{0:T(128)} %bitcast.1.first_ref, s32[640]{0:T(1024)} %owner_ref.3, bf16[20,128,640]{2,1,0:T(8,128)(2,1)} %bitcast.26, bf16[20,640,640]{2,1,0:T(8,128)(2,1)} %table_ref.7), custom_call_target="tpu_custom_call" | custom-call | flops 1342177280 | bytes 9961472 | tf_op jit(solution)/shard_map/synthesis/pallas_call | solution.py:81
  19.5 6.2 %all-to-all-start = ((bf16[32,32,1536]{2,1,0:T(8,128)(2,1)}), bf16[32,32,1536]{2,1,0:T(8,128)(2,1)}, u32[]{:S(2)}, u32[]{:S(2)}) async-start(bf16[32,32,1536]{2,1,0:T(8,128)(2,1)} %bitcast.27), calls=%async_computation | async-start | bytes 6291456 | tf_op jit(solution)/shard_map/all_to_all | solution.py:618
  27.8 7.5 %collective-permute-done.1.refs_3_ = bf16[128,768]{1,0:T(8,128)(2,1)S(1)} collective-permute-done((bf16[128,768]{1,0:T(8,128)(2,1)}, bf16[128,768]{1,0:T(8,128)(2,1)S(1)}, u32[]{:S(2)}, u32[]{:S(2)}) %collective-permute-start.1) | collective-permute-done | bytes 196640 | tf_op jit(solution)/shard_map/ppermute | solution.py:539
  41.5 6.4 %collective-permute-start.3 = (bf16[16,2560]{1,0:T(8,128)(2,1)}, bf16[16,2560]{1,0:T(8,128)(2,1)S(1)}, u32[]{:S(2)}, u32[]{:S(2)}) collective-permute-start(bf16[16,2560]{1,0:T(8,128)(2,1)} %get-tuple-element.48), channel_id=1, source_target_pairs={{0,8},{1,9},{2,10},{3,11},{4,12},{5,13},{6,14},{7,15},{8,0},{9,1},... | collective-permute-start | bytes 245768 | tf_op jit(solution)/shard_map/ppermute | solution.py:553
  54.2 4.4 %collective-permute-start.9 = (bf16[16,2560]{1,0:T(8,128)(2,1)}, bf16[16,2560]{1,0:T(8,128)(2,1)S(1)}, u32[]{:S(2)}, u32[]{:S(2)}) collective-permute-start(bf16[16,2560]{1,0:T(8,128)(2,1)} %get-tuple-element.54), channel_id=1, source_target_pairs={{0,1},{1,0},{2,3},{3,2},{4,5},{5,4},{6,7},{7,6},{8,9},{9,8},{10,11... | collective-permute-start | bytes 245768 | tf_op jit(solution)/shard_map/ppermute | solution.py:553
  62.8 3.9 %collective-permute-start.11 = (bf16[16,2560]{1,0:T(8,128)(2,1)}, bf16[16,2560]{1,0:T(8,128)(2,1)S(1)}, u32[]{:S(2)}, u32[]{:S(2)}) collective-permute-start(bf16[16,2560]{1,0:T(8,128)(2,1)} %get-tuple-element.56), channel_id=1, source_target_pairs={{0,9},{1,8},{2,11},{3,10},{4,13},{5,12},{6,15},{7,14},{8,1},{9,0},... | collective-permute-start | bytes 245768 | tf_op jit(solution)/shard_map/ppermute | solution.py:553
  73.0 6.8 %collective-permute-done.9 = bf16[16,2560]{1,0:T(8,128)(2,1)S(1)} collective-permute-done((bf16[16,2560]{1,0:T(8,128)(2,1)}, bf16[16,2560]{1,0:T(8,128)(2,1)S(1)}, u32[]{:S(2)}, u32[]{:S(2)}) %collective-permute-start.9) | collective-permute-done | bytes 81952 | tf_op jit(solution)/shard_map/ppermute | solution.py:553
  96.6 5.0 %all-to-all-done = bf16[32,32,1536]{2,1,0:T(8,128)(2,1)} async-done(((bf16[32,32,1536]{2,1,0:T(8,128)(2,1)}), bf16[32,32,1536]{2,1,0:T(8,128)(2,1)}, u32[]{:S(2)}, u32[]{:S(2)}) %all-to-all-start) | async-done | bytes 3145760 | tf_op jit(solution)/shard_map/all_to_all | solution.py:618
  101.7 5.3 %all-to-all-start.1 = ((bf16[32,32,1024]{2,1,0:T(8,128)(2,1)}), bf16[32,32,1024]{2,1,0:T(8,128)(2,1)}, u32[]{:S(2)}, u32[]{:S(2)}) async-start(bf16[32,32,1024]{2,1,0:T(8,128)(2,1)} %bitcast.12), calls=%async_computation.1 | async-start | bytes 4194304 | tf_op jit(solution)/shard_map/all_to_all | solution.py:618
  113.9 9.1 %trig.1 = (bf16[1280,2560]{1,0:T(8,128)(2,1)}, bf16[2560,1280]{1,0:T(8,128)(2,1)}) custom-call(f32[1280,4]{1,0:T(8,128)} %copy.38.small_ref, f32[1280,128]{1,0:T(8,128)} %get-tuple-element.66.cos_turn_ref, f32[1280,128]{1,0:T(8,128)} %get-tuple-element.67.sin_turn_ref), custom_call_target="tpu_custom_call" | custom-call | flops 39321600 | bytes 13107200 | tf_op jit(solution)/shard_map/trig/pallas_call | solution.py:597
  123.0 31.1 %longitudes.3 = (bf16[1024,1536]{1,0:T(8,128)(2,1)}, bf16[256,1536]{1,0:T(8,128)(2,1)}) custom-call(bf16[1024,1536]{1,0:T(8,128)(2,1)} %bitcast.11.rows_ref, bf16[256,2560]{1,0:T(8,128)(2,1)} %copy-done.20, bf16[2560,1280]{1,0:T(8,128)(2,1)} %get-tuple-element.68.by_lon_ref, bf16[1280,2560]{1,0:T(8,128)(2,1)} %get-tuple-element.69.by_wave_ref), custom_call_target="tpu_custom_call" | custom-call | flops 20132659200 | bytes 20971520 | tf_op jit(solution)/shard_map/longitudes/pallas_call | solution.py:137
  155.7 4.3 %all-to-all-start.2 = ((bf16[32,32,1536]{2,1,0:T(8,128)(2,1)}), bf16[32,32,1536]{2,1,0:T(8,128)(2,1)}, u32[]{:S(2)}, u32[]{:S(2)}) async-start(bf16[32,32,1536]{2,1,0:T(8,128)(2,1)} %bitcast.28), calls=%async_computation.2 | async-start | bytes 6291456 | tf_op jit(solution)/shard_map/all_to_all | solution.py:618
  160.1 22.0 %longitudes.2 = (bf16[1024,1024]{1,0:T(8,128)(2,1)}, bf16[256,1024]{1,0:T(8,128)(2,1)}) custom-call(bf16[1024,1024]{1,0:T(8,128)(2,1)} %bitcast.13.rows_ref, bf16[256,2560]{1,0:T(8,128)(2,1)} %copy-done.20, bf16[2560,1280]{1,0:T(8,128)(2,1)} %get-tuple-element.68.by_lon_ref, bf16[1280,2560]{1,0:T(8,128)(2,1)} %get-tuple-element.69.by_wave_ref), custom_call_target="tpu_custom_call" | custom-call | flops 13421772800 | bytes 18350080 | tf_op jit(solution)/shard_map/longitudes/pallas_call | solution.py:137
  190.0 5.5 %collective-permute-start.23 = (bf16[16,2560]{1,0:T(8,128)(2,1)S(1)}, bf16[16,2560]{1,0:T(8,128)(2,1)S(1)}, u32[]{:S(2)}, u32[]{:S(2)}) collective-permute-start(bf16[16,2560]{1,0:T(8,128)(2,1)S(1)} %get-tuple-element.89), channel_id=1, source_target_pairs={{0,28},{1,29},{2,30},{3,31},{4,24},{5,25},{6,26},{7,27},{8,20},{9,... | collective-permute-start | bytes 245768 | tf_op jit(solution)/shard_map/ppermute | solution.py:553
  197.6 4.6 %collective-permute-start.26 = (bf16[16,2560]{1,0:T(8,128)(2,1)S(1)}, bf16[16,2560]{1,0:T(8,128)(2,1)S(1)}, u32[]{:S(2)}, u32[]{:S(2)}) collective-permute-start(bf16[16,2560]{1,0:T(8,128)(2,1)S(1)} %get-tuple-element.86), channel_id=1, source_target_pairs={{0,9},{1,8},{2,11},{3,10},{4,13},{5,12},{6,15},{7,14},{8,1},{9,0},... | collective-permute-start | bytes 245768 | tf_op jit(solution)/shard_map/ppermute | solution.py:553
  203.8 4.3 %collective-permute-start.28 = (bf16[16,2560]{1,0:T(8,128)(2,1)S(1)}, bf16[16,2560]{1,0:T(8,128)(2,1)S(1)}, u32[]{:S(2)}, u32[]{:S(2)}) collective-permute-start(bf16[16,2560]{1,0:T(8,128)(2,1)S(1)} %get-tuple-element.84), channel_id=1, source_target_pairs={{0,17},{1,16},{2,19},{3,18},{4,21},{5,20},{6,23},{7,22},{8,25},{9,... | collective-permute-start | bytes 245768 | tf_op jit(solution)/shard_map/ppermute | solution.py:553
  208.2 5.6 %collective-permute-done.24.refs_12_ = bf16[16,2560]{1,0:T(8,128)(2,1)S(1)} collective-permute-done((bf16[16,2560]{1,0:T(8,128)(2,1)S(1)}, bf16[16,2560]{1,0:T(8,128)(2,1)S(1)}, u32[]{:S(2)}, u32[]{:S(2)}) %collective-permute-start.24) | collective-permute-done | bytes 81952 | tf_op jit(solution)/shard_map/ppermute | solution.py:553
  222.5 4.6 %collective-permute-done.30.refs_18_ = bf16[16,2560]{1,0:T(8,128)(2,1)S(1)} collective-permute-done((bf16[16,2560]{1,0:T(8,128)(2,1)S(1)}, bf16[16,2560]{1,0:T(8,128)(2,1)S(1)}, u32[]{:S(2)}, u32[]{:S(2)}) %collective-permute-start.30) | collective-permute-done | bytes 81952 | tf_op jit(solution)/shard_map/ppermute | solution.py:553
  244.1 5.3 %fold.1.folded_ref = bf16[16,256,384]{2,1,0:T(8,128)(2,1)} custom-call(bf16[1024,1536]{1,0:T(8,128)(2,1)} %bitcast.15.arrived_ref), custom_call_target="tpu_custom_call" | custom-call | flops 3145728 | bytes 6291456 | tf_op jit(solution)/shard_map/fold/pallas_call | solution.py:344
  249.4 8.5 %analysis.1.base_ref = f32[20,128,640]{2,1,0:T(8,128)} custom-call(bf16[16,256,384]{2,1,0:T(8,128)(2,1)} %fold.1.folded_ref, f32[20,1,640]{2,1,0:T(1,128)} %get-tuple-element.104.even_ref, f32[20,1,640]{2,1,0:T(1,128)} %get-tuple-element.103.odd_ref, bf16[20,640,640]{2,1,0:T(8,128)(2,1)} %table_ref.7, bf16[20,640,640]{2,1,0:T(8,128)(2,1)} %table_ref.7, ...), custom_call_target="tpu_custom_call" | custom-call | flops 2516582400 | bytes 20316160 | tf_op jit(solution)/shard_map/analysis/pallas_call | solution.py:387
  257.9 30.5 %all-to-all-done.3 = bf16[32,32,1024]{2,1,0:T(8,128)(2,1)} async-done(((bf16[32,32,1024]{2,1,0:T(8,128)(2,1)}), bf16[32,32,1024]{2,1,0:T(8,128)(2,1)}, u32[]{:S(2)}, u32[]{:S(2)}) %all-to-all-start.3) | async-done | bytes 2097184 | tf_op jit(solution)/shard_map/all_to_all | solution.py:618
  290.6 6.5 %closing.1 = f32[20,128,640]{2,1,0:T(8,128)} custom-call(s32[1]{0:T(128)} %bitcast.hemi_ref, bf16[1024,1024]{1,0:T(8,128)(2,1)} %bitcast.17.arrived_ref, bf16[20,640,640]{2,1,0:T(8,128)(2,1)} %table_ref.7, f32[20,128,640]{2,1,0:T(8,128)} %analysis.1.base_ref, f32[20,1,640]{2,1,0:T(1,128)} %get-tuple-element.104.even_ref, ...), custom_call_target="tpu_custom_call", output_to_operand_aliasing={{}: (3, {})} | custom-call | flops 1677721600 | bytes 15204352 | tf_op jit(solution)/shard_map/closing/pallas_call | solution.py:511
  (161 shorter events, 91.8 us)
Async XLA Ops:
  2.0 33.3 %collective-permute-start = (bf16[256,768]{1,0:T(8,128)(2,1)}, bf16[256,768]{1,0:T(8,128)(2,1)S(1)}, u32[]{:S(2)}, u32[]{:S(2)}) collective-permute-start(bf16[256,768]{1,0:T(8,128)(2,1)} %get-tuple-element.42.refs_0_), channel_id=1, source_target_pairs={{0,2},{1,3},{2,0},{3,1},{4,6},{5,7},{6,4},{7,5},{8,10},{9,11},{10,... | collective-permute-start | bytes 1179656 | tf_op jit(solution)/shard_map/ppermute | solution.py:539
  6.1 29.2 %collective-permute-start.1 = (bf16[128,768]{1,0:T(8,128)(2,1)}, bf16[128,768]{1,0:T(8,128)(2,1)S(1)}, u32[]{:S(2)}, u32[]{:S(2)}) collective-permute-start(bf16[128,768]{1,0:T(8,128)(2,1)} %get-tuple-element.45.refs_1_), channel_id=1, source_target_pairs={{0,2},{1,3},{2,0},{3,1},{4,6},{5,7},{6,4},{7,5},{8,10},{9,11},{10,... | collective-permute-start | bytes 589832 | tf_op jit(solution)/shard_map/ppermute | solution.py:539
  19.5 82.2 %all-to-all-start = ((bf16[32,32,1536]{2,1,0:T(8,128)(2,1)}), bf16[32,32,1536]{2,1,0:T(8,128)(2,1)}, u32[]{:S(2)}, u32[]{:S(2)}) async-start(bf16[32,32,1536]{2,1,0:T(8,128)(2,1)} %bitcast.27), calls=%async_computation | async-start | bytes 6291456 | tf_op jit(solution)/shard_map/all_to_all | solution.py:618
  48.0 14.8 %collective-permute-start.6 = (bf16[16,2560]{1,0:T(8,128)(2,1)}, bf16[16,2560]{1,0:T(8,128)(2,1)S(1)}, u32[]{:S(2)}, u32[]{:S(2)}) collective-permute-start(bf16[16,2560]{1,0:T(8,128)(2,1)} %get-tuple-element.51), channel_id=1, source_target_pairs={{0,20},{1,21},{2,22},{3,23},{4,16},{5,17},{6,18},{7,19},{8,28},{9,... | collective-permute-start | bytes 245768 | tf_op jit(solution)/shard_map/ppermute | solution.py:553
  49.5 17.3 %collective-permute-start.7 = (bf16[16,2560]{1,0:T(8,128)(2,1)}, bf16[16,2560]{1,0:T(8,128)(2,1)S(1)}, u32[]{:S(2)}, u32[]{:S(2)}) collective-permute-start(bf16[16,2560]{1,0:T(8,128)(2,1)} %get-tuple-element.52), channel_id=1, source_target_pairs={{0,24},{1,25},{2,26},{3,27},{4,28},{5,29},{6,30},{7,31},{8,16},{9,... | collective-permute-start | bytes 245768 | tf_op jit(solution)/shard_map/ppermute | solution.py:553
  51.9 17.6 %collective-permute-start.8 = (bf16[16,2560]{1,0:T(8,128)(2,1)}, bf16[16,2560]{1,0:T(8,128)(2,1)S(1)}, u32[]{:S(2)}, u32[]{:S(2)}) collective-permute-start(bf16[16,2560]{1,0:T(8,128)(2,1)} %get-tuple-element.53), channel_id=1, source_target_pairs={{0,28},{1,29},{2,30},{3,31},{4,24},{5,25},{6,26},{7,27},{8,20},{9,... | collective-permute-start | bytes 245768 | tf_op jit(solution)/shard_map/ppermute | solution.py:553
  54.2 25.6 %collective-permute-start.9 = (bf16[16,2560]{1,0:T(8,128)(2,1)}, bf16[16,2560]{1,0:T(8,128)(2,1)S(1)}, u32[]{:S(2)}, u32[]{:S(2)}) collective-permute-start(bf16[16,2560]{1,0:T(8,128)(2,1)} %get-tuple-element.54), channel_id=1, source_target_pairs={{0,1},{1,0},{2,3},{3,2},{4,5},{5,4},{6,7},{7,6},{8,9},{9,8},{10,11... | collective-permute-start | bytes 245768 | tf_op jit(solution)/shard_map/ppermute | solution.py:553
  59.5 22.4 %collective-permute-start.10 = (bf16[16,2560]{1,0:T(8,128)(2,1)}, bf16[16,2560]{1,0:T(8,128)(2,1)S(1)}, u32[]{:S(2)}, u32[]{:S(2)}) collective-permute-start(bf16[16,2560]{1,0:T(8,128)(2,1)} %get-tuple-element.55), channel_id=1, source_target_pairs={{0,5},{1,4},{2,7},{3,6},{4,1},{5,0},{6,3},{7,2},{8,13},{9,12},{10,... | collective-permute-start | bytes 245768 | tf_op jit(solution)/shard_map/ppermute | solution.py:553
  62.8 22.1 %collective-permute-start.11 = (bf16[16,2560]{1,0:T(8,128)(2,1)}, bf16[16,2560]{1,0:T(8,128)(2,1)S(1)}, u32[]{:S(2)}, u32[]{:S(2)}) collective-permute-start(bf16[16,2560]{1,0:T(8,128)(2,1)} %get-tuple-element.56), channel_id=1, source_target_pairs={{0,9},{1,8},{2,11},{3,10},{4,13},{5,12},{6,15},{7,14},{8,1},{9,0},... | collective-permute-start | bytes 245768 | tf_op jit(solution)/shard_map/ppermute | solution.py:553
  66.7 19.7 %collective-permute-start.12 = (bf16[16,2560]{1,0:T(8,128)(2,1)}, bf16[16,2560]{1,0:T(8,128)(2,1)S(1)}, u32[]{:S(2)}, u32[]{:S(2)}) collective-permute-start(bf16[16,2560]{1,0:T(8,128)(2,1)} %get-tuple-element.57), channel_id=1, source_target_pairs={{0,13},{1,12},{2,15},{3,14},{4,9},{5,8},{6,11},{7,10},{8,5},{9,4},... | collective-permute-start | bytes 245768 | tf_op jit(solution)/shard_map/ppermute | solution.py:553
  69.5 18.2 %collective-permute-start.13 = (bf16[16,2560]{1,0:T(8,128)(2,1)}, bf16[16,2560]{1,0:T(8,128)(2,1)S(1)}, u32[]{:S(2)}, u32[]{:S(2)}) collective-permute-start(bf16[16,2560]{1,0:T(8,128)(2,1)} %get-tuple-element.58), channel_id=1, source_target_pairs={{0,17},{1,16},{2,19},{3,18},{4,21},{5,20},{6,23},{7,22},{8,25},{9,... | collective-permute-start | bytes 245768 | tf_op jit(solution)/shard_map/ppermute | solution.py:553
  84.9 11.7 %collective-permute-start.16 = (bf16[16,2560]{1,0:T(8,128)(2,1)S(1)}, bf16[16,2560]{1,0:T(8,128)(2,1)S(1)}, u32[]{:S(2)}, u32[]{:S(2)}) collective-permute-start(bf16[16,2560]{1,0:T(8,128)(2,1)S(1)} %copy-done.22), channel_id=1, source_target_pairs={{0,29},{1,28},{2,31},{3,30},{4,25},{5,24},{6,27},{7,26},{8,21},{9,... | collective-permute-start | bytes 245768 | tf_op jit(solution)/shard_map/ppermute | solution.py:553
  101.7 54.1 %all-to-all-start.1 = ((bf16[32,32,1024]{2,1,0:T(8,128)(2,1)}), bf16[32,32,1024]{2,1,0:T(8,128)(2,1)}, u32[]{:S(2)}, u32[]{:S(2)}) async-start(bf16[32,32,1024]{2,1,0:T(8,128)(2,1)} %bitcast.12), calls=%async_computation.1 | async-start | bytes 4194304 | tf_op jit(solution)/shard_map/all_to_all | solution.py:618
  155.7 77.4 %all-to-all-start.2 = ((bf16[32,32,1536]{2,1,0:T(8,128)(2,1)}), bf16[32,32,1536]{2,1,0:T(8,128)(2,1)}, u32[]{:S(2)}, u32[]{:S(2)}) async-start(bf16[32,32,1536]{2,1,0:T(8,128)(2,1)} %bitcast.28), calls=%async_computation.2 | async-start | bytes 6291456 | tf_op jit(solution)/shard_map/all_to_all | solution.py:618
  187.4 14.8 %collective-permute-start.22 = (bf16[16,2560]{1,0:T(8,128)(2,1)S(1)}, bf16[16,2560]{1,0:T(8,128)(2,1)S(1)}, u32[]{:S(2)}, u32[]{:S(2)}) collective-permute-start(bf16[16,2560]{1,0:T(8,128)(2,1)S(1)} %get-tuple-element.90), channel_id=1, source_target_pairs={{0,24},{1,25},{2,26},{3,27},{4,28},{5,29},{6,30},{7,31},{8,16},{9,... | collective-permute-start | bytes 245768 | tf_op jit(solution)/shard_map/ppermute | solution.py:553
  190.0 13.9 %collective-permute-start.23 = (bf16[16,2560]{1,0:T(8,128)(2,1)S(1)}, bf16[16,2560]{1,0:T(8,128)(2,1)S(1)}, u32[]{:S(2)}, u32[]{:S(2)}) collective-permute-start(bf16[16,2560]{1,0:T(8,128)(2,1)S(1)} %get-tuple-element.89), channel_id=1, source_target_pairs={{0,28},{1,29},{2,30},{3,31},{4,24},{5,25},{6,26},{7,27},{8,20},{9,... | collective-permute-start | bytes 245768 | tf_op jit(solution)/shard_map/ppermute | solution.py:553
  196.0 17.8 %collective-permute-start.24 = (bf16[16,2560]{1,0:T(8,128)(2,1)S(1)}, bf16[16,2560]{1,0:T(8,128)(2,1)S(1)}, u32[]{:S(2)}, u32[]{:S(2)}) collective-permute-start(bf16[16,2560]{1,0:T(8,128)(2,1)S(1)} %get-tuple-element.88), channel_id=1, source_target_pairs={{0,1},{1,0},{2,3},{3,2},{4,5},{5,4},{6,7},{7,6},{8,9},{9,8},{10,11... | collective-permute-start | bytes 245768 | tf_op jit(solution)/shard_map/ppermute | solution.py:553
  196.0 19.9 %collective-permute-start.25 = (bf16[16,2560]{1,0:T(8,128)(2,1)S(1)}, bf16[16,2560]{1,0:T(8,128)(2,1)S(1)}, u32[]{:S(2)}, u32[]{:S(2)}) collective-permute-start(bf16[16,2560]{1,0:T(8,128)(2,1)S(1)} %get-tuple-element.87), channel_id=1, source_target_pairs={{0,5},{1,4},{2,7},{3,6},{4,1},{5,0},{6,3},{7,2},{8,13},{9,12},{10,... | collective-permute-start | bytes 245768 | tf_op jit(solution)/shard_map/ppermute | solution.py:553
  197.6 21.6 %collective-permute-start.26 = (bf16[16,2560]{1,0:T(8,128)(2,1)S(1)}, bf16[16,2560]{1,0:T(8,128)(2,1)S(1)}, u32[]{:S(2)}, u32[]{:S(2)}) collective-permute-start(bf16[16,2560]{1,0:T(8,128)(2,1)S(1)} %get-tuple-element.86), channel_id=1, source_target_pairs={{0,9},{1,8},{2,11},{3,10},{4,13},{5,12},{6,15},{7,14},{8,1},{9,0},... | collective-permute-start | bytes 245768 | tf_op jit(solution)/shard_map/ppermute | solution.py:553
  202.2 18.1 %collective-permute-start.27 = (bf16[16,2560]{1,0:T(8,128)(2,1)S(1)}, bf16[16,2560]{1,0:T(8,128)(2,1)S(1)}, u32[]{:S(2)}, u32[]{:S(2)}) collective-permute-start(bf16[16,2560]{1,0:T(8,128)(2,1)S(1)} %get-tuple-element.85), channel_id=1, source_target_pairs={{0,13},{1,12},{2,15},{3,14},{4,9},{5,8},{6,11},{7,10},{8,5},{9,4},... | collective-permute-start | bytes 245768 | tf_op jit(solution)/shard_map/ppermute | solution.py:553
  203.8 16.9 %collective-permute-start.28 = (bf16[16,2560]{1,0:T(8,128)(2,1)S(1)}, bf16[16,2560]{1,0:T(8,128)(2,1)S(1)}, u32[]{:S(2)}, u32[]{:S(2)}) collective-permute-start(bf16[16,2560]{1,0:T(8,128)(2,1)S(1)} %get-tuple-element.84), channel_id=1, source_target_pairs={{0,17},{1,16},{2,19},{3,18},{4,21},{5,20},{6,23},{7,22},{8,25},{9,... | collective-permute-start | bytes 245768 | tf_op jit(solution)/shard_map/ppermute | solution.py:553
  219.2 11.6 %collective-permute-start.31 = (bf16[16,2560]{1,0:T(8,128)(2,1)S(1)}, bf16[16,2560]{1,0:T(8,128)(2,1)S(1)}, u32[]{:S(2)}, u32[]{:S(2)}) collective-permute-start(bf16[16,2560]{1,0:T(8,128)(2,1)S(1)} %get-tuple-element.81), channel_id=1, source_target_pairs={{0,29},{1,28},{2,31},{3,30},{4,25},{5,24},{6,27},{7,26},{8,21},{9,... | collective-permute-start | bytes 245768 | tf_op jit(solution)/shard_map/ppermute | solution.py:553
  233.2 55.2 %all-to-all-start.3 = ((bf16[32,32,1024]{2,1,0:T(8,128)(2,1)}), bf16[32,32,1024]{2,1,0:T(8,128)(2,1)}, u32[]{:S(2)}, u32[]{:S(2)}) async-start(bf16[32,32,1024]{2,1,0:T(8,128)(2,1)} %bitcast.29), calls=%async_computation.3 | async-start | bytes 4194304 | tf_op jit(solution)/shard_map/all_to_all | solution.py:618
  241.7 48.3 %collective-permute-start.32 = (bf16[384,128]{1,0:T(8,128)(2,1)}, bf16[384,128]{1,0:T(8,128)(2,1)S(1)}, u32[]{:S(2)}, u32[]{:S(2)}) collective-permute-start(bf16[384,128]{1,0:T(8,128)(2,1)} %get-tuple-element.78), channel_id=1, source_target_pairs={{0,2},{1,3},{2,0},{3,1},{4,6},{5,7},{6,4},{7,5},{8,10},{9,11},{10,... | collective-permute-start | bytes 294920 | tf_op jit(solution)/shard_map/ppermute | solution.py:539
  (38 other events, 617.3 us)
